TPU v7x, 128 devices: a whole 4x4x4 slice. The times are simulated.
128 devices in a mesh: lat: 8 (over y, z_lo), lon: 16 (over z_hi, x, core).
Axes of the slice: x: 4, y: 4, z: 4 (z_hi: 2, z_lo: 2; z = z_hi * 2 + z_lo), core: 2. Of those that a mesh axis runs over, the one named last changes fastest.
Arguments:
- state: bfloat16 [8, 48, 192, 192], P(None, 'lat', 'lon'), may hold values from -6 to 6
- lat_valid: int32 [48], replicated, may hold values from 0 to 1, as said below
- norm_gains: float32 [2, 2, 192], replicated, may hold values from 0.1 to 1.9
- qkv_weight: bfloat16 [2, 192, 576], replicated, may hold values from -0.4375 to 0.4375
- proj_weight: bfloat16 [2, 192, 192], replicated, may hold values from -0.4375 to 0.4375
- fc1_weight: bfloat16 [2, 192, 768], replicated, may hold values from -0.4375 to 0.4375
- fc2_weight: bfloat16 [2, 768, 192], replicated, may hold values from -0.21875 to 0.21875
- earth_bias: bfloat16 [2, 8, 4, 19872], P(None, 'lat', None, 'lon'), may hold values from -3 to 3
- merge_gain: float32 [768], replicated, may hold values from 0.1 to 1.9
- merge_weight: bfloat16 [768, 384], replicated, may hold values from -0.21875 to 0.21875
Outputs:
- merged: bfloat16 [8, 24, 96, 384], P(None, 'lat', 'lon')
Inputs may be any that keep to these rules, and one draw needn't show every extreme that they name: `lat_valid`: 0 on the first 0 to 3 latitude rows and on the last 1 to 3 rows, 1 on all rows between.
All inputs are finite; a program needn't handle non-finite values.
Results may differ from a plain program's by a relative error of at most 0.015.
Values may be sent and summed in bfloat16 or wider, within the bound.
No kernel may reach another device: no remote copies, remote signals or barrier semaphores. Data moves between devices by JAX's collectives and lax.ppermute only.
A program may use at most 192 MiB of HBM per device.

v0:
```python
import functools

import jax
import jax.numpy as jnp
import numpy as np
from jax import lax
from jax.experimental import pallas as pl
from jax.experimental.pallas import tpu as pltpu
from jax.sharding import PartitionSpec as P

BF16 = jnp.bfloat16
F32 = jnp.float32
C = 192
HEADS = 6
HEAD_SIZE = 32
HIDDEN = 768
LEVELS, ROWS, COLS = 8, 6, 12
WINDOWS = 4
TOKENS = 144
CELLS = 576
SPAN = 23
HALF = 6 * SPAN
GROUP = 128
KEYS = 2 * GROUP
LATS, LONS = 8, 16
SHARD = 1242
SHIFT = 12.0
MASKED = -1e30


def one_hot(sources, width):
    sources = np.asarray(sources)
    matrix = np.zeros((len(sources), width), np.float32)
    rows = np.nonzero(sources >= 0)[0]
    matrix[rows, sources[rows]] = 1.0
    return jnp.asarray(matrix, BF16)


def quarter_cells():
    return [(1, 1), (0, 1), (1, 0), (0, 0)]


def query_order():
    return [a * 12 + i for i in range(12) for a in range(12)]


def quarter_chunks(qr, qc):
    return [((3 * qr + r) * COLS + 6 * qc) * LEVELS for r in range(3)]


def level_cells(level):
    return pl.ds(level, ROWS * COLS, stride=LEVELS)


def read_window(cells, first_level):
    parts = [
        jnp.concatenate([cells[0, level_cells(level % LEVELS)], cells[1, level_cells(level % LEVELS)]], axis=1)
        for level in (first_level, first_level + 1)
    ]
    return jnp.concatenate(parts, axis=0)[:, :C]


def write_window(cells, first_level, values):
    wide = jnp.concatenate([values, jnp.zeros((TOKENS, 2 * GROUP - C), F32)], axis=1)
    for offset in range(2):
        rows = wide[offset * 72 : (offset + 1) * 72]
        where = level_cells((first_level + offset) % LEVELS)
        cells[0, where] = rows[:, :GROUP]
        cells[1, where] = rows[:, GROUP:]


def read_quarter(cells, qr, qc):
    parts = [
        jnp.concatenate([cells[0, at : at + 48], cells[1, at : at + 48]], axis=1) for at in quarter_chunks(qr, qc)
    ]
    return jnp.concatenate(parts, axis=0)[:, :C]


def write_quarter(cells, qr, qc, values):
    wide = jnp.concatenate([values, jnp.zeros((TOKENS, 2 * GROUP - C), F32)], axis=1)
    for r, at in enumerate(quarter_chunks(qr, qc)):
        cells[0, at : at + 48] = wide[r * 48 : (r + 1) * 48, :GROUP]
        cells[1, at : at + 48] = wide[r * 48 : (r + 1) * 48, GROUP:]


def table_rows(block):
    sources = []
    for lead in (0, 4):
        for key_level in range(2):
            for window in range(WINDOWS):
                for slot in range(16):
                    a = slot - lead
                    inside = 0 <= a < 12
                    sources.append((a * 2 + key_level) * 8 + block * 4 + window if inside else -1)
    return sources


def column_choice(parity):
    matrix = np.zeros((HALF, 6 * GROUP), np.float32)
    for at in range(6):
        i = 2 * at + parity
        for row in range(ROWS):
            for k in range(12):
                matrix[row * SPAN + k - i + 11, at * GROUP + row * 12 + k] = 1.0
    return jnp.asarray(matrix, BF16)


def layer_norm(values, scales):
    average = jnp.mean(values, axis=-1, keepdims=True)
    centred = values - average
    spread = jnp.mean(centred * centred, axis=-1, keepdims=True)
    return centred * lax.rsqrt(spread + 1e-05) * scales


def dot(a, b):
    return jnp.dot(a, b, preferred_element_type=F32)


def dot_transposed(a, b):
    return lax.dot_general(a, b, (((1,), (1,)), ((), ())), preferred_element_type=F32)


def moved(choice, rows):
    return dot(choice, rows).astype(BF16)


def head_lanes(head):
    lane = lax.broadcasted_iota(jnp.int32, (1, C), 1)
    return (lane >= head * HEAD_SIZE) & (lane < (head + 1) * HEAD_SIZE)


def project(normed, qkv_weight, query_choice):
    queries = moved(query_choice, dot(normed, qkv_weight[:, :C]).astype(BF16))
    pad = jnp.zeros((GROUP - 72, C), F32)

    def padded(part):
        return jnp.concatenate([part[:72], pad, part[72:], pad], axis=0).astype(BF16)

    keys = padded(dot(normed, qkv_weight[:, C : 2 * C]))
    values = padded(dot(normed, qkv_weight[:, 2 * C :]))
    ones = jnp.ones((KEYS, KEYS - C), BF16)
    return queries, keys, jnp.concatenate([values, ones], axis=1)


def score(queries, keys):
    stacked = jnp.concatenate(
        [jnp.where(head_lanes(h), queries, jnp.zeros((), BF16)) for h in range(HEADS)], axis=0
    )
    return dot_transposed(stacked, keys) * HEAD_SIZE ** (-0.5)


def blend(scores, values, bias_of):
    weights = []
    for h in range(HEADS):
        part = scores[h * TOKENS : (h + 1) * TOKENS] + bias_of(h)
        weights.append(jnp.exp(part).astype(BF16))
    blended = dot(jnp.concatenate(weights, axis=0), values)
    total = jnp.zeros((TOKENS, C), F32)
    result = jnp.zeros((TOKENS, C), F32)
    for h in range(HEADS):
        part = blended[h * TOKENS : (h + 1) * TOKENS]
        result = jnp.where(head_lanes(h), part[:, :C], result)
        total = jnp.where(head_lanes(h), part[:, C : C + 1], total)
    return (result / jnp.maximum(total, np.exp(-SHIFT))).astype(BF16)


def expanded_bias(z_even, z_odd, window, head):
    rows = []
    for at in range(6):
        lanes = slice(at * GROUP, (at + 1) * GROUP)
        halves = []
        for key_level in range(2):
            first = head * 128 + (key_level * 4 + window) * 16
            top = z_even[first : first + 16, lanes]
            low = z_odd[first : first + 16, lanes]
            halves.append(jnp.concatenate([top[:8], top[8:] + low[:8], low[8:]], axis=0))
        rows.append(jnp.concatenate(halves, axis=1))
    return jnp.concatenate(rows, axis=0)


def expand_tables(table_ref, table_choice, even_ref, odd_ref, z_even, z_odd):
    tops, lows = [], []
    for h in range(HEADS):
        picked = moved(table_choice[...], table_ref[h * 192 : (h + 1) * 192, :HALF])
        tops.append(picked[:128])
        lows.append(picked[128:])
    z_even[...] = dot(jnp.concatenate(tops, axis=0), even_ref[...])
    z_odd[...] = dot(jnp.concatenate(lows, axis=0), odd_ref[...])


def erf_gelu(values):
    return 0.5 * values * (1.0 + lax.erf(values * np.float32(np.sqrt(0.5))))


def feed_forward(middle, gain, fc1, fc2, keep):
    hidden = erf_gelu(dot(layer_norm(middle, gain).astype(BF16), fc1)).astype(BF16)
    return jnp.where(keep, middle + dot_transposed(hidden, fc2), 0.0).astype(BF16)


def pack_piece(piece):
    side = jnp.concatenate(
        [piece[:80, 128:], jnp.concatenate([piece[80:, 128:], piece[:16, 128:]], axis=0)], axis=1
    )
    return jnp.concatenate([piece[:, :128], side], axis=0)


def unpack_piece(packed):
    side = packed[TOKENS:]
    ends = jnp.concatenate([side[:, :64], side[: TOKENS - 80, 64:]], axis=0)
    return jnp.concatenate([packed[:TOKENS], ends], axis=1)


def prepare_masks(lat_valid, first_mask, second_mask, keep):
    lat = lax.axis_index("lat")

    def flag(row):
        return lat_valid[row] > 0

    lane = lax.broadcasted_iota(jnp.int32, (8, KEYS), 1)
    key_row = lax.rem(lane, GROUP) // 12
    mask = jnp.full((8, KEYS), MASKED, F32)
    usable = jnp.full((8, KEYS), MASKED, F32)
    for r in range(ROWS):
        mask = jnp.where((key_row == r) & flag(lat * ROWS + r), -SHIFT, mask)
        rolled = lax.rem(lat * ROWS + 3 + r, LATS * ROWS)
        usable = jnp.where((key_row == r) & flag(rolled), 0.0, usable)
    first_mask[...] = mask
    a = lax.rem(lax.broadcasted_iota(jnp.int32, (TOKENS, 1), 0), 12)
    query_half = jnp.where(lax.rem(a, ROWS) >= 3, 1, 0)
    key_half = jnp.where(key_row[:1] >= 3, 1, 0)
    same_rows = (query_half == key_half) | (lat != LATS - 1)
    same_level = jnp.where(a >= ROWS, 1, 0) == jnp.where(lane[:1] >= GROUP, 1, 0)
    whole = jnp.where(same_rows, usable[:1], MASKED)
    second_mask[0] = whole
    second_mask[1] = jnp.where(same_level, whole, MASKED)
    for half in range(2):
        for r in range(3):
            value = jnp.where(flag(lat * ROWS + 3 * half + r), 1.0, 0.0)
            keep[half, r * 48 : (r + 1) * 48] = jnp.full((48, GROUP), value, F32)


def fetch(sources, held, sems):
    copies = [pltpu.make_async_copy(a, b, sems.at[n]) for n, (a, b) in enumerate(zip(sources, held))]
    for copy in copies:
        copy.start()
    return copies


def sliced(kernel, layers, *refs):
    kernel(*[ref.at[layers[at]] if at in layers else ref for at, ref in enumerate(refs)])


def fetch_kernel(*refs):
    count = len(refs) // 2
    for copy in fetch(refs[:count], refs[count : 2 * count], refs[-1]):
        copy.wait()


def prepare_kernel(mine, proj, fc1, fc2, *refs):
    for copy in fetch((proj, fc1, fc2), refs[:3], refs[3]):
        copy.wait()


def join_kernel(*refs):
    at = 0
    for ref in refs[:-1]:
        if ref.shape[1:] == refs[-1].shape[1:]:
            refs[-1][at : at + ref.shape[0]] = ref[...]
            at += ref.shape[0]


def before_kernel(lat_valid, halves, x, gains, qkv_weight, query_choice, *refs):
    sources, (scores_out, v_out, first_mask, second_mask, keep) = refs[:3], refs[3:8]
    held, (cells, sems) = refs[8:11], refs[11:]
    copies = fetch(sources, held, sems)
    prepare_masks(lat_valid, first_mask, second_mask, keep)
    wide = jnp.concatenate([x[...].astype(F32), jnp.zeros((CELLS, 2 * GROUP - C), F32)], axis=1)
    cells[0] = wide[:, :GROUP]
    cells[1] = wide[:, GROUP:]
    for p in range(WINDOWS):
        normed = layer_norm(read_window(cells, 2 * p), gains[0, 0:1]).astype(BF16)
        q, k, v_out[p] = project(normed, qkv_weight[...], query_choice[...])
        scores_out[p] = score(q, k)
    for copy in copies:
        copy.wait()


def first_quarter(quarter, x, cells, gains, fc1, fc2, keep):
    qr, qc = quarter_cells()[quarter]
    inputs = jnp.concatenate([x[at : at + 48] for at in quarter_chunks(qr, qc)], axis=0)
    middle = inputs.astype(F32) + read_quarter(cells, qr, qc).astype(BF16).astype(F32)
    return feed_forward(middle, gains[0, 1:2], fc1[...], fc2[...], keep[qr][:, :1] > 0)


def first_kernel(mine, theirs, scores, v, first_mask, keep, x, gains, query_choice, proj, fc1, fc2, even, odd, table_choice, sent_lat, sent_lon, sent_both, table_out, out, cells, table_f32, z_even, z_odd):
    me = lax.axis_index("lon")
    for g in range(LONS):
        slot = lax.rem(me // 2 - g // 2 + 8, 4) * 2 + jnp.where(me // 8 == g // 8, 0, 1)
        shard = jnp.where(lax.rem(me, 2) == g % 2, mine[slot], theirs[slot]).astype(F32)
        piece = jnp.concatenate([shard[0], shard[1]], axis=0)
        for n in range(9):
            at = (g * 9 + n) * 8
            table_f32[at : at + 8, :HALF] = piece[:, n * HALF : (n + 1) * HALF]
    table_out[:, :HALF] = table_f32[:, :HALF].astype(BF16)
    expand_tables(table_out, table_choice, even, odd, z_even, z_odd)
    mask = first_mask[0:1]
    for p in range(WINDOWS):
        blended = blend(scores[p], v[p], lambda h: expanded_bias(z_even, z_odd, p, h) + mask)
        write_window(cells, 2 * p, dot(moved(query_choice[...], blended), proj[...]))
    for quarter, target in ((2, sent_lon), (3, sent_both), (1, sent_lat)):
        result = first_quarter(quarter, x, cells, gains, fc1, fc2, keep)
        out[(quarter - 1) * TOKENS : quarter * TOKENS] = result
        target[...] = pack_piece(result)


def bias_kernel(*refs):
    sources, (table, second_mask, even, odd, x, cells, gains, fc1, fc2, keep) = refs[:3], refs[3:13]
    (bias_out, near), held, (z_even, z_odd, sems) = refs[13:15], refs[15:18], refs[18:]
    copies = fetch(sources, held, sems)
    table_choice = held[0]
    near[...] = first_quarter(0, x, cells, gains, fc1, fc2, keep)
    copies[0].wait()
    expand_tables(table, table_choice, even, odd, z_even, z_odd)
    for p in range(WINDOWS):
        for h in range(HEADS):
            whole = expanded_bias(z_even, z_odd, p, h) + second_mask[1 if p == WINDOWS - 1 else 0]
            bias_out[p, h * TOKENS : (h + 1) * TOKENS] = whole.astype(BF16)
    for copy in copies[1:]:
        copy.wait()


def write_normed(cells, quarter, piece, gains):
    qr, qc = quarter_cells()[quarter]
    normed = layer_norm(piece.astype(F32), gains[1, 0:1]).astype(BF16)
    write_quarter(cells, 1 - qr, 1 - qc, normed.astype(F32))


def ready_kernel(near, from_lon, from_both, gains, cells):
    write_normed(cells, 0, near[...], gains)
    write_normed(cells, 2, unpack_piece(from_lon[...]), gains)
    write_normed(cells, 3, unpack_piece(from_both[...]), gains)


def second_kernel(ready, from_lat, bias, gains, qkv_weight, proj, query_choice, own, sent_lat, sent_lon, sent_both, cells, results):
    for quarter in (0, 2, 3):
        qr, qc = quarter_cells()[quarter]
        for at in quarter_chunks(1 - qr, 1 - qc):
            for half in range(2):
                cells[half, at : at + 48] = ready[half, at : at + 48]
    write_normed(cells, 1, unpack_piece(from_lat[...]), gains)
    for p in range(WINDOWS):
        normed = read_window(cells, 2 * p + 1).astype(BF16)
        q, k, v = project(normed, qkv_weight[...], query_choice[...])

        def bias_of(h):
            return bias[p, h * TOKENS : (h + 1) * TOKENS].astype(F32) - SHIFT

        blended = blend(score(q, k), v, bias_of)
        write_window(results, 2 * p + 1, dot(moved(query_choice[...], blended), proj[...]))
    pieces = [read_quarter(results, 1 - qr, 1 - qc).astype(BF16) for qr, qc in quarter_cells()]
    own[...] = pieces[0]
    sent_lat[...] = pack_piece(pieces[1])
    sent_lon[...] = pack_piece(pieces[2])
    sent_both[...] = pack_piece(pieces[3])


def own_kernel(*refs):
    sources, (keep, near, own, gains), result, held, sems = refs[:3], refs[3:7], refs[7], refs[8:11], refs[11]
    copies = fetch(sources, held, sems)
    for copy in copies:
        copy.wait()
    middle = near[...].astype(F32) + own[...].astype(F32)
    result[...] = feed_forward(middle, gains[1, 1:2], held[0][...], held[1][...], keep[1][:, :1] > 0)


def last_kernel(keep, far, done, from_lat, from_lon, from_both, gains, fc1, fc2, merge_gain, merge_weight, merged):
    groups = {}
    for quarter, (qr, qc) in enumerate(quarter_cells()):
        if quarter == 0:
            result = done[...]
        else:
            attended = unpack_piece((from_lat, from_lon, from_both)[quarter - 1][...])
            middle = far[(quarter - 1) * TOKENS : quarter * TOKENS].astype(F32) + attended.astype(F32)
            result = feed_forward(middle, gains[1, 1:2], fc1[...], fc2[...], keep[qr][:, :1] > 0)
        result = result.astype(F32)
        for r in range(3):
            for c in range(6):
                at = (r * 6 + c) * LEVELS
                groups[3 * qr + r, 6 * qc + c] = result[at : at + LEVELS]
    parts = [
        jnp.concatenate([groups[2 * r + dr, 2 * c + dc] for r in range(3) for c in range(6)], axis=0)
        for dr in range(2)
        for dc in range(2)
    ]
    average = sum(jnp.sum(part, axis=-1, keepdims=True) for part in parts) / (4 * C)
    parts = [part - average for part in parts]
    spread = sum(jnp.sum(part * part, axis=-1, keepdims=True) for part in parts) / (4 * C)
    scale = lax.rsqrt(spread + 1e-05)
    total = jnp.zeros((TOKENS, 2 * C), F32)
    for d, part in enumerate(parts):
        normed = (part * scale * merge_gain[d : d + 1]).astype(BF16)
        total = total + dot(normed, merge_weight[d * C : (d + 1) * C])
    merged[...] = total.astype(BF16)


VMEM_SPEC = pl.BlockSpec(memory_space=pltpu.VMEM)
SMEM_SPEC = pl.BlockSpec(memory_space=pltpu.SMEM)


def call(kernel, name, micros, outs, scratch, *operands, in_specs=None):
    return pl.pallas_call(
        kernel,
        name=name,
        out_shape=outs,
        in_specs=in_specs or [VMEM_SPEC] * len(operands),
        out_specs=jax.tree.map(lambda _: VMEM_SPEC, outs),
        scratch_shapes=scratch,
        cost_estimate=pl.CostEstimate(flops=int(micros * 1e9), bytes_accessed=2**20, transcendentals=0),
        compiler_params=pltpu.CompilerParams(vmem_limit_bytes=16 * 2**20),
    )(*operands)


def shape(*dims, dtype=BF16):
    return jax.ShapeDtypeStruct(dims, dtype)


def sent(block, distance_lat, distance_lon):
    route = []
    for i in range(LATS):
        for j in range(LONS):
            to = ((i + distance_lat) % LATS) * LONS + (j + distance_lon) % LONS
            route.append((i * LONS + j, to))
    return lax.ppermute(block, ("lat", "lon"), route)


def turned(block, place):
    route = []
    for j in range(LONS):
        z, x, core = place(j // 8, j // 2 % 4, j % 2)
        route.append((j, z * 8 + x * 2 + core))
    return lax.ppermute(block, "lon", route)


def shards(state, lat_valid, norm_gains, qkv_weight, proj_weight, fc1_weight, fc2_weight, earth_bias, merge_gain, merge_weight):
    shard = earth_bias[:, 0]
    cells = pltpu.VMEM((2, CELLS, GROUP), F32)
    z_scratch = [pltpu.VMEM((768, 768), F32), pltpu.VMEM((768, 768), F32)]
    packed = shape(224, 128)

    def in_hbm(array):
        return pltpu.with_memory_space_constraint(array, pltpu.HBM)

    def like(arrays):
        return [shape(*array.shape, dtype=array.dtype) for array in arrays]

    hbm_spec = pl.BlockSpec(memory_space=pltpu.HBM)
    fc2_turned = jnp.swapaxes(fc2_weight, 1, 2)
    early = [
        shard[None],
        state.transpose(1, 2, 0, 3).reshape(CELLS, C),
        norm_gains,
        qkv_weight,
        one_hot(query_order(), TOKENS),
    ]
    constants = [column_choice(0), column_choice(1), one_hot(table_rows(0), 192)]
    layer = [shape(C, C), shape(C, HIDDEN), shape(C, HIDDEN)]
    other_half = turned(shard, lambda z, x, core: (1 - z, x, core))
    held_shard, x, gains, qkv0, query_choice = call(
        functools.partial(sliced, fetch_kernel, {3: 0}),
        "fetch",
        1.4,
        like(early[:3]) + [shape(C, 3 * C)] + like(early[4:]),
        [pltpu.SemaphoreType.DMA((len(early),))],
        *[in_hbm(array) for array in early],
        in_specs=[hbm_spec] * len(early),
    )
    halves = call(join_kernel, "halves", 0.2, shape(2, 2, WINDOWS, SHARD), [], held_shard, other_half[None])
    ring = [turned(halves, lambda z, x, core: (z, (x + hop) % 4, core)) for hop in range(1, 4)]
    scores, v, first_mask, second_mask, keep, even, odd, rows0 = call(
        before_kernel,
        "before",
        2.5,
        [
            shape(WINDOWS, HEADS * TOKENS, KEYS, dtype=F32),
            shape(WINDOWS, KEYS, KEYS),
            shape(8, KEYS, dtype=F32),
            shape(2, TOKENS, KEYS, dtype=F32),
            shape(2, TOKENS, GROUP, dtype=F32),
        ]
        + like(constants),
        [cells, pltpu.SemaphoreType.DMA((len(constants),))],
        in_hbm(lat_valid), halves, x, gains, qkv0, query_choice,
        *[in_hbm(array) for array in constants],
        in_specs=[SMEM_SPEC] + [VMEM_SPEC] * 5 + [hbm_spec] * len(constants),
    )
    mine = call(join_kernel, "mine", 0.3, shape(8, 2, WINDOWS, SHARD), [], halves, *ring, v)
    theirs = turned(mine, lambda z, x, core: (z, x, 1 - core))
    proj0, fc1_0, fc2_0 = call(
        functools.partial(sliced, prepare_kernel, {1: 0, 2: 0, 3: 0}),
        "prepare",
        1.2,
        layer,
        [pltpu.SemaphoreType.DMA((3,))],
        mine, in_hbm(proj_weight), in_hbm(fc1_weight), in_hbm(fc2_turned),
        in_specs=[VMEM_SPEC] + [hbm_spec] * 3,
    )
    to_lat, to_lon, to_both, tables, far, attended = call(
        first_kernel,
        "first",
        4.5,
        [packed, packed, packed, shape(1152, KEYS), shape(3 * TOKENS, C), shape(2, CELLS, GROUP, dtype=F32)],
        [pltpu.VMEM((1152, KEYS), F32)] + z_scratch,
        mine, theirs, scores, v, first_mask, keep, x, gains, query_choice, proj0, fc1_0, fc2_0, even, odd, rows0,
    )
    from_lon, from_both, from_lat = sent(to_lon, 0, -1), sent(to_both, -1, -1), sent(to_lat, -1, 0)
    late = [one_hot(table_rows(1), 192), qkv_weight, proj_weight]
    bias, near, _, qkv1, proj1 = call(
        functools.partial(sliced, bias_kernel, {1: 1, 2: 1}),
        "bias",
        0.2,
        [shape(WINDOWS, HEADS * TOKENS, KEYS), shape(TOKENS, C)]
        + like(late[:1])
        + [shape(C, 3 * C), shape(C, C)],
        z_scratch + [pltpu.SemaphoreType.DMA((len(late),))],
        *[in_hbm(array) for array in late],
        tables, second_mask, even, odd, x, attended, gains, fc1_0, fc2_0, keep,
        in_specs=[hbm_spec] * len(late) + [VMEM_SPEC] * 10,
    )
    ready = call(
        ready_kernel,
        "ready",
        0.6,
        shape(2, CELLS, GROUP, dtype=F32),
        [],
        near, from_lon, from_both, gains,
    )
    own, to_lat, to_lon, to_both = call(
        second_kernel,
        "second",
        4.5,
        [shape(TOKENS, C), packed, packed, packed],
        [cells, cells],
        ready, from_lat, bias, gains, qkv1, proj1, query_choice,
    )
    from_lon, from_both, from_lat = sent(to_lon, 0, 1), sent(to_both, 1, 1), sent(to_lat, 1, 0)
    done, fc1_1, fc2_1, merge = call(
        functools.partial(sliced, own_kernel, {0: 1, 1: 1}),
        "own",
        0.5,
        [shape(TOKENS, C)] + layer[1:] + like([merge_weight]),
        [pltpu.SemaphoreType.DMA((3,))],
        in_hbm(fc1_weight), in_hbm(fc2_turned), in_hbm(merge_weight), keep, near, own, gains,
        in_specs=[hbm_spec] * 3 + [VMEM_SPEC] * 4,
    )
    merged = call(
        last_kernel,
        "last",
        2.0,
        shape(TOKENS, 2 * C),
        [],
        keep, far, done, from_lat, from_lon, from_both, gains, fc1_1, fc2_1, merge_gain.reshape(4, C), merge,
    )
    return merged.reshape(3, 6, LEVELS, 2 * C).transpose(2, 0, 1, 3)


def solution(mesh):
    return jax.shard_map(
        shards,
        mesh=mesh,
        in_specs=(
            P(None, "lat", "lon", None),
            P(),
            P(),
            P(),
            P(),
            P(),
            P(),
            P(None, "lat", None, "lon"),
            P(),
            P(),
        ),
        out_specs=P(None, "lat", "lon", None),
        check_vma=False,
    )
```

profile of v0, /device:TPU:0, one launch (start us, length us, event | category | flops | bytes accessed | tf_op | source)
XLA Modules:
  0.0 48.9 jit_solution(7952058799995000183)
XLA Ops:
  0.0 4.0 %collective-permute-start = (bf16[2,4,1242]{2,1,0:T(4,128)(2,1)}, bf16[2,4,1242]{2,1,0:T(4,128)(2,1)S(1)}, u32[]{:S(2)}, u32[]{:S(2)}) collective-permute-start(bf16[2,4,1242]{2,1,0:T(4,128)(2,1)} %bitcast.14), channel_id=1, source_target_pairs={{0,8},{1,9},{2,10},{3,11},{4,12},{5,13},{6,14},{7,15},{8,0},{9,1},... | collective-permute-start | bytes 59624 | tf_op jit(solution)/shard_map/ppermute | solution.py:441
  4.0 1.2 %fetch.1 = (bf16[1,2,4,1242]{3,2,1,0:T(4,128)(2,1)S(1)}, bf16[576,192]{1,0:T(8,128)(2,1)S(1)}, f32[2,2,192]{2,1,0:T(2,128)S(1)}, bf16[192,576]{1,0:T(8,128)(2,1)S(1)}, bf16[144,144]{1,0:T(8,128)(2,1)S(1)}) custom-call(bf16[1,2,4,1242]{3,2,1,0:T(4,128)(2,1)} %bitcast.15, bf16[576,192]{1,0:T(8,128)(2,1)} %bitcast.13, f32[2,2,192]{2,1,0:T(2,128)} %refs_2_.5, ...), custom_call_target="tpu_custom_call" | custom-call | flops 1400000000 | bytes 1048576 | tf_op jit(solution)/shard_map/fetch/pallas_call | solution.py:411
  5.1 0.8 %collective-permute-done = bf16[2,4,1242]{2,1,0:T(4,128)(2,1)S(1)} collective-permute-done((bf16[2,4,1242]{2,1,0:T(4,128)(2,1)}, bf16[2,4,1242]{2,1,0:T(4,128)(2,1)S(1)}, u32[]{:S(2)}, u32[]{:S(2)}) %collective-permute-start) | collective-permute-done | bytes 19904 | tf_op jit(solution)/shard_map/ppermute | solution.py:441
  5.9 1.5 %collective-permute-start.1 = (bf16[2,2,4,1242]{3,2,1,0:T(4,128)(2,1)S(1)}, bf16[2,2,4,1242]{3,2,1,0:T(4,128)(2,1)S(1)}, u32[]{:S(2)}, u32[]{:S(2)}) collective-permute-start(bf16[2,2,4,1242]{3,2,1,0:T(4,128)(2,1)S(1)} %halves.1.refs_0_), channel_id=1, source_target_pairs={{0,2},{1,3},{2,4},{3,5},{4,6},{5,7},{6,0},{7,1},{8,10},{9,11},{10,... | collective-permute-start | bytes 119240 | tf_op jit(solution)/shard_map/ppermute | solution.py:441
  7.4 2.7 %collective-permute-start.2 = (bf16[2,2,4,1242]{3,2,1,0:T(4,128)(2,1)S(1)}, bf16[2,2,4,1242]{3,2,1,0:T(4,128)(2,1)S(1)}, u32[]{:S(2)}, u32[]{:S(2)}) collective-permute-start(bf16[2,2,4,1242]{3,2,1,0:T(4,128)(2,1)S(1)} %halves.1.refs_0_), channel_id=1, source_target_pairs={{0,4},{1,5},{2,6},{3,7},{4,0},{5,1},{6,2},{7,3},{8,12},{9,13},{10,... | collective-permute-start | bytes 119240 | tf_op jit(solution)/shard_map/ppermute | solution.py:441
  10.2 1.4 %collective-permute-start.3 = (bf16[2,2,4,1242]{3,2,1,0:T(4,128)(2,1)S(1)}, bf16[2,2,4,1242]{3,2,1,0:T(4,128)(2,1)S(1)}, u32[]{:S(2)}, u32[]{:S(2)}) collective-permute-start(bf16[2,2,4,1242]{3,2,1,0:T(4,128)(2,1)S(1)} %halves.1.refs_0_), channel_id=1, source_target_pairs={{0,6},{1,7},{2,0},{3,1},{4,2},{5,3},{6,4},{7,5},{8,14},{9,15},{10,... | collective-permute-start | bytes 119240 | tf_op jit(solution)/shard_map/ppermute | solution.py:441
  11.6 3.1 %before.1 = (f32[4,864,256]{2,1,0:T(8,128)S(1)}, bf16[4,256,256]{2,1,0:T(8,128)(2,1)S(1)}, f32[8,256]{1,0:T(8,128)S(1)}, f32[2,144,256]{2,1,0:T(8,128)S(1)}, f32...) custom-call(s32[48]{0:T(128)} %lat_valid.1, ...), custom_call_target="tpu_custom_call" | custom-call | flops 2500000000 | bytes 1048576 | tf_op jit(solution)/shard_map/before/pallas_call | solution.py:411
  14.7 0.0 collective-permute-done.1.refs_1_
  14.8 0.0 collective-permute-done.2.refs_2_
  14.8 0.0 collective-permute-done.3.refs_3_
  14.8 0.1 collective-permute-start.4
  14.9 1.1 %prepare.1 = (bf16[192,192]{1,0:T(8,128)(2,1)S(1)}, bf16[192,768]{1,0:T(8,128)(2,1)S(1)}, bf16[192,768]{1,0:T(8,128)(2,1)S(1)}) custom-call(bf16[8,2,4,1242]{3,2,1,0:T(4,128)(2,1)S(1)} %mine.1.refs_0_, bf16[2,192,192]{2,1,0:T(8,128)(2,1)} %refs_2_.7, bf16[2,192,768]{2,1,0:T(8,128)(2,1)} %refs_0_.3, bf16[2,192,768]{2,1,0:T(8,128)(2,1)} %bitcast.11), custom_call_target="tpu_custom_call" | custom-call | flops 1200000000 | bytes 1048576 | tf_op jit(solution)/shard_map/prepare/pallas_call | solution.py:411
  16.0 0.2 collective-permute-done.4.theirs
  16.3 4.6 %first.1 = (bf16[224,128]{1,0:T(8,128)(2,1)S(1)}, bf16[224,128]{1,0:T(8,128)(2,1)S(1)}, bf16[224,128]{1,0:T(8,128)(2,1)S(1)}, bf16[1152,256]{1,0:T(8,128)(2,1)S(...) custom-call(bf16[8,2,4,1242]{3,2,1,0:T(4,128)(2,1)S(1)} %mine.1.refs_0_, ...), custom_call_target="tpu_custom_call" | custom-call | flops 4499999744 | bytes 1048576 | tf_op jit(solution)/shard_map/first/pallas_call | solution.py:411
  20.9 4.9 %collective-permute-start.5 = (bf16[224,128]{1,0:T(8,128)(2,1)S(1)}, bf16[224,128]{1,0:T(8,128)(2,1)S(1)}, u32[]{:S(2)}, u32[]{:S(2)}) collective-permute-start(bf16[224,128]{1,0:T(8,128)(2,1)S(1)} %get-tuple-element.59), channel_id=1, source_target_pairs={{0,15},{1,0},{2,1},{3,2},{4,3},{5,4},{6,5},{7,6},{8,7},{9,8},{10,9... | collective-permute-start | bytes 172040 | tf_op jit(solution)/shard_map/ppermute | solution.py:433
  25.9 2.8 %collective-permute-start.6 = (bf16[224,128]{1,0:T(8,128)(2,1)S(1)}, bf16[224,128]{1,0:T(8,128)(2,1)S(1)}, u32[]{:S(2)}, u32[]{:S(2)}) collective-permute-start(bf16[224,128]{1,0:T(8,128)(2,1)S(1)} %get-tuple-element.60), channel_id=1, source_target_pairs={{0,127},{1,112},{2,113},{3,114},{4,115},{5,116},{6,117},{7,118},{8... | collective-permute-start | bytes 172040 | tf_op jit(solution)/shard_map/ppermute | solution.py:433
  28.7 0.7 %collective-permute-start.7 = (bf16[224,128]{1,0:T(8,128)(2,1)S(1)}, bf16[224,128]{1,0:T(8,128)(2,1)S(1)}, u32[]{:S(2)}, u32[]{:S(2)}) collective-permute-start(bf16[224,128]{1,0:T(8,128)(2,1)S(1)} %get-tuple-element.61), channel_id=1, source_target_pairs={{0,112},{1,113},{2,114},{3,115},{4,116},{5,117},{6,118},{7,119},{8... | collective-permute-start | bytes 172040 | tf_op jit(solution)/shard_map/ppermute | solution.py:433
  29.4 2.7 %bias.1 = (bf16[4,864,256]{2,1,0:T(8,128)(2,1)S(1)}, bf16[144,192]{1,0:T(8,128)(2,1)S(1)}, bf16[256,192]{1,0:T(8,128)(2,1)}, bf16[192,576]{1,0:T(8,128)(2,1)S(1)}, bf16[192,192]{1,0:T(8,128)(2,1)S(1)}) custom-call(bf16[256,192]{1,0:T(8,128)(2,1)} %constant.14.clone.refs_0_, bf16[2,192,576]{2,1,0:T(8,128)(2,1)} %refs_1_.4, bf16[2,192,192]{2,1,0:T(8,128)(2,1)} %refs_2_.7, ...), custom_call_target="tpu_custom_call" | custom-call | flops 200000000 | bytes 1048576 | tf_op jit(solution)/shard_map/bias/pallas_call | solution.py:411
  32.1 0.0 collective-permute-done.5.from_lon
  32.1 0.0 collective-permute-done.6.from_both
  32.1 0.3 ready.1
  32.4 0.9 %collective-permute-done.7.from_lat = bf16[224,128]{1,0:T(8,128)(2,1)S(1)} collective-permute-done((bf16[224,128]{1,0:T(8,128)(2,1)S(1)}, bf16[224,128]{1,0:T(8,128)(2,1)S(1)}, u32[]{:S(2)}, u32[]{:S(2)}) %collective-permute-start.7) | collective-permute-done | bytes 57376 | tf_op jit(solution)/shard_map/ppermute | solution.py:433
  33.3 0.0 copy-start
  33.3 4.1 %second.1 = (bf16[144,192]{1,0:T(8,128)(2,1)S(1)}, bf16[224,128]{1,0:T(8,128)(2,1)S(1)}, bf16[224,128]{1,0:T(8,128)(2,1)S(1)}, bf16[224,128]{1,0:T(8,128)(2,1)S(1)}) custom-call(f32[2,576,128]{2,1,0:T(8,128)S(1)} %ready.1, bf16[224,128]{1,0:T(8,128)(2,1)S(1)} %collective-permute-done.7.from_lat, bf16[4,864,256]{2,1,0:T(8,128)(2,1)S(1)} %get-tuple-element.62.bias, ...), custom_call_target="tpu_custom_call" | custom-call | flops 4499999744 | bytes 1048576 | tf_op jit(solution)/shard_map/second/pallas_call | solution.py:411
  37.4 0.7 %collective-permute-start.10 = (bf16[224,128]{1,0:T(8,128)(2,1)S(1)}, bf16[224,128]{1,0:T(8,128)(2,1)S(1)}, u32[]{:S(2)}, u32[]{:S(2)}) collective-permute-start(bf16[224,128]{1,0:T(8,128)(2,1)S(1)} %get-tuple-element.69), channel_id=1, source_target_pairs={{0,17},{1,18},{2,19},{3,20},{4,21},{5,22},{6,23},{7,24},{8,25},{9,... | collective-permute-start | bytes 172040 | tf_op jit(solution)/shard_map/ppermute | solution.py:433
  38.1 0.0 collective-permute-start.8
  38.1 0.2 collective-permute-start.9
  38.3 0.0 copy-done
  38.3 0.1 reshape.10.merge_gain
  38.4 1.8 %own.1 = (bf16[144,192]{1,0:T(8,128)(2,1)S(1)}, bf16[192,768]{1,0:T(8,128)(2,1)S(1)}, bf16[192,768]{1,0:T(8,128)(2,1)S(1)}, bf16[768,384]{1,0:T(8,128)(2,1)S(1)}) custom-call(bf16[2,192,768]{2,1,0:T(8,128)(2,1)} %refs_0_.3, bf16[2,192,768]{2,1,0:T(8,128)(2,1)} %bitcast.12, bf16[768,384]{1,0:T(8,128)(2,1)} %refs_2_.8, ...), custom_call_target="tpu_custom_call" | custom-call | flops 500000000 | bytes 1048576 | tf_op jit(solution)/shard_map/own/pallas_call | solution.py:411
  40.2 6.3 %collective-permute-done.10.from_both = bf16[224,128]{1,0:T(8,128)(2,1)S(1)} collective-permute-done((bf16[224,128]{1,0:T(8,128)(2,1)S(1)}, bf16[224,128]{1,0:T(8,128)(2,1)S(1)}, u32[]{:S(2)}, u32[]{:S(2)}) %collective-permute-start.10) | collective-permute-done | bytes 57376 | tf_op jit(solution)/shard_map/ppermute | solution.py:433
  46.5 0.0 collective-permute-done.8.from_lat
  46.5 0.0 collective-permute-done.9.from_lon
  46.5 2.3 %last.1 = bf16[144,384]{1,0:T(8,128)(2,1)} custom-call(f32[2,144,128]{2,1,0:T(8,128)S(1)} %get-tuple-element.44.keep.refs_12_.refs_3_, bf16[432,192]{1,0:T(8,128)(2,1)S(1)} %get-tuple-element.54.far, bf16[144,192]{1,0:T(8,128)(2,1)S(1)} %get-tuple-element.66.done, bf16[224,128]{1,0:T(8,128)(2,1)S(1)} %collective-permute-done.8.from_lat, ...), custom_call_target="tpu_custom_call" | custom-call | flops 2000000000 | bytes 1048576 | tf_op jit(solution)/shard_map/last/pallas_call | solution.py:411
  (2 shorter events, 0.0 us)
Async XLA Ops:
  0.0 5.9 %collective-permute-start = (bf16[2,4,1242]{2,1,0:T(4,128)(2,1)}, bf16[2,4,1242]{2,1,0:T(4,128)(2,1)S(1)}, u32[]{:S(2)}, u32[]{:S(2)}) collective-permute-start(bf16[2,4,1242]{2,1,0:T(4,128)(2,1)} %bitcast.14), channel_id=1, source_target_pairs={{0,8},{1,9},{2,10},{3,11},{4,12},{5,13},{6,14},{7,15},{8,0},{9,1},... | collective-permute-start | bytes 59624 | tf_op jit(solution)/shard_map/ppermute | solution.py:441
  5.9 8.8 %collective-permute-start.1 = (bf16[2,2,4,1242]{3,2,1,0:T(4,128)(2,1)S(1)}, bf16[2,2,4,1242]{3,2,1,0:T(4,128)(2,1)S(1)}, u32[]{:S(2)}, u32[]{:S(2)}) collective-permute-start(bf16[2,2,4,1242]{3,2,1,0:T(4,128)(2,1)S(1)} %halves.1.refs_0_), channel_id=1, source_target_pairs={{0,2},{1,3},{2,4},{3,5},{4,6},{5,7},{6,0},{7,1},{8,10},{9,11},{10,... | collective-permute-start | bytes 119240 | tf_op jit(solution)/shard_map/ppermute | solution.py:441
  7.4 7.3 %collective-permute-start.2 = (bf16[2,2,4,1242]{3,2,1,0:T(4,128)(2,1)S(1)}, bf16[2,2,4,1242]{3,2,1,0:T(4,128)(2,1)S(1)}, u32[]{:S(2)}, u32[]{:S(2)}) collective-permute-start(bf16[2,2,4,1242]{3,2,1,0:T(4,128)(2,1)S(1)} %halves.1.refs_0_), channel_id=1, source_target_pairs={{0,4},{1,5},{2,6},{3,7},{4,0},{5,1},{6,2},{7,3},{8,12},{9,13},{10,... | collective-permute-start | bytes 119240 | tf_op jit(solution)/shard_map/ppermute | solution.py:441
  10.2 4.6 %collective-permute-start.3 = (bf16[2,2,4,1242]{3,2,1,0:T(4,128)(2,1)S(1)}, bf16[2,2,4,1242]{3,2,1,0:T(4,128)(2,1)S(1)}, u32[]{:S(2)}, u32[]{:S(2)}) collective-permute-start(bf16[2,2,4,1242]{3,2,1,0:T(4,128)(2,1)S(1)} %halves.1.refs_0_), channel_id=1, source_target_pairs={{0,6},{1,7},{2,0},{3,1},{4,2},{5,3},{6,4},{7,5},{8,14},{9,15},{10,... | collective-permute-start | bytes 119240 | tf_op jit(solution)/shard_map/ppermute | solution.py:441
  14.8 1.5 %collective-permute-start.4 = (bf16[8,2,4,1242]{3,2,1,0:T(4,128)(2,1)S(1)}, bf16[8,2,4,1242]{3,2,1,0:T(4,128)(2,1)S(1)}, u32[]{:S(2)}, u32[]{:S(2)}) collective-permute-start(bf16[8,2,4,1242]{3,2,1,0:T(4,128)(2,1)S(1)} %mine.1.refs_0_), channel_id=1, source_target_pairs={{0,1},{1,0},{2,3},{3,2},{4,5},{5,4},{6,7},{7,6},{8,9},{9,8},{10,11... | collective-permute-start | bytes 476936 | tf_op jit(solution)/shard_map/ppermute | solution.py:441
  20.9 11.1 %collective-permute-start.5 = (bf16[224,128]{1,0:T(8,128)(2,1)S(1)}, bf16[224,128]{1,0:T(8,128)(2,1)S(1)}, u32[]{:S(2)}, u32[]{:S(2)}) collective-permute-start(bf16[224,128]{1,0:T(8,128)(2,1)S(1)} %get-tuple-element.59), channel_id=1, source_target_pairs={{0,15},{1,0},{2,1},{3,2},{4,3},{5,4},{6,5},{7,6},{8,7},{9,8},{10,9... | collective-permute-start | bytes 172040 | tf_op jit(solution)/shard_map/ppermute | solution.py:433
  25.9 6.2 %collective-permute-start.6 = (bf16[224,128]{1,0:T(8,128)(2,1)S(1)}, bf16[224,128]{1,0:T(8,128)(2,1)S(1)}, u32[]{:S(2)}, u32[]{:S(2)}) collective-permute-start(bf16[224,128]{1,0:T(8,128)(2,1)S(1)} %get-tuple-element.60), channel_id=1, source_target_pairs={{0,127},{1,112},{2,113},{3,114},{4,115},{5,116},{6,117},{7,118},{8... | collective-permute-start | bytes 172040 | tf_op jit(solution)/shard_map/ppermute | solution.py:433
  28.7 4.6 %collective-permute-start.7 = (bf16[224,128]{1,0:T(8,128)(2,1)S(1)}, bf16[224,128]{1,0:T(8,128)(2,1)S(1)}, u32[]{:S(2)}, u32[]{:S(2)}) collective-permute-start(bf16[224,128]{1,0:T(8,128)(2,1)S(1)} %get-tuple-element.61), channel_id=1, source_target_pairs={{0,112},{1,113},{2,114},{3,115},{4,116},{5,117},{6,118},{7,119},{8... | collective-permute-start | bytes 172040 | tf_op jit(solution)/shard_map/ppermute | solution.py:433
  33.3 5.0 %copy-start = (f32[768]{0:T(1024)S(1)}, f32[768]{0:T(1024)}, u32[]{:S(2)}) copy-start(f32[768]{0:T(1024)} %param.23) | copy-start | bytes 9220
  37.4 9.1 %collective-permute-start.10 = (bf16[224,128]{1,0:T(8,128)(2,1)S(1)}, bf16[224,128]{1,0:T(8,128)(2,1)S(1)}, u32[]{:S(2)}, u32[]{:S(2)}) collective-permute-start(bf16[224,128]{1,0:T(8,128)(2,1)S(1)} %get-tuple-element.69), channel_id=1, source_target_pairs={{0,17},{1,18},{2,19},{3,20},{4,21},{5,22},{6,23},{7,24},{8,25},{9,... | collective-permute-start | bytes 172040 | tf_op jit(solution)/shard_map/ppermute | solution.py:433
  38.1 8.4 %collective-permute-start.8 = (bf16[224,128]{1,0:T(8,128)(2,1)S(1)}, bf16[224,128]{1,0:T(8,128)(2,1)S(1)}, u32[]{:S(2)}, u32[]{:S(2)}) collective-permute-start(bf16[224,128]{1,0:T(8,128)(2,1)S(1)} %get-tuple-element.67), channel_id=1, source_target_pairs={{0,16},{1,17},{2,18},{3,19},{4,20},{5,21},{6,22},{7,23},{8,24},{9,... | collective-permute-start | bytes 172040 | tf_op jit(solution)/shard_map/ppermute | solution.py:433
  38.1 8.4 %collective-permute-start.9 = (bf16[224,128]{1,0:T(8,128)(2,1)S(1)}, bf16[224,128]{1,0:T(8,128)(2,1)S(1)}, u32[]{:S(2)}, u32[]{:S(2)}) collective-permute-start(bf16[224,128]{1,0:T(8,128)(2,1)S(1)} %get-tuple-element.68), channel_id=1, source_target_pairs={{0,1},{1,2},{2,3},{3,4},{4,5},{5,6},{6,7},{7,8},{8,9},{9,10},{10,1... | collective-permute-start | bytes 172040 | tf_op jit(solution)/shard_map/ppermute | solution.py:433
where the time goes:
time: 49.1 us; the launch traced here: 48.9 us
  Pallas kernels  21.4 us (44%)
  starting transfers between devices  19 us (39%)
  waiting for transfers between devices  8.22 us (17%)
    pallas_call x11, Pallas kernels, call(): pl.pallas_call(kernel, name=name, out_shape=outs, in_specs=in_specs or [V...  21.4 us
    ppermute x5, starting transfers between devices, turned(): return lax.ppermute(block, 'lon', route)  9.7 us
    ppermute x6, starting transfers between devices, sent(): return lax.ppermute(block, ('lat', 'lon'), route)  9.31 us
    ppermute x6, waiting for transfers between devices, sent(): return lax.ppermute(block, ('lat', 'lon'), route)  7.18 us
    ppermute x5, waiting for transfers between devices, turned(): return lax.ppermute(block, 'lon', route)  1.04 us
  transfers between devices with their start and end apart: 11, of which 4 were waited for; matrix products, arithmetic and copies ran while one was open for 0% of the time, Pallas kernels for 21%

commit v1 on v0

v1 whole, which is shorter than its diff:
```python
import functools

import jax
import jax.numpy as jnp
import numpy as np
from jax import lax
from jax.experimental import pallas as pl
from jax.experimental.pallas import tpu as pltpu
from jax.sharding import PartitionSpec as P

BF16 = jnp.bfloat16
F32 = jnp.float32
C = 192
HEADS = 6
HEAD_SIZE = 32
HIDDEN = 768
LEVELS, ROWS, COLS = 8, 6, 12
WINDOWS = 4
TOKENS = 144
CELLS = 576
RUN = 24
SPAN = 23
HALF = 6 * SPAN
GROUP = 128
KEYS = 2 * GROUP
LATS, LONS = 8, 16
SHARD = 1242
SHIFT = 12.0
MASKED = -1e30


def one_hot(sources, width):
    sources = np.asarray(sources)
    matrix = np.zeros((len(sources), width), np.float32)
    rows = np.nonzero(sources >= 0)[0]
    matrix[rows, sources[rows]] = 1.0
    return jnp.asarray(matrix, BF16)


ROW_HALF = (1, 0, 1, 0)


def own_half(quarter):
    odd = lax.rem(lax.axis_index("lat"), 2)
    return (1 - odd, odd, odd, 1 - odd)[quarter]


def window_half(quarter):
    odd = lax.rem(lax.axis_index("lat"), 2)
    return (odd, odd, 1 - odd, 1 - odd)[quarter]


def query_order():
    return [level * 72 + c * 6 + r for c in range(COLS) for level in range(2) for r in range(ROWS)]


def natural_order():
    return [c * 12 + level * 6 + r for level in range(2) for c in range(COLS) for r in range(ROWS)]


def quarter_runs(qr, qc):
    starts = [qc * (6 * ROWS * LEVELS) + (c * ROWS + 3 * qr) * LEVELS for c in range(6)]
    return [pl.ds(pl.multiple_of(start, LEVELS), RUN) for start in starts]


def level_cells(level):
    return pl.ds(level, ROWS * COLS, stride=LEVELS)


def read_window(cells, first_level):
    parts = [
        jnp.concatenate([cells[0, level_cells(level % LEVELS)], cells[1, level_cells(level % LEVELS)]], axis=1)
        for level in (first_level, first_level + 1)
    ]
    return jnp.concatenate(parts, axis=0)[:, :C]


def write_window(cells, first_level, values):
    wide = jnp.concatenate([values, jnp.zeros((TOKENS, 2 * GROUP - C), F32)], axis=1)
    for offset in range(2):
        rows = wide[offset * 72 : (offset + 1) * 72]
        where = level_cells((first_level + offset) % LEVELS)
        cells[0, where] = rows[:, :GROUP]
        cells[1, where] = rows[:, GROUP:]


def read_quarter(cells, qr, qc):
    parts = [jnp.concatenate([cells[0, run, :], cells[1, run, :]], axis=1) for run in quarter_runs(qr, qc)]
    return jnp.concatenate(parts, axis=0)[:, :C]


def write_quarter(cells, qr, qc, values):
    wide = jnp.concatenate([values, jnp.zeros((TOKENS, 2 * GROUP - C), F32)], axis=1)
    for c, run in enumerate(quarter_runs(qr, qc)):
        cells[0, run, :] = wide[c * RUN : (c + 1) * RUN, :GROUP]
        cells[1, run, :] = wide[c * RUN : (c + 1) * RUN, GROUP:]


def layer_norm(values, scales):
    average = jnp.mean(values, axis=-1, keepdims=True)
    centred = values - average
    spread = jnp.mean(centred * centred, axis=-1, keepdims=True)
    return centred * lax.rsqrt(spread + 1e-05) * scales


def dot(a, b):
    return jnp.dot(a, b, preferred_element_type=F32)


def dot_transposed(a, b):
    return lax.dot_general(a, b, (((1,), (1,)), ((), ())), preferred_element_type=F32)


def moved(choice, rows):
    return dot(choice, rows).astype(BF16)


def head_lanes(head):
    lane = lax.broadcasted_iota(jnp.int32, (1, C), 1)
    return (lane >= head * HEAD_SIZE) & (lane < (head + 1) * HEAD_SIZE)


def project(normed, qkv_weight, orders):
    queries = moved(orders[0], dot(normed, qkv_weight[:, :C]).astype(BF16))
    pad = jnp.zeros((GROUP - 72, C), F32)

    def padded(part):
        return jnp.concatenate([part[:72], pad, part[72:], pad], axis=0).astype(BF16)

    keys = padded(dot(normed, qkv_weight[:, C : 2 * C]))
    values = padded(dot(normed, qkv_weight[:, 2 * C :]))
    ones = jnp.ones((KEYS, KEYS - C), BF16)
    return queries, keys, jnp.concatenate([values, ones], axis=1)


def score(queries, keys):
    stacked = jnp.concatenate(
        [jnp.where(head_lanes(h), queries, jnp.zeros((), BF16)) for h in range(HEADS)], axis=0
    )
    return dot_transposed(stacked, keys) * HEAD_SIZE ** (-0.5)


def blend(scores, values, bias_of):
    weights = []
    for h in range(HEADS):
        part = scores[h * TOKENS : (h + 1) * TOKENS] + bias_of(h)
        weights.append(jnp.exp(part).astype(BF16))
    blended = dot(jnp.concatenate(weights, axis=0), values)
    total = jnp.zeros((TOKENS, C), F32)
    result = jnp.zeros((TOKENS, C), F32)
    for h in range(HEADS):
        part = blended[h * TOKENS : (h + 1) * TOKENS]
        result = jnp.where(head_lanes(h), part[:, :C], result)
        total = jnp.where(head_lanes(h), part[:, C : C + 1], total)
    return (result / jnp.maximum(total, np.exp(-SHIFT))).astype(BF16)


def selected_bias(z_even, z_odd, window, head):
    rows = []
    for at in range(6):
        lanes = slice(at * GROUP, (at + 1) * GROUP)
        halves = []
        for key_level in range(2):
            first = head * 128 + (key_level * 4 + window) * 16
            top = z_even[first : first + 16, lanes]
            low = z_odd[first : first + 16, lanes]
            halves.append(jnp.concatenate([top[:8], top[8:] + low[:8], low[8:]], axis=0))
        rows.append(jnp.concatenate(halves, axis=1))
    return jnp.concatenate(rows, axis=0)


def window_lanes(tile, first):
    turn = (GROUP - first) % GROUP
    near = pltpu.roll(tile[:, :GROUP], turn, 1) if turn else tile[:, :GROUP]
    if first + 72 <= GROUP:
        return near
    lane = lax.broadcasted_iota(jnp.int32, (1, GROUP), 1)
    return jnp.where(lane < GROUP - first, near, pltpu.roll(tile[:, GROUP:], turn, 1))


def expanded_bias(t_top, t_low, window, head):
    halves = []
    for key_level in range(2):
        first = head * 128 + (key_level * 4 + window) * 16
        top_tile, low_tile = t_top[first : first + 16], t_low[first : first + 16]
        rows = []
        for column in range(0, 12, 2):
            top = window_lanes(top_tile, (11 - column) * ROWS)
            low = window_lanes(low_tile, (10 - column) * ROWS)
            rows += [top[:8], top[8:] + low[:8], low[8:]]
        halves.append(jnp.concatenate(rows, axis=0))
    return jnp.concatenate(halves, axis=1)


def picked_rows(table_ref, table_choice):
    tops, lows = [], []
    for h in range(HEADS):
        picked = moved(table_choice, table_ref[h * 192 : (h + 1) * 192, :HALF])
        tops.append(picked[:128])
        lows.append(picked[128:])
    return jnp.concatenate(tops, axis=0), jnp.concatenate(lows, axis=0)


def erf_gelu(values):
    return 0.5 * values * (1.0 + lax.erf(values * np.float32(np.sqrt(0.5))))


def feed_forward(middle, gain, fc1, fc2, keep):
    hidden = erf_gelu(dot(layer_norm(middle, gain).astype(BF16), fc1)).astype(BF16)
    return jnp.where(keep, middle + dot_transposed(hidden, fc2), 0.0).astype(BF16)


def pack_piece(piece):
    side = jnp.concatenate(
        [piece[:80, 128:], jnp.concatenate([piece[80:, 128:], piece[:16, 128:]], axis=0)], axis=1
    )
    return jnp.concatenate([piece[:, :128], side], axis=0)


def unpack_piece(packed):
    side = packed[TOKENS:]
    ends = jnp.concatenate([side[:, :64], side[: TOKENS - 80, 64:]], axis=0)
    return jnp.concatenate([packed[:TOKENS], ends], axis=1)


def prepare_masks(lat_valid, first_mask, second_mask, keep):
    lat = lax.axis_index("lat")

    def flag(row):
        return lat_valid[row] > 0

    lane = lax.broadcasted_iota(jnp.int32, (8, KEYS), 1)
    inner = lax.rem(lane, GROUP)
    key_row = jnp.where(inner < 72, lax.rem(inner, ROWS), -1)
    mask = jnp.full((8, KEYS), MASKED, F32)
    usable = jnp.full((8, KEYS), MASKED, F32)
    for r in range(ROWS):
        mask = jnp.where((key_row == r) & flag(lat * ROWS + r), -SHIFT, mask)
        rolled = lax.rem(lat * ROWS + 3 + r, LATS * ROWS)
        usable = jnp.where((key_row == r) & flag(rolled), 0.0, usable)
    first_mask[...] = mask
    a = lax.rem(lax.broadcasted_iota(jnp.int32, (TOKENS, 1), 0), 12)
    query_half = jnp.where(lax.rem(a, ROWS) >= 3, 1, 0)
    key_half = jnp.where(key_row[:1] >= 3, 1, 0)
    same_rows = (query_half == key_half) | (lat != LATS - 1)
    same_level = jnp.where(a >= ROWS, 1, 0) == jnp.where(lane[:1] >= GROUP, 1, 0)
    whole = jnp.where(same_rows, usable[:1], MASKED)
    second_mask[0] = whole
    second_mask[1] = jnp.where(same_level, whole, MASKED)
    for half in range(2):
        for r in range(3):
            value = jnp.where(flag(lat * ROWS + 3 * half + r), 1.0, 0.0)
            for c in range(6):
                at = (c * 3 + r) * LEVELS
                keep[half, at : at + LEVELS] = jnp.full((LEVELS, GROUP), value, F32)


def fetch(sources, held, sems):
    copies = [pltpu.make_async_copy(a, b, sems.at[n]) for n, (a, b) in enumerate(zip(sources, held))]
    for copy in copies:
        copy.start()
    return copies


def sliced(kernel, layers, *refs):
    kernel(*[ref.at[layers[at]] if at in layers else ref for at, ref in enumerate(refs)])


def fetch_kernel(*refs):
    sources, held, (first_mask, second_mask, keep, flags, sems) = refs[:6], refs[6:11], refs[11:]
    copies = fetch(sources, (flags,) + tuple(held), sems)
    copies[0].wait()
    prepare_masks(flags, first_mask, second_mask, keep)
    for copy in copies[1:]:
        copy.wait()


def choose(row_keys, lane_keys):
    return jnp.where(row_keys == lane_keys, 1.0, 0.0).astype(BF16)


def prepare_kernel(mine, proj, fc1, fc2, *refs):
    copies = fetch((proj, fc1, fc2), refs[:3], refs[-1])
    lanes, rows, columns = refs[3:6]

    def place(shape, axis):
        return lax.broadcasted_iota(jnp.int32, shape, axis)

    at = place((HALF, 1), 0)
    row, position = at // SPAN, lax.rem(at, SPAN)
    lanes[...] = choose(position * ROWS + row, place((HALF, KEYS), 1))
    at = place((256, 1), 0)
    a = lax.rem(at, 16) - 4 * (at // 128)
    source = (a * 2 + lax.rem(at // 64, 2)) * 8 + lax.rem(at // 16, 4)
    for block in range(2):
        rows[block] = choose(jnp.where((a >= 0) & (a < 12), source + 4 * block, -1), place((256, 192), 1))
    lane = place((1, 6 * GROUP), 1)
    inner = lax.rem(lane, GROUP)
    for parity in range(2):
        met = inner // ROWS - (lane // GROUP * 2 + parity) + 11
        wanted = jnp.where(inner < 72, met * ROWS + lax.rem(inner, ROWS), -1)
        columns[parity] = choose(position * ROWS + row, wanted)
    for copy in copies:
        copy.wait()


def join_kernel(*refs):
    at = 0
    for ref in refs[:-1]:
        if ref.shape[1:] == refs[-1].shape[1:]:
            refs[-1][at : at + ref.shape[0]] = ref[...]
            at += ref.shape[0]


def before_kernel(halves, x, gains, qkv_weight, query_choice, *refs):
    sources, (scores_out, v_out, cells), held, sems = refs[:5], refs[5:8], refs[8:13], refs[13]
    copies = fetch(sources, held, sems)
    wide = jnp.concatenate([x[...].astype(F32), jnp.zeros((CELLS, 2 * GROUP - C), F32)], axis=1)
    for r in range(ROWS):
        for c in range(COLS):
            group = wide[(r * COLS + c) * LEVELS : (r * COLS + c + 1) * LEVELS]
            at = (c * ROWS + r) * LEVELS
            cells[0, at : at + LEVELS] = group[:, :GROUP]
            cells[1, at : at + LEVELS] = group[:, GROUP:]
    for p in range(WINDOWS):
        normed = layer_norm(read_window(cells, 2 * p), gains[0, 0:1]).astype(BF16)
        q, k, v_out[p] = project(normed, qkv_weight[...], query_choice)
        scores_out[p] = score(q, k)
    for copy in copies:
        copy.wait()


def first_quarter(quarter, inputs, cells, gains, fc1, fc2, keep):
    qr, qc = ROW_HALF[quarter], own_half(quarter)
    middle = read_quarter(inputs, qr, qc) + read_quarter(cells, qr, qc).astype(BF16).astype(F32)
    return feed_forward(middle, gains[0, 1:2], fc1[...], fc2[...], keep[qr][:, :1] > 0)


def first_kernel(mine, theirs, scores, v, first_mask, keep, inputs, gains, query_choice, proj, fc1, fc2, lanes, rows, sent_lat, sent_lon, sent_both, table_out, out, cells, table_f32, t_top, t_low):
    me = lax.axis_index("lon")
    for g in range(LONS):
        slot = lax.rem(me // 2 - g // 2 + 8, 4) * 2 + jnp.where(me // 8 == g // 8, 0, 1)
        shard = jnp.where(lax.rem(me, 2) == g % 2, mine[slot], theirs[slot]).astype(F32)
        piece = jnp.concatenate([shard[0], shard[1]], axis=0)
        for n in range(9):
            at = (g * 9 + n) * 8
            table_f32[at : at + 8, :HALF] = piece[:, n * HALF : (n + 1) * HALF]
    table_out[:, :HALF] = table_f32[:, :HALF].astype(BF16)
    tops, lows = picked_rows(table_out, rows[0])
    t_top[...] = dot(tops, lanes[...])
    t_low[...] = dot(lows, lanes[...])
    mask = first_mask[0:1]
    for p in range(WINDOWS):
        blended = blend(scores[p], v[p], lambda h: expanded_bias(t_top, t_low, p, h) + mask)
        write_window(cells, 2 * p, dot(moved(query_choice[1], blended), proj[...]))
    for quarter, target in ((2, sent_lon), (3, sent_both), (1, sent_lat)):
        result = first_quarter(quarter, inputs, cells, gains, fc1, fc2, keep)
        out[(quarter - 1) * TOKENS : quarter * TOKENS] = result
        target[...] = pack_piece(result)


def bias_kernel(table, second_mask, columns, rows, inputs, cells, gains, fc1, fc2, keep, bias_out, near, z_even, z_odd):
    near[...] = first_quarter(0, inputs, cells, gains, fc1, fc2, keep)
    tops, lows = picked_rows(table, rows[1])
    z_even[...] = dot(tops, columns[0])
    z_odd[...] = dot(lows, columns[1])
    for p in range(WINDOWS):
        for h in range(HEADS):
            whole = selected_bias(z_even, z_odd, p, h) + second_mask[1 if p == WINDOWS - 1 else 0]
            bias_out[p, h * TOKENS : (h + 1) * TOKENS] = whole.astype(BF16)


def write_normed(cells, quarter, piece, gains):
    normed = layer_norm(piece.astype(F32), gains[1, 0:1]).astype(BF16)
    write_quarter(cells, 1 - ROW_HALF[quarter], window_half(quarter), normed.astype(F32))


def ready_kernel(near, from_lon, from_both, gains, cells):
    write_normed(cells, 0, near[...], gains)
    write_normed(cells, 2, unpack_piece(from_lon[...]), gains)
    write_normed(cells, 3, unpack_piece(from_both[...]), gains)


def second_kernel(given, from_lat, bias, gains, qkv_weight, proj, query_choice, own, sent_lat, sent_lon, sent_both, cells, results):
    cells[...] = given[...]
    write_normed(cells, 1, unpack_piece(from_lat[...]), gains)
    for p in range(WINDOWS):
        normed = read_window(cells, 2 * p + 1).astype(BF16)
        q, k, v = project(normed, qkv_weight[...], query_choice)

        def bias_of(h):
            return bias[p, h * TOKENS : (h + 1) * TOKENS].astype(F32) - SHIFT

        blended = blend(score(q, k), v, bias_of)
        write_window(results, 2 * p + 1, dot(moved(query_choice[1], blended), proj[...]))
    pieces = [read_quarter(results, 1 - ROW_HALF[k], window_half(k)).astype(BF16) for k in range(4)]
    own[...] = pieces[0]
    sent_lat[...] = pack_piece(pieces[1])
    sent_lon[...] = pack_piece(pieces[2])
    sent_both[...] = pack_piece(pieces[3])


def own_kernel(keep, near, own, gains, fc1, fc2, result):
    middle = near[...].astype(F32) + own[...].astype(F32)
    result[...] = feed_forward(middle, gains[1, 1:2], fc1[...], fc2[...], keep[1][:, :1] > 0)


def add_kernel(far, from_lon, from_both, middle):
    for at, piece in enumerate((from_lon, from_both)):
        inputs = far[(at + 1) * TOKENS : (at + 2) * TOKENS].astype(F32)
        middle[at] = inputs + unpack_piece(piece[...]).astype(F32)


def last_kernel(keep, far, done, middle, from_lat, gains, fc1, fc2, merge_gain, merge_weight, merged):
    results = [done[...].astype(F32)]
    upper = far[:TOKENS].astype(F32) + unpack_piece(from_lat[...]).astype(F32)
    for quarter, whole in ((1, upper), (2, middle[0]), (3, middle[1])):
        flags = keep[ROW_HALF[quarter]][:, :1] > 0
        results.append(feed_forward(whole, gains[1, 1:2], fc1[...], fc2[...], flags).astype(F32))
    odd = lax.rem(lax.axis_index("lat"), 2) == 1
    groups = {}
    for qr, (first, second) in enumerate(((1, 3), (0, 2))):
        turned_round = odd if qr == 1 else jnp.logical_not(odd)
        right = jnp.where(turned_round, results[second], results[first])
        left = jnp.where(turned_round, results[first], results[second])
        for qc, result in enumerate((left, right)):
            for r in range(3):
                for c in range(6):
                    at = (c * 3 + r) * LEVELS
                    groups[3 * qr + r, 6 * qc + c] = result[at : at + LEVELS]
    parts = [
        jnp.concatenate([groups[2 * r + dr, 2 * c + dc] for r in range(3) for c in range(6)], axis=0)
        for dr in range(2)
        for dc in range(2)
    ]
    average = sum(jnp.sum(part, axis=-1, keepdims=True) for part in parts) / (4 * C)
    parts = [part - average for part in parts]
    spread = sum(jnp.sum(part * part, axis=-1, keepdims=True) for part in parts) / (4 * C)
    scale = lax.rsqrt(spread + 1e-05)
    total = jnp.zeros((TOKENS, 2 * C), F32)
    for d, part in enumerate(parts):
        normed = (part * scale * merge_gain[d : d + 1]).astype(BF16)
        total = total + dot(normed, merge_weight[d * C : (d + 1) * C])
    merged[...] = total.astype(BF16)


VMEM_SPEC = pl.BlockSpec(memory_space=pltpu.VMEM)
SMEM_SPEC = pl.BlockSpec(memory_space=pltpu.SMEM)


def call(kernel, name, micros, outs, scratch, *operands, in_specs=None, aliases=None):
    return pl.pallas_call(
        kernel,
        name=name,
        out_shape=outs,
        in_specs=in_specs or [VMEM_SPEC] * len(operands),
        out_specs=jax.tree.map(lambda _: VMEM_SPEC, outs),
        scratch_shapes=scratch,
        input_output_aliases=aliases or {},
        cost_estimate=pl.CostEstimate(flops=int(micros * 1e9), bytes_accessed=2**20, transcendentals=0),
        compiler_params=pltpu.CompilerParams(vmem_limit_bytes=16 * 2**20),
    )(*operands)


def shape(*dims, dtype=BF16):
    return jax.ShapeDtypeStruct(dims, dtype)


def sent(block, rows, across, back=False):
    route = []
    for i in range(LATS):
        for j in range(LONS):
            to = (i + rows) % LATS
            owner = i if back else to
            step = (1 if owner % 2 == 1 else -1) * (-1 if back else 1)
            route.append((i * LONS + j, to * LONS + (j + across * step) % LONS))
    return lax.ppermute(block, ("lat", "lon"), route)


def turned(block, place):
    route = []
    for j in range(LONS):
        z, x, core = place(j // 8, j // 2 % 4, j % 2)
        route.append((j, z * 8 + x * 2 + core))
    return lax.ppermute(block, "lon", route)


def shards(state, lat_valid, norm_gains, qkv_weight, proj_weight, fc1_weight, fc2_weight, earth_bias, merge_gain, merge_weight):
    shard = earth_bias[:, 0]
    cells = pltpu.VMEM((2, CELLS, GROUP), F32)
    cell_rows = shape(2, CELLS, GROUP, dtype=F32)
    t_scratch = [pltpu.VMEM((768, KEYS), F32), pltpu.VMEM((768, KEYS), F32)]
    packed = shape(224, 128)

    def in_hbm(array):
        return pltpu.with_memory_space_constraint(array, pltpu.HBM)

    def like(arrays):
        return [shape(*array.shape, dtype=array.dtype) for array in arrays]

    hbm_spec = pl.BlockSpec(memory_space=pltpu.HBM)
    fc2_turned = jnp.swapaxes(fc2_weight, 1, 2)
    early = [
        shard[None],
        state.transpose(1, 2, 0, 3).reshape(CELLS, C),
        norm_gains,
        qkv_weight,
        jnp.stack([one_hot(query_order(), TOKENS), one_hot(natural_order(), TOKENS)]),
    ]
    late = [merge_weight, qkv_weight, proj_weight, fc1_weight, fc2_turned]
    layer = [shape(C, C), shape(C, HIDDEN), shape(C, HIDDEN)]
    other_half = turned(shard, lambda z, x, core: (1 - z, x, core))
    held_shard, x, gains, qkv0, query_choice, first_mask, second_mask, keep = call(
        functools.partial(sliced, fetch_kernel, {4: 0}),
        "fetch",
        1.4,
        like(early[:3])
        + [shape(C, 3 * C)]
        + like(early[4:])
        + [
            shape(8, KEYS, dtype=F32),
            shape(2, TOKENS, KEYS, dtype=F32),
            shape(2, TOKENS, GROUP, dtype=F32),
        ],
        [pltpu.SMEM((LATS * ROWS,), jnp.int32), pltpu.SemaphoreType.DMA((len(early) + 1,))],
        in_hbm(lat_valid),
        *[in_hbm(array) for array in early],
        in_specs=[hbm_spec] * (len(early) + 1),
    )
    halves = call(join_kernel, "halves", 0.2, shape(2, 2, WINDOWS, SHARD), [], held_shard, other_half[None])
    ring = [turned(halves, lambda z, x, core: (z, (x + hop) % 4, core)) for hop in range(1, 4)]
    scores, v, inputs, merge, qkv1, proj1, fc1_1, fc2_1 = call(
        functools.partial(sliced, before_kernel, {6: 1, 7: 1, 8: 1, 9: 1}),
        "before",
        2.5,
        [shape(WINDOWS, HEADS * TOKENS, KEYS, dtype=F32), shape(WINDOWS, KEYS, KEYS), cell_rows]
        + like([merge_weight])
        + [shape(C, 3 * C)]
        + layer,
        [pltpu.SemaphoreType.DMA((len(late),))],
        halves, x, gains, qkv0, query_choice,
        *[in_hbm(array) for array in late],
        in_specs=[VMEM_SPEC] * 5 + [hbm_spec] * len(late),
    )
    mine = call(join_kernel, "mine", 0.3, shape(8, 2, WINDOWS, SHARD), [], halves, *ring, v)
    theirs = turned(mine, lambda z, x, core: (z, x, 1 - core))
    proj0, fc1_0, fc2_0, lanes, rows, columns = call(
        functools.partial(sliced, prepare_kernel, {1: 0, 2: 0, 3: 0}),
        "prepare",
        1.2,
        layer + [shape(HALF, KEYS), shape(2, 256, 192), shape(2, HALF, 6 * GROUP)],
        [pltpu.SemaphoreType.DMA((3,))],
        mine, in_hbm(proj_weight), in_hbm(fc1_weight), in_hbm(fc2_turned),
        in_specs=[VMEM_SPEC] + [hbm_spec] * 3,
    )
    to_lat, to_lon, to_both, tables, far, attended = call(
        first_kernel,
        "first",
        4.5,
        [packed, packed, packed, shape(1152, KEYS), shape(3 * TOKENS, C), cell_rows],
        [pltpu.VMEM((1152, KEYS), F32)] + t_scratch,
        mine, theirs, scores, v, first_mask, keep, inputs, gains, query_choice, proj0, fc1_0, fc2_0, lanes, rows,
    )
    from_lat, from_lon, from_both = sent(to_lat, -1, 0), sent(to_lon, 0, 1), sent(to_both, -1, 1)
    bias, near = call(
        bias_kernel,
        "bias",
        0.2,
        [shape(WINDOWS, HEADS * TOKENS, KEYS), shape(TOKENS, C)],
        [pltpu.VMEM((768, 768), F32), pltpu.VMEM((768, 768), F32)],
        tables, second_mask, columns, rows, inputs, attended, gains, fc1_0, fc2_0, keep,
    )
    ready = call(ready_kernel, "ready", 0.4, cell_rows, [], near, from_lon, from_both, gains)
    own, to_lat, to_lon, to_both = call(
        second_kernel,
        "second",
        4.5,
        [shape(TOKENS, C), packed, packed, packed],
        [cells, cells],
        ready, from_lat, bias, gains, qkv1, proj1, query_choice,
    )
    from_lon, from_both, from_lat = sent(to_lon, 0, 1, True), sent(to_both, 1, 1, True), sent(to_lat, 1, 0, True)
    done = call(own_kernel, "own", 0.5, shape(TOKENS, C), [], keep, near, own, gains, fc1_1, fc2_1)
    middle = call(
        add_kernel, "add", 0.2, shape(2, TOKENS, C, dtype=F32), [], far, from_lon, from_both
    )
    merged = call(
        last_kernel,
        "last",
        2.0,
        shape(TOKENS, 2 * C),
        [],
        keep, far, done, middle, from_lat, gains, fc1_1, fc2_1, merge_gain.reshape(4, C), merge,
    )
    return merged.reshape(3, 6, LEVELS, 2 * C).transpose(2, 0, 1, 3)


def solution(mesh):
    return jax.shard_map(
        shards,
        mesh=mesh,
        in_specs=(
            P(None, "lat", "lon", None),
            P(),
            P(),
            P(),
            P(),
            P(),
            P(),
            P(None, "lat", None, "lon"),
            P(),
            P(),
        ),
        out_specs=P(None, "lat", "lon", None),
        check_vma=False,
    )
```

time: 49.1 us -> 48.3 us (0.984)
  the two profiles are of different devices: /device:TPU:0 before, /device:TPU:7 now
where the time goes in v1:
time: 48.3 us; the launch traced here: 48.2 us
  starting transfers between devices  21.4 us (44%)
  Pallas kernels  18.3 us (38%)
  waiting for transfers between devices  8.31 us (17%)
    pallas_call x12, Pallas kernels, call(): pl.pallas_call(kernel, name=name, out_shape=outs, in_specs=in_specs or [V...  18.3 us
    ppermute x6, starting transfers between devices, sent(): return lax.ppermute(block, ('lat', 'lon'), route)  12.1 us
    ppermute x5, starting transfers between devices, turned(): return lax.ppermute(block, 'lon', route)  9.27 us
    ppermute x6, waiting for transfers between devices, sent(): return lax.ppermute(block, ('lat', 'lon'), route)  6.86 us
    ppermute x5, waiting for transfers between devices, turned(): return lax.ppermute(block, 'lon', route)  1.45 us
  transfers between devices with their start and end apart: 11, of which 4 were waited for; matrix products, arithmetic and copies ran while one was open for 0% of the time, Pallas kernels for 15%

profile of v1, /device:TPU:7, one launch (start us, length us, event | category | flops | bytes accessed | tf_op | source)
XLA Modules:
  0.0 48.2 jit_solution(15802727213003618619)
XLA Ops:
  0.0 3.6 %collective-permute-start = (bf16[2,4,1242]{2,1,0:T(4,128)(2,1)}, bf16[2,4,1242]{2,1,0:T(4,128)(2,1)S(1)}, u32[]{:S(2)}, u32[]{:S(2)}) collective-permute-start(bf16[2,4,1242]{2,1,0:T(4,128)(2,1)} %bitcast.14), channel_id=1, source_target_pairs={{0,8},{1,9},{2,10},{3,11},{4,12},{5,13},{6,14},{7,15},{8,0},{9,1},... | collective-permute-start | bytes 59624 | tf_op jit(solution)/shard_map/ppermute | solution.py:485
  3.6 1.2 %fetch.1 = (bf16[1,2,4,1242]{3,2,1,0:T(4,128)(2,1)S(1)}, bf16[576,192]{1,0:T(8,128)(2,1)S(1)}, f32[2,2,192]{2,1,0:T(2,128)S(1)}, bf16[192,576]{1,0:T(8,128)(2,1)...) custom-call(s32[48]{0:T(128)} %refs_0_.1, ...), custom_call_target="tpu_custom_call" | custom-call | flops 1400000000 | bytes 1048576 | tf_op jit(solution)/shard_map/fetch/pallas_call | solution.py:452
  4.8 0.2 collective-permute-done
  5.0 0.2 collective-permute-start.1
  5.2 2.1 %collective-permute-start.2 = (bf16[2,2,4,1242]{3,2,1,0:T(4,128)(2,1)S(1)}, bf16[2,2,4,1242]{3,2,1,0:T(4,128)(2,1)S(1)}, u32[]{:S(2)}, u32[]{:S(2)}) collective-permute-start(bf16[2,2,4,1242]{3,2,1,0:T(4,128)(2,1)S(1)} %halves.1.refs_0_), channel_id=1, source_target_pairs={{0,4},{1,5},{2,6},{3,7},{4,0},{5,1},{6,2},{7,3},{8,12},{9,13},{10,... | collective-permute-start | bytes 119240 | tf_op jit(solution)/shard_map/ppermute | solution.py:485
  7.3 0.0 collective-permute-start.3
  7.3 2.8 %before.1 = (f32[4,864,256]{2,1,0:T(8,128)S(1)}, bf16[4,256,256]{2,1,0:T(8,128)(2,1)S(1)}, f32[2,576,128]{2,1,0:T(8,128)S(1)}, bf16[768,384]{1,0:T(8,128)(2,1)S(...) custom-call(bf16[2,2,4,1242]{3,2,1,0:T(4,128)(2,1)S(1)} %halves.1.re, ...), custom_call_target="tpu_custom_call" | custom-call | flops 2500000000 | bytes 1048576 | tf_op jit(solution)/shard_map/before/pallas_call | solution.py:452
  10.1 0.0 collective-permute-done.1.refs_1_
  10.1 0.0 collective-permute-done.2.refs_2_
  10.1 1.3 %collective-permute-done.3.refs_3_ = bf16[2,2,4,1242]{3,2,1,0:T(4,128)(2,1)S(1)} collective-permute-done((bf16[2,2,4,1242]{3,2,1,0:T(4,128)(2,1)S(1)}, bf16[2,2,4,1242]{3,2,1,0:T(4,128)(2,1)S(1)}, u32[]{:S(2)}, u32[]{:S(2)}) %collective-permute-start.3) | collective-permute-done | bytes 39776 | tf_op jit(solution)/shard_map/ppermute | solution.py:485
  11.4 3.3 %collective-permute-start.4 = (bf16[8,2,4,1242]{3,2,1,0:T(4,128)(2,1)S(1)}, bf16[8,2,4,1242]{3,2,1,0:T(4,128)(2,1)S(1)}, u32[]{:S(2)}, u32[]{:S(2)}) collective-permute-start(bf16[8,2,4,1242]{3,2,1,0:T(4,128)(2,1)S(1)} %mine.1.refs_0_), channel_id=1, source_target_pairs={{0,1},{1,0},{2,3},{3,2},{4,5},{5,4},{6,7},{7,6},{8,9},{9,8},{10,11... | collective-permute-start | bytes 476936 | tf_op jit(solution)/shard_map/ppermute | solution.py:485
  14.7 1.1 %prepare.1 = (bf16[192,192]{1,0:T(8,128)(2,1)S(1)}, bf16[192,768]{1,0:T(8,128)(2,1)S(1)}, bf16[192,768]{1,0:T(8,128)(2,1)S(1)}, bf16[138,256]{1,0:T(8,128)(2,1)S...) custom-call(bf16[8,2,4,1242]{3,2,1,0:T(4,128)(2,1)S(1)} %mine.1.refs_0_, ...), custom_call_target="tpu_custom_call" | custom-call | flops 1200000000 | bytes 1048576 | tf_op jit(solution)/shard_map/prepare/pallas_call | solution.py:452
  15.9 0.0 collective-permute-done.4.theirs
  15.9 4.4 %first.1 = (bf16[224,128]{1,0:T(8,128)(2,1)S(1)}, bf16[224,128]{1,0:T(8,128)(2,1)S(1)}, bf16[224,128]{1,0:T(8,128)(2,1)S(1)}, bf16[1152,256]{1,0:T(8,128)(2,1)S(...) custom-call(bf16[8,2,4,1242]{3,2,1,0:T(4,128)(2,1)S(1)} %mine.1.refs_0_, ...), custom_call_target="tpu_custom_call" | custom-call | flops 4499999744 | bytes 1048576 | tf_op jit(solution)/shard_map/first/pallas_call | solution.py:452
  20.2 0.3 collective-permute-start.5
  20.5 6.3 %collective-permute-start.6 = (bf16[224,128]{1,0:T(8,128)(2,1)S(1)}, bf16[224,128]{1,0:T(8,128)(2,1)S(1)}, u32[]{:S(2)}, u32[]{:S(2)}) collective-permute-start(bf16[224,128]{1,0:T(8,128)(2,1)S(1)} %get-tuple-element.61), channel_id=1, source_target_pairs={{0,113},{1,114},{2,115},{3,116},{4,117},{5,118},{6,119},{7,120},{8... | collective-permute-start | bytes 172040 | tf_op jit(solution)/shard_map/ppermute | solution.py:477
  26.8 0.3 collective-permute-start.7
  27.2 1.4 %bias.1 = (bf16[4,864,256]{2,1,0:T(8,128)(2,1)S(1)}, bf16[144,192]{1,0:T(8,128)(2,1)S(1)}) custom-call(bf16[1152,256]{1,0:T(8,128)(2,1)S(1)} %get-tuple-element.55.table, f32[2,144,256]{2,1,0:T(8,128)S(1)} %get-tuple-element.56.second_mask, bf16[2,138,768]{2,1,0:T(8,128)(2,1)S(1)} %get-tuple-element.57.columns, ...), custom_call_target="tpu_custom_call" | custom-call | flops 200000000 | bytes 1048576 | tf_op jit(solution)/shard_map/bias/pallas_call | solution.py:452
  28.5 0.0 collective-permute-done.5.from_lon
  28.6 0.0 collective-permute-done.6.from_both
  28.6 0.3 ready.1.given
  28.9 1.0 %collective-permute-done.7.from_lat = bf16[224,128]{1,0:T(8,128)(2,1)S(1)} collective-permute-done((bf16[224,128]{1,0:T(8,128)(2,1)S(1)}, bf16[224,128]{1,0:T(8,128)(2,1)S(1)}, u32[]{:S(2)}, u32[]{:S(2)}) %collective-permute-start.7) | collective-permute-done | bytes 57376 | tf_op jit(solution)/shard_map/ppermute | solution.py:477
  29.9 0.0 copy-start
  29.9 4.2 %second.1 = (bf16[144,192]{1,0:T(8,128)(2,1)S(1)}, bf16[224,128]{1,0:T(8,128)(2,1)S(1)}, bf16[224,128]{1,0:T(8,128)(2,1)S(1)}, bf16[224,128]{1,0:T(8,128)(2,1)S(1)}) custom-call(f32[2,576,128]{2,1,0:T(8,128)S(1)} %ready.1.given, bf16[224,128]{1,0:T(8,128)(2,1)S(1)} %collective-permute-done.7.from_lat, bf16[4,864,256]{2,1,0:T(8,128)(2,1)S(1)} %get-tuple-element.63.bias, ...), custom_call_target="tpu_custom_call" | custom-call | flops 4499999744 | bytes 1048576 | tf_op jit(solution)/shard_map/second/pallas_call | solution.py:452
  34.0 2.7 %collective-permute-start.8 = (bf16[224,128]{1,0:T(8,128)(2,1)S(1)}, bf16[224,128]{1,0:T(8,128)(2,1)S(1)}, u32[]{:S(2)}, u32[]{:S(2)}) collective-permute-start(bf16[224,128]{1,0:T(8,128)(2,1)S(1)} %get-tuple-element.69), channel_id=1, source_target_pairs={{0,1},{1,2},{2,3},{3,4},{4,5},{5,6},{6,7},{7,8},{8,9},{9,10},{10,1... | collective-permute-start | bytes 172040 | tf_op jit(solution)/shard_map/ppermute | solution.py:477
  36.7 2.5 %collective-permute-start.9 = (bf16[224,128]{1,0:T(8,128)(2,1)S(1)}, bf16[224,128]{1,0:T(8,128)(2,1)S(1)}, u32[]{:S(2)}, u32[]{:S(2)}) collective-permute-start(bf16[224,128]{1,0:T(8,128)(2,1)S(1)} %get-tuple-element.70), channel_id=1, source_target_pairs={{0,17},{1,18},{2,19},{3,20},{4,21},{5,22},{6,23},{7,24},{8,25},{9,... | collective-permute-start | bytes 172040 | tf_op jit(solution)/shard_map/ppermute | solution.py:477
  39.2 0.0 copy-done
  39.2 0.1 reshape.10.merge_gain
  39.3 0.0 collective-permute-start.10
  39.3 0.5 %own.1.done = bf16[144,192]{1,0:T(8,128)(2,1)S(1)} custom-call(f32[2,144,128]{2,1,0:T(8,128)S(1)} %get-tuple-element.39.keep, bf16[144,192]{1,0:T(8,128)(2,1)S(1)} %get-tuple-element.59.near, bf16[144,192]{1,0:T(8,128)(2,1)S(1)} %get-tuple-element.66.own, f32[2,2,192]{2,1,0:T(2,128)S(1)} %get-tuple-element.42.refs_2_.gains, ...), custom_call_target="tpu_custom_call" | custom-call | flops 500000000 | bytes 1048576 | tf_op jit(solution)/shard_map/own/pallas_call | solution.py:452
  39.9 0.0 collective-permute-done.8.from_lon
  39.9 5.9 %collective-permute-done.9.from_both = bf16[224,128]{1,0:T(8,128)(2,1)S(1)} collective-permute-done((bf16[224,128]{1,0:T(8,128)(2,1)S(1)}, bf16[224,128]{1,0:T(8,128)(2,1)S(1)}, u32[]{:S(2)}, u32[]{:S(2)}) %collective-permute-start.9) | collective-permute-done | bytes 57376 | tf_op jit(solution)/shard_map/ppermute | solution.py:477
  45.8 0.1 add.1.middle
  45.9 0.0 collective-permute-done.10.from_lat
  45.9 2.3 %last.1 = bf16[144,384]{1,0:T(8,128)(2,1)} custom-call(f32[2,144,128]{2,1,0:T(8,128)S(1)} %get-tuple-element.39.keep, bf16[432,192]{1,0:T(8,128)(2,1)S(1)} %get-tuple-element.54.far, bf16[144,192]{1,0:T(8,128)(2,1)S(1)} %own.1.done, f32[2,144,192]{2,1,0:T(8,128)S(1)} %add.1.middle, bf16[224,128]{1,0:T(8,128)(2,1)S(1)} %collective-permute-done.10.from_lat, ...), custom_call_target="tpu_custom_call" | custom-call | flops 2000000000 | bytes 1048576 | tf_op jit(solution)/shard_map/last/pallas_call | solution.py:452
  (2 shorter events, 0.0 us)
Async XLA Ops:
  0.0 5.0 %collective-permute-start = (bf16[2,4,1242]{2,1,0:T(4,128)(2,1)}, bf16[2,4,1242]{2,1,0:T(4,128)(2,1)S(1)}, u32[]{:S(2)}, u32[]{:S(2)}) collective-permute-start(bf16[2,4,1242]{2,1,0:T(4,128)(2,1)} %bitcast.14), channel_id=1, source_target_pairs={{0,8},{1,9},{2,10},{3,11},{4,12},{5,13},{6,14},{7,15},{8,0},{9,1},... | collective-permute-start | bytes 59624 | tf_op jit(solution)/shard_map/ppermute | solution.py:485
  5.0 5.1 %collective-permute-start.1 = (bf16[2,2,4,1242]{3,2,1,0:T(4,128)(2,1)S(1)}, bf16[2,2,4,1242]{3,2,1,0:T(4,128)(2,1)S(1)}, u32[]{:S(2)}, u32[]{:S(2)}) collective-permute-start(bf16[2,2,4,1242]{3,2,1,0:T(4,128)(2,1)S(1)} %halves.1.refs_0_), channel_id=1, source_target_pairs={{0,2},{1,3},{2,4},{3,5},{4,6},{5,7},{6,0},{7,1},{8,10},{9,11},{10,... | collective-permute-start | bytes 119240 | tf_op jit(solution)/shard_map/ppermute | solution.py:485
  5.2 4.9 %collective-permute-start.2 = (bf16[2,2,4,1242]{3,2,1,0:T(4,128)(2,1)S(1)}, bf16[2,2,4,1242]{3,2,1,0:T(4,128)(2,1)S(1)}, u32[]{:S(2)}, u32[]{:S(2)}) collective-permute-start(bf16[2,2,4,1242]{3,2,1,0:T(4,128)(2,1)S(1)} %halves.1.refs_0_), channel_id=1, source_target_pairs={{0,4},{1,5},{2,6},{3,7},{4,0},{5,1},{6,2},{7,3},{8,12},{9,13},{10,... | collective-permute-start | bytes 119240 | tf_op jit(solution)/shard_map/ppermute | solution.py:485
  7.3 4.1 %collective-permute-start.3 = (bf16[2,2,4,1242]{3,2,1,0:T(4,128)(2,1)S(1)}, bf16[2,2,4,1242]{3,2,1,0:T(4,128)(2,1)S(1)}, u32[]{:S(2)}, u32[]{:S(2)}) collective-permute-start(bf16[2,2,4,1242]{3,2,1,0:T(4,128)(2,1)S(1)} %halves.1.refs_0_), channel_id=1, source_target_pairs={{0,6},{1,7},{2,0},{3,1},{4,2},{5,3},{6,4},{7,5},{8,14},{9,15},{10,... | collective-permute-start | bytes 119240 | tf_op jit(solution)/shard_map/ppermute | solution.py:485
  11.4 4.5 %collective-permute-start.4 = (bf16[8,2,4,1242]{3,2,1,0:T(4,128)(2,1)S(1)}, bf16[8,2,4,1242]{3,2,1,0:T(4,128)(2,1)S(1)}, u32[]{:S(2)}, u32[]{:S(2)}) collective-permute-start(bf16[8,2,4,1242]{3,2,1,0:T(4,128)(2,1)S(1)} %mine.1.refs_0_), channel_id=1, source_target_pairs={{0,1},{1,0},{2,3},{3,2},{4,5},{5,4},{6,7},{7,6},{8,9},{9,8},{10,11... | collective-permute-start | bytes 476936 | tf_op jit(solution)/shard_map/ppermute | solution.py:485
  20.2 8.3 %collective-permute-start.5 = (bf16[224,128]{1,0:T(8,128)(2,1)S(1)}, bf16[224,128]{1,0:T(8,128)(2,1)S(1)}, u32[]{:S(2)}, u32[]{:S(2)}) collective-permute-start(bf16[224,128]{1,0:T(8,128)(2,1)S(1)} %get-tuple-element.60), channel_id=1, source_target_pairs={{0,15},{1,0},{2,1},{3,2},{4,3},{5,4},{6,5},{7,6},{8,7},{9,8},{10,9... | collective-permute-start | bytes 172040 | tf_op jit(solution)/shard_map/ppermute | solution.py:477
  20.5 8.0 %collective-permute-start.6 = (bf16[224,128]{1,0:T(8,128)(2,1)S(1)}, bf16[224,128]{1,0:T(8,128)(2,1)S(1)}, u32[]{:S(2)}, u32[]{:S(2)}) collective-permute-start(bf16[224,128]{1,0:T(8,128)(2,1)S(1)} %get-tuple-element.61), channel_id=1, source_target_pairs={{0,113},{1,114},{2,115},{3,116},{4,117},{5,118},{6,119},{7,120},{8... | collective-permute-start | bytes 172040 | tf_op jit(solution)/shard_map/ppermute | solution.py:477
  26.8 3.0 %collective-permute-start.7 = (bf16[224,128]{1,0:T(8,128)(2,1)S(1)}, bf16[224,128]{1,0:T(8,128)(2,1)S(1)}, u32[]{:S(2)}, u32[]{:S(2)}) collective-permute-start(bf16[224,128]{1,0:T(8,128)(2,1)S(1)} %get-tuple-element.62), channel_id=1, source_target_pairs={{0,112},{1,113},{2,114},{3,115},{4,116},{5,117},{6,118},{7,119},{8... | collective-permute-start | bytes 172040 | tf_op jit(solution)/shard_map/ppermute | solution.py:477
  29.9 9.4 %copy-start = (f32[768]{0:T(1024)S(1)}, f32[768]{0:T(1024)}, u32[]{:S(2)}) copy-start(f32[768]{0:T(1024)} %param.20) | copy-start | bytes 9220
  34.0 5.8 %collective-permute-start.8 = (bf16[224,128]{1,0:T(8,128)(2,1)S(1)}, bf16[224,128]{1,0:T(8,128)(2,1)S(1)}, u32[]{:S(2)}, u32[]{:S(2)}) collective-permute-start(bf16[224,128]{1,0:T(8,128)(2,1)S(1)} %get-tuple-element.69), channel_id=1, source_target_pairs={{0,1},{1,2},{2,3},{3,4},{4,5},{5,6},{6,7},{7,8},{8,9},{9,10},{10,1... | collective-permute-start | bytes 172040 | tf_op jit(solution)/shard_map/ppermute | solution.py:477
  36.7 9.0 %collective-permute-start.9 = (bf16[224,128]{1,0:T(8,128)(2,1)S(1)}, bf16[224,128]{1,0:T(8,128)(2,1)S(1)}, u32[]{:S(2)}, u32[]{:S(2)}) collective-permute-start(bf16[224,128]{1,0:T(8,128)(2,1)S(1)} %get-tuple-element.70), channel_id=1, source_target_pairs={{0,17},{1,18},{2,19},{3,20},{4,21},{5,22},{6,23},{7,24},{8,25},{9,... | collective-permute-start | bytes 172040 | tf_op jit(solution)/shard_map/ppermute | solution.py:477
  39.3 6.6 %collective-permute-start.10 = (bf16[224,128]{1,0:T(8,128)(2,1)S(1)}, bf16[224,128]{1,0:T(8,128)(2,1)S(1)}, u32[]{:S(2)}, u32[]{:S(2)}) collective-permute-start(bf16[224,128]{1,0:T(8,128)(2,1)S(1)} %get-tuple-element.71), channel_id=1, source_target_pairs={{0,16},{1,17},{2,18},{3,19},{4,20},{5,21},{6,22},{7,23},{8,24},{9,... | collective-permute-start | bytes 172040 | tf_op jit(solution)/shard_map/ppermute | solution.py:477

commit v2 on v1

--- a/solution.py
+++ b/solution.py
@@ -121,16 +121,28 @@
 
 
 def project(normed, qkv_weight, orders):
-    queries = moved(orders[0], dot(normed, qkv_weight[:, :C]).astype(BF16))
+    all_queries = dot(normed, qkv_weight[:, :C]).astype(BF16)
+    all_keys = dot(normed, qkv_weight[:, C : 2 * C])
+    all_values = dot(normed, qkv_weight[:, 2 * C :])
     pad = jnp.zeros((GROUP - 72, C), F32)
+    ones = jnp.ones((KEYS, KEYS - C), BF16)
 
     def padded(part):
         return jnp.concatenate([part[:72], pad, part[72:], pad], axis=0).astype(BF16)
 
-    keys = padded(dot(normed, qkv_weight[:, C : 2 * C]))
-    values = padded(dot(normed, qkv_weight[:, 2 * C :]))
-    ones = jnp.ones((KEYS, KEYS - C), BF16)
-    return queries, keys, jnp.concatenate([values, ones], axis=1)
+    results = []
+    for p in range(WINDOWS):
+        rows = slice(p * TOKENS, (p + 1) * TOKENS)
+        values = jnp.concatenate([padded(all_values[rows]), ones], axis=1)
+        results.append((moved(orders[0], all_queries[rows]), padded(all_keys[rows]), values))
+    return results
+
+
+def write_attended(cells, first_level, blended, orders, proj):
+    natural = jnp.concatenate([moved(orders[1], part) for part in blended], axis=0)
+    attended = dot(natural, proj)
+    for p in range(WINDOWS):
+        write_window(cells, 2 * p + first_level, attended[p * TOKENS : (p + 1) * TOKENS])
 
 
 def score(queries, keys):
@@ -208,6 +220,11 @@
 def feed_forward(middle, gain, fc1, fc2, keep):
     hidden = erf_gelu(dot(layer_norm(middle, gain).astype(BF16), fc1)).astype(BF16)
     return jnp.where(keep, middle + dot_transposed(hidden, fc2), 0.0).astype(BF16)
+
+
+def finished(quarters, middle, gain, fc1, fc2, keep):
+    flags = jnp.concatenate([keep[ROW_HALF[quarter]][:, :1] for quarter in quarters], axis=0) > 0
+    return feed_forward(jnp.concatenate(middle, axis=0), gain, fc1[...], fc2[...], flags)
 
 
 def pack_piece(piece):
@@ -313,7 +330,7 @@
 
 
 def before_kernel(halves, x, gains, qkv_weight, query_choice, *refs):
-    sources, (scores_out, v_out, cells), held, sems = refs[:5], refs[5:8], refs[8:13], refs[13]
+    sources, (scores_out, v_out, cells), held, sems = refs[:2], refs[2:5], refs[5:7], refs[7]
     copies = fetch(sources, held, sems)
     wide = jnp.concatenate([x[...].astype(F32), jnp.zeros((CELLS, 2 * GROUP - C), F32)], axis=1)
     for r in range(ROWS):
@@ -322,18 +339,21 @@
             at = (c * ROWS + r) * LEVELS
             cells[0, at : at + LEVELS] = group[:, :GROUP]
             cells[1, at : at + LEVELS] = group[:, GROUP:]
-    for p in range(WINDOWS):
-        normed = layer_norm(read_window(cells, 2 * p), gains[0, 0:1]).astype(BF16)
-        q, k, v_out[p] = project(normed, qkv_weight[...], query_choice)
+    windows = jnp.concatenate([read_window(cells, 2 * p) for p in range(WINDOWS)], axis=0)
+    normed = layer_norm(windows, gains[0, 0:1]).astype(BF16)
+    for p, (q, k, v) in enumerate(project(normed, qkv_weight[...], query_choice)):
+        v_out[p] = v
         scores_out[p] = score(q, k)
     for copy in copies:
         copy.wait()
 
 
-def first_quarter(quarter, inputs, cells, gains, fc1, fc2, keep):
-    qr, qc = ROW_HALF[quarter], own_half(quarter)
-    middle = read_quarter(inputs, qr, qc) + read_quarter(cells, qr, qc).astype(BF16).astype(F32)
-    return feed_forward(middle, gains[0, 1:2], fc1[...], fc2[...], keep[qr][:, :1] > 0)
+def first_quarters(quarters, inputs, cells, gains, fc1, fc2, keep):
+    middle = []
+    for quarter in quarters:
+        qr, qc = ROW_HALF[quarter], own_half(quarter)
+        middle.append(read_quarter(inputs, qr, qc) + read_quarter(cells, qr, qc).astype(BF16).astype(F32))
+    return finished(quarters, middle, gains[0, 1:2], fc1, fc2, keep)
 
 
 def first_kernel(mine, theirs, scores, v, first_mask, keep, inputs, gains, query_choice, proj, fc1, fc2, lanes, rows, sent_lat, sent_lon, sent_both, table_out, out, cells, table_f32, t_top, t_low):
@@ -350,17 +370,16 @@
     t_top[...] = dot(tops, lanes[...])
     t_low[...] = dot(lows, lanes[...])
     mask = first_mask[0:1]
-    for p in range(WINDOWS):
-        blended = blend(scores[p], v[p], lambda h: expanded_bias(t_top, t_low, p, h) + mask)
-        write_window(cells, 2 * p, dot(moved(query_choice[1], blended), proj[...]))
-    for quarter, target in ((2, sent_lon), (3, sent_both), (1, sent_lat)):
-        result = first_quarter(quarter, inputs, cells, gains, fc1, fc2, keep)
-        out[(quarter - 1) * TOKENS : quarter * TOKENS] = result
-        target[...] = pack_piece(result)
+    blended = [blend(scores[p], v[p], lambda h: expanded_bias(t_top, t_low, p, h) + mask) for p in range(WINDOWS)]
+    write_attended(cells, 0, blended, query_choice, proj[...])
+    results = first_quarters((1, 2, 3), inputs, cells, gains, fc1, fc2, keep)
+    out[...] = results
+    for at, target in enumerate((sent_lat, sent_lon, sent_both)):
+        target[...] = pack_piece(results[at * TOKENS : (at + 1) * TOKENS])
 
 
 def bias_kernel(table, second_mask, columns, rows, inputs, cells, gains, fc1, fc2, keep, bias_out, near, z_even, z_odd):
-    near[...] = first_quarter(0, inputs, cells, gains, fc1, fc2, keep)
+    near[...] = first_quarters((0,), inputs, cells, gains, fc1, fc2, keep)
     tops, lows = picked_rows(table, rows[1])
     z_even[...] = dot(tops, columns[0])
     z_odd[...] = dot(lows, columns[1])
@@ -384,15 +403,15 @@
 def second_kernel(given, from_lat, bias, gains, qkv_weight, proj, query_choice, own, sent_lat, sent_lon, sent_both, cells, results):
     cells[...] = given[...]
     write_normed(cells, 1, unpack_piece(from_lat[...]), gains)
-    for p in range(WINDOWS):
-        normed = read_window(cells, 2 * p + 1).astype(BF16)
-        q, k, v = project(normed, qkv_weight[...], query_choice)
+    normed = jnp.concatenate([read_window(cells, 2 * p + 1) for p in range(WINDOWS)], axis=0).astype(BF16)
+    blended = []
+    for p, (q, k, v) in enumerate(project(normed, qkv_weight[...], query_choice)):
 
         def bias_of(h):
             return bias[p, h * TOKENS : (h + 1) * TOKENS].astype(F32) - SHIFT
 
-        blended = blend(score(q, k), v, bias_of)
-        write_window(results, 2 * p + 1, dot(moved(query_choice[1], blended), proj[...]))
+        blended.append(blend(score(q, k), v, bias_of))
+    write_attended(results, 1, blended, query_choice, proj[...])
     pieces = [read_quarter(results, 1 - ROW_HALF[k], window_half(k)).astype(BF16) for k in range(4)]
     own[...] = pieces[0]
     sent_lat[...] = pack_piece(pieces[1])
@@ -400,9 +419,12 @@
     sent_both[...] = pack_piece(pieces[3])
 
 
-def own_kernel(keep, near, own, gains, fc1, fc2, result):
+def own_kernel(fc1, fc2, merge, keep, near, own, gains, result, *refs):
+    copies = fetch((fc1, fc2, merge), refs[:3], refs[3])
     middle = near[...].astype(F32) + own[...].astype(F32)
-    result[...] = feed_forward(middle, gains[1, 1:2], fc1[...], fc2[...], keep[1][:, :1] > 0)
+    for copy in copies:
+        copy.wait()
+    result[...] = feed_forward(middle, gains[1, 1:2], refs[0][...], refs[1][...], keep[1][:, :1] > 0)
 
 
 def add_kernel(far, from_lon, from_both, middle):
@@ -412,11 +434,9 @@
 
 
 def last_kernel(keep, far, done, middle, from_lat, gains, fc1, fc2, merge_gain, merge_weight, merged):
-    results = [done[...].astype(F32)]
     upper = far[:TOKENS].astype(F32) + unpack_piece(from_lat[...]).astype(F32)
-    for quarter, whole in ((1, upper), (2, middle[0]), (3, middle[1])):
-        flags = keep[ROW_HALF[quarter]][:, :1] > 0
-        results.append(feed_forward(whole, gains[1, 1:2], fc1[...], fc2[...], flags).astype(F32))
+    fresh = finished((1, 2, 3), [upper, middle[0], middle[1]], gains[1, 1:2], fc1, fc2, keep).astype(F32)
+    results = [done[...].astype(F32)] + [fresh[at * TOKENS : (at + 1) * TOKENS] for at in range(3)]
     odd = lax.rem(lax.axis_index("lat"), 2) == 1
     groups = {}
     for qr, (first, second) in enumerate(((1, 3), (0, 2))):
@@ -507,7 +527,7 @@
         qkv_weight,
         jnp.stack([one_hot(query_order(), TOKENS), one_hot(natural_order(), TOKENS)]),
     ]
-    late = [merge_weight, qkv_weight, proj_weight, fc1_weight, fc2_turned]
+    late = [qkv_weight, proj_weight]
     layer = [shape(C, C), shape(C, HIDDEN), shape(C, HIDDEN)]
     other_half = turned(shard, lambda z, x, core: (1 - z, x, core))
     held_shard, x, gains, qkv0, query_choice, first_mask, second_mask, keep = call(
@@ -529,14 +549,12 @@
     )
     halves = call(join_kernel, "halves", 0.2, shape(2, 2, WINDOWS, SHARD), [], held_shard, other_half[None])
     ring = [turned(halves, lambda z, x, core: (z, (x + hop) % 4, core)) for hop in range(1, 4)]
-    scores, v, inputs, merge, qkv1, proj1, fc1_1, fc2_1 = call(
-        functools.partial(sliced, before_kernel, {6: 1, 7: 1, 8: 1, 9: 1}),
+    scores, v, inputs, qkv1, proj1 = call(
+        functools.partial(sliced, before_kernel, {5: 1, 6: 1}),
         "before",
         2.5,
         [shape(WINDOWS, HEADS * TOKENS, KEYS, dtype=F32), shape(WINDOWS, KEYS, KEYS), cell_rows]
-        + like([merge_weight])
-        + [shape(C, 3 * C)]
-        + layer,
+        + [shape(C, 3 * C), shape(C, C)],
         [pltpu.SemaphoreType.DMA((len(late),))],
         halves, x, gains, qkv0, query_choice,
         *[in_hbm(array) for array in late],
@@ -580,7 +598,15 @@
         ready, from_lat, bias, gains, qkv1, proj1, query_choice,
     )
     from_lon, from_both, from_lat = sent(to_lon, 0, 1, True), sent(to_both, 1, 1, True), sent(to_lat, 1, 0, True)
-    done = call(own_kernel, "own", 0.5, shape(TOKENS, C), [], keep, near, own, gains, fc1_1, fc2_1)
+    done, fc1_1, fc2_1, merge = call(
+        functools.partial(sliced, own_kernel, {0: 1, 1: 1}),
+        "own",
+        0.5,
+        [shape(TOKENS, C)] + layer[1:] + like([merge_weight]),
+        [pltpu.SemaphoreType.DMA((3,))],
+        in_hbm(fc1_weight), in_hbm(fc2_turned), in_hbm(merge_weight), keep, near, own, gains,
+        in_specs=[hbm_spec] * 3 + [VMEM_SPEC] * 4,
+    )
     middle = call(
         add_kernel, "add", 0.2, shape(2, TOKENS, C, dtype=F32), [], far, from_lon, from_both
     )

time: 48.3 us -> 45.5 us (0.942)
  Pallas kernels: 18.3 us -> 15.9 us
    pallas_call x12, Pallas kernels: 18.3 us -> 15.9 us  [call(): pl.pallas_call(kernel, name=name, out_shape=outs, in_specs=in_specs or [V...]
    ppermute x6, waiting for transfers between devices: 6.86 us -> 5.44 us  [sent(): return lax.ppermute(block, ('lat', 'lon'), route)]
    ppermute x5, waiting for transfers between devices: 1.45 us -> 2.74 us  [turned(): return lax.ppermute(block, 'lon', route)]
  transfers between devices with their start and end apart: 11 -> 11, of which waited for: 4 -> 5; matrix products, arithmetic and copies ran while one was open for 0% -> 0% of each run, Pallas kernels for 15% -> 16%
where the time goes in v2:
time: 45.5 us; the launch traced here: 45.3 us
  starting transfers between devices  21 us (46%)
  Pallas kernels  15.9 us (35%)
  waiting for transfers between devices  8.18 us (18%)
    pallas_call x12, Pallas kernels, call(): pl.pallas_call(kernel, name=name, out_shape=outs, in_specs=in_specs or [V...  15.9 us
    ppermute x6, starting transfers between devices, sent(): return lax.ppermute(block, ('lat', 'lon'), route)  11.7 us
    ppermute x5, starting transfers between devices, turned(): return lax.ppermute(block, 'lon', route)  9.27 us
    ppermute x6, waiting for transfers between devices, sent(): return lax.ppermute(block, ('lat', 'lon'), route)  5.44 us
    ppermute x5, waiting for transfers between devices, turned(): return lax.ppermute(block, 'lon', route)  2.74 us
  transfers between devices with their start and end apart: 11, of which 5 were waited for; matrix products, arithmetic and copies ran while one was open for 0% of the time, Pallas kernels for 16%

profile of v2, /device:TPU:7, one launch (start us, length us, event | category | flops | bytes accessed | tf_op | source)
XLA Modules:
  0.0 45.3 jit_solution(8079069392798235305)
XLA Ops:
  0.0 3.6 %collective-permute-start = (bf16[2,4,1242]{2,1,0:T(4,128)(2,1)}, bf16[2,4,1242]{2,1,0:T(4,128)(2,1)S(1)}, u32[]{:S(2)}, u32[]{:S(2)}) collective-permute-start(bf16[2,4,1242]{2,1,0:T(4,128)(2,1)} %bitcast.14), channel_id=1, source_target_pairs={{0,8},{1,9},{2,10},{3,11},{4,12},{5,13},{6,14},{7,15},{8,0},{9,1},... | collective-permute-start | bytes 59624 | tf_op jit(solution)/shard_map/ppermute | solution.py:505
  3.6 1.2 %fetch.1 = (bf16[1,2,4,1242]{3,2,1,0:T(4,128)(2,1)S(1)}, bf16[576,192]{1,0:T(8,128)(2,1)S(1)}, f32[2,2,192]{2,1,0:T(2,128)S(1)}, bf16[192,576]{1,0:T(8,128)(2,1)...) custom-call(s32[48]{0:T(128)} %refs_0_.2, ...), custom_call_target="tpu_custom_call" | custom-call | flops 1400000000 | bytes 1048576 | tf_op jit(solution)/shard_map/fetch/pallas_call | solution.py:472
  4.8 0.2 collective-permute-done
  5.0 0.2 collective-permute-start.1
  5.2 2.1 %collective-permute-start.2 = (bf16[2,2,4,1242]{3,2,1,0:T(4,128)(2,1)S(1)}, bf16[2,2,4,1242]{3,2,1,0:T(4,128)(2,1)S(1)}, u32[]{:S(2)}, u32[]{:S(2)}) collective-permute-start(bf16[2,2,4,1242]{3,2,1,0:T(4,128)(2,1)S(1)} %halves.1.refs_0_), channel_id=1, source_target_pairs={{0,4},{1,5},{2,6},{3,7},{4,0},{5,1},{6,2},{7,3},{8,12},{9,13},{10,... | collective-permute-start | bytes 119240 | tf_op jit(solution)/shard_map/ppermute | solution.py:505
  7.3 0.0 collective-permute-start.3
  7.3 1.5 %before.1 = (f32[4,864,256]{2,1,0:T(8,128)S(1)}, bf16[4,256,256]{2,1,0:T(8,128)(2,1)S(1)}, f32[2,576,128]{2,1,0:T(8,128)S(1)}, bf16[192,576]{1,0:T(8,128)(2,1)S(1)}, bf16[192,192]{1,0:T(8,128)(2,1)S(1)}) custom-call(bf16[2,2,4,1242]{3,2,1,0:T(4,128)(2,1)S(1)} %halves.1.refs_0_, bf16[576,192]{1,0:T(8,128)(2,1)S(1)} %get-tuple-element.42.refs_1_, ...), custom_call_target="tpu_custom_call" | custom-call | flops 2500000000 | bytes 1048576 | tf_op jit(solution)/shard_map/before/pallas_call | solution.py:472
  8.8 0.0 collective-permute-done.1.refs_1_
  8.8 0.7 %collective-permute-done.2.refs_2_ = bf16[2,2,4,1242]{3,2,1,0:T(4,128)(2,1)S(1)} collective-permute-done((bf16[2,2,4,1242]{3,2,1,0:T(4,128)(2,1)S(1)}, bf16[2,2,4,1242]{3,2,1,0:T(4,128)(2,1)S(1)}, u32[]{:S(2)}, u32[]{:S(2)}) %collective-permute-start.2) | collective-permute-done | bytes 39776 | tf_op jit(solution)/shard_map/ppermute | solution.py:505
  9.5 1.8 %collective-permute-done.3.refs_3_ = bf16[2,2,4,1242]{3,2,1,0:T(4,128)(2,1)S(1)} collective-permute-done((bf16[2,2,4,1242]{3,2,1,0:T(4,128)(2,1)S(1)}, bf16[2,2,4,1242]{3,2,1,0:T(4,128)(2,1)S(1)}, u32[]{:S(2)}, u32[]{:S(2)}) %collective-permute-start.3) | collective-permute-done | bytes 39776 | tf_op jit(solution)/shard_map/ppermute | solution.py:505
  11.4 3.3 %collective-permute-start.4 = (bf16[8,2,4,1242]{3,2,1,0:T(4,128)(2,1)S(1)}, bf16[8,2,4,1242]{3,2,1,0:T(4,128)(2,1)S(1)}, u32[]{:S(2)}, u32[]{:S(2)}) collective-permute-start(bf16[8,2,4,1242]{3,2,1,0:T(4,128)(2,1)S(1)} %mine.1.refs_0_), channel_id=1, source_target_pairs={{0,1},{1,0},{2,3},{3,2},{4,5},{5,4},{6,7},{7,6},{8,9},{9,8},{10,11... | collective-permute-start | bytes 476936 | tf_op jit(solution)/shard_map/ppermute | solution.py:505
  14.7 1.1 %prepare.1 = (bf16[192,192]{1,0:T(8,128)(2,1)S(1)}, bf16[192,768]{1,0:T(8,128)(2,1)S(1)}, bf16[192,768]{1,0:T(8,128)(2,1)S(1)}, bf16[138,256]{1,0:T(8,128)(2,1)S...) custom-call(bf16[8,2,4,1242]{3,2,1,0:T(4,128)(2,1)S(1)} %mine.1.refs_0_, ...), custom_call_target="tpu_custom_call" | custom-call | flops 1200000000 | bytes 1048576 | tf_op jit(solution)/shard_map/prepare/pallas_call | solution.py:472
  15.9 0.0 collective-permute-done.4.theirs
  15.9 3.9 %first.1 = (bf16[224,128]{1,0:T(8,128)(2,1)S(1)}, bf16[224,128]{1,0:T(8,128)(2,1)S(1)}, bf16[224,128]{1,0:T(8,128)(2,1)S(1)}, bf16[1152,256]{1,0:T(8,128)(2,1)S(...) custom-call(bf16[8,2,4,1242]{3,2,1,0:T(4,128)(2,1)S(1)} %mine.1.refs_0_, ...), custom_call_target="tpu_custom_call" | custom-call | flops 4499999744 | bytes 1048576 | tf_op jit(solution)/shard_map/first/pallas_call | solution.py:472
  19.8 0.3 collective-permute-start.5
  20.1 6.1 %collective-permute-start.6 = (bf16[224,128]{1,0:T(8,128)(2,1)S(1)}, bf16[224,128]{1,0:T(8,128)(2,1)S(1)}, u32[]{:S(2)}, u32[]{:S(2)}) collective-permute-start(bf16[224,128]{1,0:T(8,128)(2,1)S(1)} %get-tuple-element.62), channel_id=1, source_target_pairs={{0,113},{1,114},{2,115},{3,116},{4,117},{5,118},{6,119},{7,120},{8... | collective-permute-start | bytes 172040 | tf_op jit(solution)/shard_map/ppermute | solution.py:497
  26.1 0.3 collective-permute-start.7
  26.5 1.4 %bias.1 = (bf16[4,864,256]{2,1,0:T(8,128)(2,1)S(1)}, bf16[144,192]{1,0:T(8,128)(2,1)S(1)}) custom-call(bf16[1152,256]{1,0:T(8,128)(2,1)S(1)} %get-tuple-element.56.table, f32[2,144,256]{2,1,0:T(8,128)S(1)} %get-tuple-element.57.second_mask, bf16[2,138,768]{2,1,0:T(8,128)(2,1)S(1)} %get-tuple-element.58.columns, ...), custom_call_target="tpu_custom_call" | custom-call | flops 200000000 | bytes 1048576 | tf_op jit(solution)/shard_map/bias/pallas_call | solution.py:472
  27.9 0.0 collective-permute-done.5.from_lon
  27.9 0.0 collective-permute-done.6.from_both
  27.9 0.3 ready.1.given
  28.2 1.0 %collective-permute-done.7.from_lat = bf16[224,128]{1,0:T(8,128)(2,1)S(1)} collective-permute-done((bf16[224,128]{1,0:T(8,128)(2,1)S(1)}, bf16[224,128]{1,0:T(8,128)(2,1)S(1)}, u32[]{:S(2)}, u32[]{:S(2)}) %collective-permute-start.7) | collective-permute-done | bytes 57376 | tf_op jit(solution)/shard_map/ppermute | solution.py:497
  29.2 0.0 copy-start
  29.2 2.4 %second.1 = (bf16[144,192]{1,0:T(8,128)(2,1)S(1)}, bf16[224,128]{1,0:T(8,128)(2,1)S(1)}, bf16[224,128]{1,0:T(8,128)(2,1)S(1)}, bf16[224,128]{1,0:T(8,128)(2,1)S(1)}) custom-call(f32[2,576,128]{2,1,0:T(8,128)S(1)} %ready.1.given, bf16[224,128]{1,0:T(8,128)(2,1)S(1)} %collective-permute-done.7.from_lat, bf16[4,864,256]{2,1,0:T(8,128)(2,1)S(1)} %get-tuple-element.64.bias, ...), custom_call_target="tpu_custom_call" | custom-call | flops 4499999744 | bytes 1048576 | tf_op jit(solution)/shard_map/second/pallas_call | solution.py:472
  31.5 2.4 %collective-permute-start.8 = (bf16[224,128]{1,0:T(8,128)(2,1)S(1)}, bf16[224,128]{1,0:T(8,128)(2,1)S(1)}, u32[]{:S(2)}, u32[]{:S(2)}) collective-permute-start(bf16[224,128]{1,0:T(8,128)(2,1)S(1)} %get-tuple-element.69), channel_id=1, source_target_pairs={{0,1},{1,2},{2,3},{3,4},{4,5},{5,6},{6,7},{7,8},{8,9},{9,10},{10,1... | collective-permute-start | bytes 172040 | tf_op jit(solution)/shard_map/ppermute | solution.py:497
  34.0 2.6 %collective-permute-start.9 = (bf16[224,128]{1,0:T(8,128)(2,1)S(1)}, bf16[224,128]{1,0:T(8,128)(2,1)S(1)}, u32[]{:S(2)}, u32[]{:S(2)}) collective-permute-start(bf16[224,128]{1,0:T(8,128)(2,1)S(1)} %get-tuple-element.70), channel_id=1, source_target_pairs={{0,17},{1,18},{2,19},{3,20},{4,21},{5,22},{6,23},{7,24},{8,25},{9,... | collective-permute-start | bytes 172040 | tf_op jit(solution)/shard_map/ppermute | solution.py:497
  36.6 0.0 copy-done
  36.6 0.1 reshape.10.merge_gain
  36.7 0.0 collective-permute-start.10
  36.7 1.8 %own.1 = (bf16[144,192]{1,0:T(8,128)(2,1)S(1)}, bf16[192,768]{1,0:T(8,128)(2,1)S(1)}, bf16[192,768]{1,0:T(8,128)(2,1)S(1)}, bf16[768,384]{1,0:T(8,128)(2,1)S(1)}) custom-call(bf16[2,192,768]{2,1,0:T(8,128)(2,1)} %refs_0_.3, bf16[2,192,768]{2,1,0:T(8,128)(2,1)} %bitcast.12, bf16[768,384]{1,0:T(8,128)(2,1)} %refs_2_.3, ...), custom_call_target="tpu_custom_call" | custom-call | flops 500000000 | bytes 1048576 | tf_op jit(solution)/shard_map/own/pallas_call | solution.py:472
  38.5 0.0 collective-permute-done.8.from_lon
  38.5 4.5 %collective-permute-done.9.from_both = bf16[224,128]{1,0:T(8,128)(2,1)S(1)} collective-permute-done((bf16[224,128]{1,0:T(8,128)(2,1)S(1)}, bf16[224,128]{1,0:T(8,128)(2,1)S(1)}, u32[]{:S(2)}, u32[]{:S(2)}) %collective-permute-start.9) | collective-permute-done | bytes 57376 | tf_op jit(solution)/shard_map/ppermute | solution.py:497
  43.0 0.1 add.1.middle
  43.1 0.0 collective-permute-done.10.from_lat
  43.1 2.2 %last.1 = bf16[144,384]{1,0:T(8,128)(2,1)} custom-call(f32[2,144,128]{2,1,0:T(8,128)S(1)} %get-tuple-element.40.keep.refs_3_, bf16[432,192]{1,0:T(8,128)(2,1)S(1)} %get-tuple-element.55.far, bf16[144,192]{1,0:T(8,128)(2,1)S(1)} %get-tuple-element.68.done, f32[2,144,192]{2,1,0:T(8,128)S(1)} %add.1.middle, ...), custom_call_target="tpu_custom_call" | custom-call | flops 2000000000 | bytes 1048576 | tf_op jit(solution)/shard_map/last/pallas_call | solution.py:472
  (2 shorter events, 0.0 us)
Async XLA Ops:
  0.0 5.0 %collective-permute-start = (bf16[2,4,1242]{2,1,0:T(4,128)(2,1)}, bf16[2,4,1242]{2,1,0:T(4,128)(2,1)S(1)}, u32[]{:S(2)}, u32[]{:S(2)}) collective-permute-start(bf16[2,4,1242]{2,1,0:T(4,128)(2,1)} %bitcast.14), channel_id=1, source_target_pairs={{0,8},{1,9},{2,10},{3,11},{4,12},{5,13},{6,14},{7,15},{8,0},{9,1},... | collective-permute-start | bytes 59624 | tf_op jit(solution)/shard_map/ppermute | solution.py:505
  5.0 3.8 %collective-permute-start.1 = (bf16[2,2,4,1242]{3,2,1,0:T(4,128)(2,1)S(1)}, bf16[2,2,4,1242]{3,2,1,0:T(4,128)(2,1)S(1)}, u32[]{:S(2)}, u32[]{:S(2)}) collective-permute-start(bf16[2,2,4,1242]{3,2,1,0:T(4,128)(2,1)S(1)} %halves.1.refs_0_), channel_id=1, source_target_pairs={{0,2},{1,3},{2,4},{3,5},{4,6},{5,7},{6,0},{7,1},{8,10},{9,11},{10,... | collective-permute-start | bytes 119240 | tf_op jit(solution)/shard_map/ppermute | solution.py:505
  5.2 4.4 %collective-permute-start.2 = (bf16[2,2,4,1242]{3,2,1,0:T(4,128)(2,1)S(1)}, bf16[2,2,4,1242]{3,2,1,0:T(4,128)(2,1)S(1)}, u32[]{:S(2)}, u32[]{:S(2)}) collective-permute-start(bf16[2,2,4,1242]{3,2,1,0:T(4,128)(2,1)S(1)} %halves.1.refs_0_), channel_id=1, source_target_pairs={{0,4},{1,5},{2,6},{3,7},{4,0},{5,1},{6,2},{7,3},{8,12},{9,13},{10,... | collective-permute-start | bytes 119240 | tf_op jit(solution)/shard_map/ppermute | solution.py:505
  7.3 4.1 %collective-permute-start.3 = (bf16[2,2,4,1242]{3,2,1,0:T(4,128)(2,1)S(1)}, bf16[2,2,4,1242]{3,2,1,0:T(4,128)(2,1)S(1)}, u32[]{:S(2)}, u32[]{:S(2)}) collective-permute-start(bf16[2,2,4,1242]{3,2,1,0:T(4,128)(2,1)S(1)} %halves.1.refs_0_), channel_id=1, source_target_pairs={{0,6},{1,7},{2,0},{3,1},{4,2},{5,3},{6,4},{7,5},{8,14},{9,15},{10,... | collective-permute-start | bytes 119240 | tf_op jit(solution)/shard_map/ppermute | solution.py:505
  11.4 4.5 %collective-permute-start.4 = (bf16[8,2,4,1242]{3,2,1,0:T(4,128)(2,1)S(1)}, bf16[8,2,4,1242]{3,2,1,0:T(4,128)(2,1)S(1)}, u32[]{:S(2)}, u32[]{:S(2)}) collective-permute-start(bf16[8,2,4,1242]{3,2,1,0:T(4,128)(2,1)S(1)} %mine.1.refs_0_), channel_id=1, source_target_pairs={{0,1},{1,0},{2,3},{3,2},{4,5},{5,4},{6,7},{7,6},{8,9},{9,8},{10,11... | collective-permute-start | bytes 476936 | tf_op jit(solution)/shard_map/ppermute | solution.py:505
  19.8 8.1 %collective-permute-start.5 = (bf16[224,128]{1,0:T(8,128)(2,1)S(1)}, bf16[224,128]{1,0:T(8,128)(2,1)S(1)}, u32[]{:S(2)}, u32[]{:S(2)}) collective-permute-start(bf16[224,128]{1,0:T(8,128)(2,1)S(1)} %get-tuple-element.61), channel_id=1, source_target_pairs={{0,15},{1,0},{2,1},{3,2},{4,3},{5,4},{6,5},{7,6},{8,7},{9,8},{10,9... | collective-permute-start | bytes 172040 | tf_op jit(solution)/shard_map/ppermute | solution.py:497
  20.1 7.8 %collective-permute-start.6 = (bf16[224,128]{1,0:T(8,128)(2,1)S(1)}, bf16[224,128]{1,0:T(8,128)(2,1)S(1)}, u32[]{:S(2)}, u32[]{:S(2)}) collective-permute-start(bf16[224,128]{1,0:T(8,128)(2,1)S(1)} %get-tuple-element.62), channel_id=1, source_target_pairs={{0,113},{1,114},{2,115},{3,116},{4,117},{5,118},{6,119},{7,120},{8... | collective-permute-start | bytes 172040 | tf_op jit(solution)/shard_map/ppermute | solution.py:497
  26.1 3.0 %collective-permute-start.7 = (bf16[224,128]{1,0:T(8,128)(2,1)S(1)}, bf16[224,128]{1,0:T(8,128)(2,1)S(1)}, u32[]{:S(2)}, u32[]{:S(2)}) collective-permute-start(bf16[224,128]{1,0:T(8,128)(2,1)S(1)} %get-tuple-element.63), channel_id=1, source_target_pairs={{0,112},{1,113},{2,114},{3,115},{4,116},{5,117},{6,118},{7,119},{8... | collective-permute-start | bytes 172040 | tf_op jit(solution)/shard_map/ppermute | solution.py:497
  29.2 7.4 %copy-start = (f32[768]{0:T(1024)S(1)}, f32[768]{0:T(1024)}, u32[]{:S(2)}) copy-start(f32[768]{0:T(1024)} %param.20) | copy-start | bytes 9220
  31.5 7.0 %collective-permute-start.8 = (bf16[224,128]{1,0:T(8,128)(2,1)S(1)}, bf16[224,128]{1,0:T(8,128)(2,1)S(1)}, u32[]{:S(2)}, u32[]{:S(2)}) collective-permute-start(bf16[224,128]{1,0:T(8,128)(2,1)S(1)} %get-tuple-element.69), channel_id=1, source_target_pairs={{0,1},{1,2},{2,3},{3,4},{4,5},{5,6},{6,7},{7,8},{8,9},{9,10},{10,1... | collective-permute-start | bytes 172040 | tf_op jit(solution)/shard_map/ppermute | solution.py:497
  34.0 9.0 %collective-permute-start.9 = (bf16[224,128]{1,0:T(8,128)(2,1)S(1)}, bf16[224,128]{1,0:T(8,128)(2,1)S(1)}, u32[]{:S(2)}, u32[]{:S(2)}) collective-permute-start(bf16[224,128]{1,0:T(8,128)(2,1)S(1)} %get-tuple-element.70), channel_id=1, source_target_pairs={{0,17},{1,18},{2,19},{3,20},{4,21},{5,22},{6,23},{7,24},{8,25},{9,... | collective-permute-start | bytes 172040 | tf_op jit(solution)/shard_map/ppermute | solution.py:497
  36.7 6.4 %collective-permute-start.10 = (bf16[224,128]{1,0:T(8,128)(2,1)S(1)}, bf16[224,128]{1,0:T(8,128)(2,1)S(1)}, u32[]{:S(2)}, u32[]{:S(2)}) collective-permute-start(bf16[224,128]{1,0:T(8,128)(2,1)S(1)} %get-tuple-element.71), channel_id=1, source_target_pairs={{0,16},{1,17},{2,18},{3,19},{4,20},{5,21},{6,22},{7,23},{8,24},{9,... | collective-permute-start | bytes 172040 | tf_op jit(solution)/shard_map/ppermute | solution.py:497

commit v3 on v2

--- a/solution.py
+++ b/solution.py
@@ -197,8 +197,8 @@
         top_tile, low_tile = t_top[first : first + 16], t_low[first : first + 16]
         rows = []
         for column in range(0, 12, 2):
-            top = window_lanes(top_tile, (11 - column) * ROWS)
-            low = window_lanes(low_tile, (10 - column) * ROWS)
+            top = window_lanes(top_tile, (11 - column) * ROWS).astype(F32)
+            low = window_lanes(low_tile, (10 - column) * ROWS).astype(F32)
             rows += [top[:8], top[8:] + low[:8], low[8:]]
         halves.append(jnp.concatenate(rows, axis=0))
     return jnp.concatenate(halves, axis=1)
@@ -367,8 +367,8 @@
             table_f32[at : at + 8, :HALF] = piece[:, n * HALF : (n + 1) * HALF]
     table_out[:, :HALF] = table_f32[:, :HALF].astype(BF16)
     tops, lows = picked_rows(table_out, rows[0])
-    t_top[...] = dot(tops, lanes[...])
-    t_low[...] = dot(lows, lanes[...])
+    t_top[...] = dot(tops, lanes[...]).astype(BF16)
+    t_low[...] = dot(lows, lanes[...]).astype(BF16)
     mask = first_mask[0:1]
     blended = [blend(scores[p], v[p], lambda h: expanded_bias(t_top, t_low, p, h) + mask) for p in range(WINDOWS)]
     write_attended(cells, 0, blended, query_choice, proj[...])
@@ -509,7 +509,7 @@
     shard = earth_bias[:, 0]
     cells = pltpu.VMEM((2, CELLS, GROUP), F32)
     cell_rows = shape(2, CELLS, GROUP, dtype=F32)
-    t_scratch = [pltpu.VMEM((768, KEYS), F32), pltpu.VMEM((768, KEYS), F32)]
+    t_scratch = [pltpu.VMEM((768, KEYS), BF16), pltpu.VMEM((768, KEYS), BF16)]
     packed = shape(224, 128)
 
     def in_hbm(array):

time: 45.5 us -> 45.1 us (level)
  transfers between devices with their start and end apart: 11 -> 11, of which waited for: 5 -> 5; matrix products, arithmetic and copies ran while one was open for 0% -> 0% of each run, Pallas kernels for 16% -> 17%
where the time goes in v3:
time: 45.1 us; the launch traced here: 44.9 us
  starting transfers between devices  21 us (47%)
  Pallas kernels  15.5 us (34%)
  waiting for transfers between devices  8.17 us (18%)
    pallas_call x12, Pallas kernels, call(): pl.pallas_call(kernel, name=name, out_shape=outs, in_specs=in_specs or [V...  15.5 us
    ppermute x6, starting transfers between devices, sent(): return lax.ppermute(block, ('lat', 'lon'), route)  11.7 us
    ppermute x5, starting transfers between devices, turned(): return lax.ppermute(block, 'lon', route)  9.27 us
    ppermute x6, waiting for transfers between devices, sent(): return lax.ppermute(block, ('lat', 'lon'), route)  5.43 us
    ppermute x5, waiting for transfers between devices, turned(): return lax.ppermute(block, 'lon', route)  2.74 us
  transfers between devices with their start and end apart: 11, of which 5 were waited for; matrix products, arithmetic and copies ran while one was open for 0% of the time, Pallas kernels for 17%

profile of v3, /device:TPU:7, one launch (start us, length us, event | category | flops | bytes accessed | tf_op | source)
XLA Modules:
  0.0 44.9 jit_solution(13084399717922613048)
XLA Ops:
  0.0 3.6 %collective-permute-start = (bf16[2,4,1242]{2,1,0:T(4,128)(2,1)}, bf16[2,4,1242]{2,1,0:T(4,128)(2,1)S(1)}, u32[]{:S(2)}, u32[]{:S(2)}) collective-permute-start(bf16[2,4,1242]{2,1,0:T(4,128)(2,1)} %bitcast.14), channel_id=1, source_target_pairs={{0,8},{1,9},{2,10},{3,11},{4,12},{5,13},{6,14},{7,15},{8,0},{9,1},... | collective-permute-start | bytes 59624 | tf_op jit(solution)/shard_map/ppermute | solution.py:505
  3.6 1.2 %fetch.1 = (bf16[1,2,4,1242]{3,2,1,0:T(4,128)(2,1)S(1)}, bf16[576,192]{1,0:T(8,128)(2,1)S(1)}, f32[2,2,192]{2,1,0:T(2,128)S(1)}, bf16[192,576]{1,0:T(8,128)(2,1)...) custom-call(s32[48]{0:T(128)} %refs_0_.2, ...), custom_call_target="tpu_custom_call" | custom-call | flops 1400000000 | bytes 1048576 | tf_op jit(solution)/shard_map/fetch/pallas_call | solution.py:472
  4.8 0.2 collective-permute-done
  5.0 0.2 collective-permute-start.1
  5.2 2.1 %collective-permute-start.2 = (bf16[2,2,4,1242]{3,2,1,0:T(4,128)(2,1)S(1)}, bf16[2,2,4,1242]{3,2,1,0:T(4,128)(2,1)S(1)}, u32[]{:S(2)}, u32[]{:S(2)}) collective-permute-start(bf16[2,2,4,1242]{3,2,1,0:T(4,128)(2,1)S(1)} %halves.1.refs_0_), channel_id=1, source_target_pairs={{0,4},{1,5},{2,6},{3,7},{4,0},{5,1},{6,2},{7,3},{8,12},{9,13},{10,... | collective-permute-start | bytes 119240 | tf_op jit(solution)/shard_map/ppermute | solution.py:505
  7.3 0.0 collective-permute-start.3
  7.3 1.5 %before.1 = (f32[4,864,256]{2,1,0:T(8,128)S(1)}, bf16[4,256,256]{2,1,0:T(8,128)(2,1)S(1)}, f32[2,576,128]{2,1,0:T(8,128)S(1)}, bf16[192,576]{1,0:T(8,128)(2,1)S(1)}, bf16[192,192]{1,0:T(8,128)(2,1)S(1)}) custom-call(bf16[2,2,4,1242]{3,2,1,0:T(4,128)(2,1)S(1)} %halves.1.refs_0_, bf16[576,192]{1,0:T(8,128)(2,1)S(1)} %get-tuple-element.42.refs_1_, ...), custom_call_target="tpu_custom_call" | custom-call | flops 2500000000 | bytes 1048576 | tf_op jit(solution)/shard_map/before/pallas_call | solution.py:472
  8.8 0.0 collective-permute-done.1.refs_1_
  8.8 0.7 %collective-permute-done.2.refs_2_ = bf16[2,2,4,1242]{3,2,1,0:T(4,128)(2,1)S(1)} collective-permute-done((bf16[2,2,4,1242]{3,2,1,0:T(4,128)(2,1)S(1)}, bf16[2,2,4,1242]{3,2,1,0:T(4,128)(2,1)S(1)}, u32[]{:S(2)}, u32[]{:S(2)}) %collective-permute-start.2) | collective-permute-done | bytes 39776 | tf_op jit(solution)/shard_map/ppermute | solution.py:505
  9.5 1.8 %collective-permute-done.3.refs_3_ = bf16[2,2,4,1242]{3,2,1,0:T(4,128)(2,1)S(1)} collective-permute-done((bf16[2,2,4,1242]{3,2,1,0:T(4,128)(2,1)S(1)}, bf16[2,2,4,1242]{3,2,1,0:T(4,128)(2,1)S(1)}, u32[]{:S(2)}, u32[]{:S(2)}) %collective-permute-start.3) | collective-permute-done | bytes 39776 | tf_op jit(solution)/shard_map/ppermute | solution.py:505
  11.4 3.3 %collective-permute-start.4 = (bf16[8,2,4,1242]{3,2,1,0:T(4,128)(2,1)S(1)}, bf16[8,2,4,1242]{3,2,1,0:T(4,128)(2,1)S(1)}, u32[]{:S(2)}, u32[]{:S(2)}) collective-permute-start(bf16[8,2,4,1242]{3,2,1,0:T(4,128)(2,1)S(1)} %mine.1.refs_0_), channel_id=1, source_target_pairs={{0,1},{1,0},{2,3},{3,2},{4,5},{5,4},{6,7},{7,6},{8,9},{9,8},{10,11... | collective-permute-start | bytes 476936 | tf_op jit(solution)/shard_map/ppermute | solution.py:505
  14.7 1.1 %prepare.1 = (bf16[192,192]{1,0:T(8,128)(2,1)S(1)}, bf16[192,768]{1,0:T(8,128)(2,1)S(1)}, bf16[192,768]{1,0:T(8,128)(2,1)S(1)}, bf16[138,256]{1,0:T(8,128)(2,1)S...) custom-call(bf16[8,2,4,1242]{3,2,1,0:T(4,128)(2,1)S(1)} %mine.1.refs_0_, ...), custom_call_target="tpu_custom_call" | custom-call | flops 1200000000 | bytes 1048576 | tf_op jit(solution)/shard_map/prepare/pallas_call | solution.py:472
  15.9 0.0 collective-permute-done.4.theirs
  15.9 3.5 %first.1 = (bf16[224,128]{1,0:T(8,128)(2,1)S(1)}, bf16[224,128]{1,0:T(8,128)(2,1)S(1)}, bf16[224,128]{1,0:T(8,128)(2,1)S(1)}, bf16[1152,256]{1,0:T(8,128)(2,1)S(...) custom-call(bf16[8,2,4,1242]{3,2,1,0:T(4,128)(2,1)S(1)} %mine.1.refs_0_, ...), custom_call_target="tpu_custom_call" | custom-call | flops 4499999744 | bytes 1048576 | tf_op jit(solution)/shard_map/first/pallas_call | solution.py:472
  19.4 0.3 collective-permute-start.5
  19.7 6.1 %collective-permute-start.6 = (bf16[224,128]{1,0:T(8,128)(2,1)S(1)}, bf16[224,128]{1,0:T(8,128)(2,1)S(1)}, u32[]{:S(2)}, u32[]{:S(2)}) collective-permute-start(bf16[224,128]{1,0:T(8,128)(2,1)S(1)} %get-tuple-element.62), channel_id=1, source_target_pairs={{0,113},{1,114},{2,115},{3,116},{4,117},{5,118},{6,119},{7,120},{8... | collective-permute-start | bytes 172040 | tf_op jit(solution)/shard_map/ppermute | solution.py:497
  25.8 0.3 collective-permute-start.7
  26.1 1.4 %bias.1 = (bf16[4,864,256]{2,1,0:T(8,128)(2,1)S(1)}, bf16[144,192]{1,0:T(8,128)(2,1)S(1)}) custom-call(bf16[1152,256]{1,0:T(8,128)(2,1)S(1)} %get-tuple-element.56.table, f32[2,144,256]{2,1,0:T(8,128)S(1)} %get-tuple-element.57.second_mask, bf16[2,138,768]{2,1,0:T(8,128)(2,1)S(1)} %get-tuple-element.58.columns, ...), custom_call_target="tpu_custom_call" | custom-call | flops 200000000 | bytes 1048576 | tf_op jit(solution)/shard_map/bias/pallas_call | solution.py:472
  27.5 0.0 collective-permute-done.5.from_lon
  27.5 0.0 collective-permute-done.6.from_both
  27.5 0.3 ready.1.given
  27.8 1.0 %collective-permute-done.7.from_lat = bf16[224,128]{1,0:T(8,128)(2,1)S(1)} collective-permute-done((bf16[224,128]{1,0:T(8,128)(2,1)S(1)}, bf16[224,128]{1,0:T(8,128)(2,1)S(1)}, u32[]{:S(2)}, u32[]{:S(2)}) %collective-permute-start.7) | collective-permute-done | bytes 57376 | tf_op jit(solution)/shard_map/ppermute | solution.py:497
  28.8 0.0 copy-start
  28.8 2.4 %second.1 = (bf16[144,192]{1,0:T(8,128)(2,1)S(1)}, bf16[224,128]{1,0:T(8,128)(2,1)S(1)}, bf16[224,128]{1,0:T(8,128)(2,1)S(1)}, bf16[224,128]{1,0:T(8,128)(2,1)S(1)}) custom-call(f32[2,576,128]{2,1,0:T(8,128)S(1)} %ready.1.given, bf16[224,128]{1,0:T(8,128)(2,1)S(1)} %collective-permute-done.7.from_lat, bf16[4,864,256]{2,1,0:T(8,128)(2,1)S(1)} %get-tuple-element.64.bias, ...), custom_call_target="tpu_custom_call" | custom-call | flops 4499999744 | bytes 1048576 | tf_op jit(solution)/shard_map/second/pallas_call | solution.py:472
  31.1 2.4 %collective-permute-start.8 = (bf16[224,128]{1,0:T(8,128)(2,1)S(1)}, bf16[224,128]{1,0:T(8,128)(2,1)S(1)}, u32[]{:S(2)}, u32[]{:S(2)}) collective-permute-start(bf16[224,128]{1,0:T(8,128)(2,1)S(1)} %get-tuple-element.69), channel_id=1, source_target_pairs={{0,1},{1,2},{2,3},{3,4},{4,5},{5,6},{6,7},{7,8},{8,9},{9,10},{10,1... | collective-permute-start | bytes 172040 | tf_op jit(solution)/shard_map/ppermute | solution.py:497
  33.6 2.6 %collective-permute-start.9 = (bf16[224,128]{1,0:T(8,128)(2,1)S(1)}, bf16[224,128]{1,0:T(8,128)(2,1)S(1)}, u32[]{:S(2)}, u32[]{:S(2)}) collective-permute-start(bf16[224,128]{1,0:T(8,128)(2,1)S(1)} %get-tuple-element.70), channel_id=1, source_target_pairs={{0,17},{1,18},{2,19},{3,20},{4,21},{5,22},{6,23},{7,24},{8,25},{9,... | collective-permute-start | bytes 172040 | tf_op jit(solution)/shard_map/ppermute | solution.py:497
  36.2 0.0 copy-done
  36.2 0.1 reshape.10.merge_gain
  36.3 0.0 collective-permute-start.10
  36.3 1.8 %own.1 = (bf16[144,192]{1,0:T(8,128)(2,1)S(1)}, bf16[192,768]{1,0:T(8,128)(2,1)S(1)}, bf16[192,768]{1,0:T(8,128)(2,1)S(1)}, bf16[768,384]{1,0:T(8,128)(2,1)S(1)}) custom-call(bf16[2,192,768]{2,1,0:T(8,128)(2,1)} %refs_0_.3, bf16[2,192,768]{2,1,0:T(8,128)(2,1)} %bitcast.12, bf16[768,384]{1,0:T(8,128)(2,1)} %refs_2_.3, ...), custom_call_target="tpu_custom_call" | custom-call | flops 500000000 | bytes 1048576 | tf_op jit(solution)/shard_map/own/pallas_call | solution.py:472
  38.1 0.0 collective-permute-done.8.from_lon
  38.1 4.5 %collective-permute-done.9.from_both = bf16[224,128]{1,0:T(8,128)(2,1)S(1)} collective-permute-done((bf16[224,128]{1,0:T(8,128)(2,1)S(1)}, bf16[224,128]{1,0:T(8,128)(2,1)S(1)}, u32[]{:S(2)}, u32[]{:S(2)}) %collective-permute-start.9) | collective-permute-done | bytes 57376 | tf_op jit(solution)/shard_map/ppermute | solution.py:497
  42.6 0.1 add.1.middle
  42.7 0.0 collective-permute-done.10.from_lat
  42.7 2.2 %last.1 = bf16[144,384]{1,0:T(8,128)(2,1)} custom-call(f32[2,144,128]{2,1,0:T(8,128)S(1)} %get-tuple-element.40.keep.refs_3_, bf16[432,192]{1,0:T(8,128)(2,1)S(1)} %get-tuple-element.55.far, bf16[144,192]{1,0:T(8,128)(2,1)S(1)} %get-tuple-element.68.done, f32[2,144,192]{2,1,0:T(8,128)S(1)} %add.1.middle, ...), custom_call_target="tpu_custom_call" | custom-call | flops 2000000000 | bytes 1048576 | tf_op jit(solution)/shard_map/last/pallas_call | solution.py:472
  (2 shorter events, 0.0 us)
Async XLA Ops:
  0.0 5.0 %collective-permute-start = (bf16[2,4,1242]{2,1,0:T(4,128)(2,1)}, bf16[2,4,1242]{2,1,0:T(4,128)(2,1)S(1)}, u32[]{:S(2)}, u32[]{:S(2)}) collective-permute-start(bf16[2,4,1242]{2,1,0:T(4,128)(2,1)} %bitcast.14), channel_id=1, source_target_pairs={{0,8},{1,9},{2,10},{3,11},{4,12},{5,13},{6,14},{7,15},{8,0},{9,1},... | collective-permute-start | bytes 59624 | tf_op jit(solution)/shard_map/ppermute | solution.py:505
  5.0 3.8 %collective-permute-start.1 = (bf16[2,2,4,1242]{3,2,1,0:T(4,128)(2,1)S(1)}, bf16[2,2,4,1242]{3,2,1,0:T(4,128)(2,1)S(1)}, u32[]{:S(2)}, u32[]{:S(2)}) collective-permute-start(bf16[2,2,4,1242]{3,2,1,0:T(4,128)(2,1)S(1)} %halves.1.refs_0_), channel_id=1, source_target_pairs={{0,2},{1,3},{2,4},{3,5},{4,6},{5,7},{6,0},{7,1},{8,10},{9,11},{10,... | collective-permute-start | bytes 119240 | tf_op jit(solution)/shard_map/ppermute | solution.py:505
  5.2 4.4 %collective-permute-start.2 = (bf16[2,2,4,1242]{3,2,1,0:T(4,128)(2,1)S(1)}, bf16[2,2,4,1242]{3,2,1,0:T(4,128)(2,1)S(1)}, u32[]{:S(2)}, u32[]{:S(2)}) collective-permute-start(bf16[2,2,4,1242]{3,2,1,0:T(4,128)(2,1)S(1)} %halves.1.refs_0_), channel_id=1, source_target_pairs={{0,4},{1,5},{2,6},{3,7},{4,0},{5,1},{6,2},{7,3},{8,12},{9,13},{10,... | collective-permute-start | bytes 119240 | tf_op jit(solution)/shard_map/ppermute | solution.py:505
  7.3 4.1 %collective-permute-start.3 = (bf16[2,2,4,1242]{3,2,1,0:T(4,128)(2,1)S(1)}, bf16[2,2,4,1242]{3,2,1,0:T(4,128)(2,1)S(1)}, u32[]{:S(2)}, u32[]{:S(2)}) collective-permute-start(bf16[2,2,4,1242]{3,2,1,0:T(4,128)(2,1)S(1)} %halves.1.refs_0_), channel_id=1, source_target_pairs={{0,6},{1,7},{2,0},{3,1},{4,2},{5,3},{6,4},{7,5},{8,14},{9,15},{10,... | collective-permute-start | bytes 119240 | tf_op jit(solution)/shard_map/ppermute | solution.py:505
  11.4 4.5 %collective-permute-start.4 = (bf16[8,2,4,1242]{3,2,1,0:T(4,128)(2,1)S(1)}, bf16[8,2,4,1242]{3,2,1,0:T(4,128)(2,1)S(1)}, u32[]{:S(2)}, u32[]{:S(2)}) collective-permute-start(bf16[8,2,4,1242]{3,2,1,0:T(4,128)(2,1)S(1)} %mine.1.refs_0_), channel_id=1, source_target_pairs={{0,1},{1,0},{2,3},{3,2},{4,5},{5,4},{6,7},{7,6},{8,9},{9,8},{10,11... | collective-permute-start | bytes 476936 | tf_op jit(solution)/shard_map/ppermute | solution.py:505
  19.4 8.1 %collective-permute-start.5 = (bf16[224,128]{1,0:T(8,128)(2,1)S(1)}, bf16[224,128]{1,0:T(8,128)(2,1)S(1)}, u32[]{:S(2)}, u32[]{:S(2)}) collective-permute-start(bf16[224,128]{1,0:T(8,128)(2,1)S(1)} %get-tuple-element.61), channel_id=1, source_target_pairs={{0,15},{1,0},{2,1},{3,2},{4,3},{5,4},{6,5},{7,6},{8,7},{9,8},{10,9... | collective-permute-start | bytes 172040 | tf_op jit(solution)/shard_map/ppermute | solution.py:497
  19.7 7.8 %collective-permute-start.6 = (bf16[224,128]{1,0:T(8,128)(2,1)S(1)}, bf16[224,128]{1,0:T(8,128)(2,1)S(1)}, u32[]{:S(2)}, u32[]{:S(2)}) collective-permute-start(bf16[224,128]{1,0:T(8,128)(2,1)S(1)} %get-tuple-element.62), channel_id=1, source_target_pairs={{0,113},{1,114},{2,115},{3,116},{4,117},{5,118},{6,119},{7,120},{8... | collective-permute-start | bytes 172040 | tf_op jit(solution)/shard_map/ppermute | solution.py:497
  25.8 3.0 %collective-permute-start.7 = (bf16[224,128]{1,0:T(8,128)(2,1)S(1)}, bf16[224,128]{1,0:T(8,128)(2,1)S(1)}, u32[]{:S(2)}, u32[]{:S(2)}) collective-permute-start(bf16[224,128]{1,0:T(8,128)(2,1)S(1)} %get-tuple-element.63), channel_id=1, source_target_pairs={{0,112},{1,113},{2,114},{3,115},{4,116},{5,117},{6,118},{7,119},{8... | collective-permute-start | bytes 172040 | tf_op jit(solution)/shard_map/ppermute | solution.py:497
  28.8 7.4 %copy-start = (f32[768]{0:T(1024)S(1)}, f32[768]{0:T(1024)}, u32[]{:S(2)}) copy-start(f32[768]{0:T(1024)} %param.20) | copy-start | bytes 9220
  31.1 7.0 %collective-permute-start.8 = (bf16[224,128]{1,0:T(8,128)(2,1)S(1)}, bf16[224,128]{1,0:T(8,128)(2,1)S(1)}, u32[]{:S(2)}, u32[]{:S(2)}) collective-permute-start(bf16[224,128]{1,0:T(8,128)(2,1)S(1)} %get-tuple-element.69), channel_id=1, source_target_pairs={{0,1},{1,2},{2,3},{3,4},{4,5},{5,6},{6,7},{7,8},{8,9},{9,10},{10,1... | collective-permute-start | bytes 172040 | tf_op jit(solution)/shard_map/ppermute | solution.py:497
  33.6 9.0 %collective-permute-start.9 = (bf16[224,128]{1,0:T(8,128)(2,1)S(1)}, bf16[224,128]{1,0:T(8,128)(2,1)S(1)}, u32[]{:S(2)}, u32[]{:S(2)}) collective-permute-start(bf16[224,128]{1,0:T(8,128)(2,1)S(1)} %get-tuple-element.70), channel_id=1, source_target_pairs={{0,17},{1,18},{2,19},{3,20},{4,21},{5,22},{6,23},{7,24},{8,25},{9,... | collective-permute-start | bytes 172040 | tf_op jit(solution)/shard_map/ppermute | solution.py:497
  36.3 6.4 %collective-permute-start.10 = (bf16[224,128]{1,0:T(8,128)(2,1)S(1)}, bf16[224,128]{1,0:T(8,128)(2,1)S(1)}, u32[]{:S(2)}, u32[]{:S(2)}) collective-permute-start(bf16[224,128]{1,0:T(8,128)(2,1)S(1)} %get-tuple-element.71), channel_id=1, source_target_pairs={{0,16},{1,17},{2,18},{3,19},{4,20},{5,21},{6,22},{7,23},{8,24},{9,... | collective-permute-start | bytes 172040 | tf_op jit(solution)/shard_map/ppermute | solution.py:497

commit v4 on v3

--- a/solution.py
+++ b/solution.py
@@ -358,13 +358,15 @@
 
 def first_kernel(mine, theirs, scores, v, first_mask, keep, inputs, gains, query_choice, proj, fc1, fc2, lanes, rows, sent_lat, sent_lon, sent_both, table_out, out, cells, table_f32, t_top, t_low):
     me = lax.axis_index("lon")
-    for g in range(LONS):
-        slot = lax.rem(me // 2 - g // 2 + 8, 4) * 2 + jnp.where(me // 8 == g // 8, 0, 1)
-        shard = jnp.where(lax.rem(me, 2) == g % 2, mine[slot], theirs[slot]).astype(F32)
-        piece = jnp.concatenate([shard[0], shard[1]], axis=0)
-        for n in range(9):
-            at = (g * 9 + n) * 8
-            table_f32[at : at + 8, :HALF] = piece[:, n * HALF : (n + 1) * HALF]
+    for core, shards_of in ((lax.rem(me, 2), mine), (1 - lax.rem(me, 2), theirs)):
+        for slot in range(LONS // 2):
+            z = jnp.where(me >= 8, 1, 0) if slot % 2 == 0 else jnp.where(me >= 8, 0, 1)
+            g = z * 8 + lax.rem(me // 2 - slot // 2 + 8, 4) * 2 + core
+            shard = shards_of[slot].astype(F32)
+            piece = jnp.concatenate([shard[0], shard[1]], axis=0)
+            for n in range(9):
+                rows_at = pl.ds(pl.multiple_of(g * 72 + n * 8, 8), 8)
+                table_f32[rows_at, :HALF] = piece[:, n * HALF : (n + 1) * HALF]
     table_out[:, :HALF] = table_f32[:, :HALF].astype(BF16)
     tops, lows = picked_rows(table_out, rows[0])
     t_top[...] = dot(tops, lanes[...]).astype(BF16)
@@ -548,7 +550,7 @@
         in_specs=[hbm_spec] * (len(early) + 1),
     )
     halves = call(join_kernel, "halves", 0.2, shape(2, 2, WINDOWS, SHARD), [], held_shard, other_half[None])
-    ring = [turned(halves, lambda z, x, core: (z, (x + hop) % 4, core)) for hop in range(1, 4)]
+    ring = {hop: turned(halves, lambda z, x, core: (z, (x + hop) % 4, core)) for hop in (2, 1, 3)}
     scores, v, inputs, qkv1, proj1 = call(
         functools.partial(sliced, before_kernel, {5: 1, 6: 1}),
         "before",
@@ -560,7 +562,7 @@
         *[in_hbm(array) for array in late],
         in_specs=[VMEM_SPEC] * 5 + [hbm_spec] * len(late),
     )
-    mine = call(join_kernel, "mine", 0.3, shape(8, 2, WINDOWS, SHARD), [], halves, *ring, v)
+    mine = call(join_kernel, "mine", 0.3, shape(8, 2, WINDOWS, SHARD), [], halves, ring[1], ring[2], ring[3], v)
     theirs = turned(mine, lambda z, x, core: (z, x, 1 - core))
     proj0, fc1_0, fc2_0, lanes, rows, columns = call(
         functools.partial(sliced, prepare_kernel, {1: 0, 2: 0, 3: 0}),

time: 45.1 us -> 45.2 us (level)
  transfers between devices with their start and end apart: 11 -> 11, of which waited for: 5 -> 5; matrix products, arithmetic and copies ran while one was open for 0% -> 0% of each run, Pallas kernels for 17% -> 16%
where the time goes in v4:
time: 45.2 us; the launch traced here: 45 us
  starting transfers between devices  21 us (46%)
  Pallas kernels  15.6 us (35%)
  waiting for transfers between devices  8.16 us (18%)
    pallas_call x12, Pallas kernels, call(): pl.pallas_call(kernel, name=name, out_shape=outs, in_specs=in_specs or [V...  15.6 us
    ppermute x6, starting transfers between devices, sent(): return lax.ppermute(block, ('lat', 'lon'), route)  11.8 us
    ppermute x5, starting transfers between devices, turned(): return lax.ppermute(block, 'lon', route)  9.27 us
    ppermute x6, waiting for transfers between devices, sent(): return lax.ppermute(block, ('lat', 'lon'), route)  5.42 us
    ppermute x5, waiting for transfers between devices, turned(): return lax.ppermute(block, 'lon', route)  2.74 us
  transfers between devices with their start and end apart: 11, of which 5 were waited for; matrix products, arithmetic and copies ran while one was open for 0% of the time, Pallas kernels for 16%

profile of v4, /device:TPU:7, one launch (start us, length us, event | category | flops | bytes accessed | tf_op | source)
XLA Modules:
  0.0 45.0 jit_solution(9569913643119768994)
XLA Ops:
  0.0 3.6 %collective-permute-start = (bf16[2,4,1242]{2,1,0:T(4,128)(2,1)}, bf16[2,4,1242]{2,1,0:T(4,128)(2,1)S(1)}, u32[]{:S(2)}, u32[]{:S(2)}) collective-permute-start(bf16[2,4,1242]{2,1,0:T(4,128)(2,1)} %bitcast.14), channel_id=1, source_target_pairs={{0,8},{1,9},{2,10},{3,11},{4,12},{5,13},{6,14},{7,15},{8,0},{9,1},... | collective-permute-start | bytes 59624 | tf_op jit(solution)/shard_map/ppermute | solution.py:507
  3.6 1.2 %fetch.1 = (bf16[1,2,4,1242]{3,2,1,0:T(4,128)(2,1)S(1)}, bf16[576,192]{1,0:T(8,128)(2,1)S(1)}, f32[2,2,192]{2,1,0:T(2,128)S(1)}, bf16[192,576]{1,0:T(8,128)(2,1)...) custom-call(s32[48]{0:T(128)} %refs_0_.2, ...), custom_call_target="tpu_custom_call" | custom-call | flops 1400000000 | bytes 1048576 | tf_op jit(solution)/shard_map/fetch/pallas_call | solution.py:474
  4.8 0.2 collective-permute-done
  5.0 0.2 collective-permute-start.1
  5.2 2.1 %collective-permute-start.2 = (bf16[2,2,4,1242]{3,2,1,0:T(4,128)(2,1)S(1)}, bf16[2,2,4,1242]{3,2,1,0:T(4,128)(2,1)S(1)}, u32[]{:S(2)}, u32[]{:S(2)}) collective-permute-start(bf16[2,2,4,1242]{3,2,1,0:T(4,128)(2,1)S(1)} %halves.1.refs_0_), channel_id=1, source_target_pairs={{0,4},{1,5},{2,6},{3,7},{4,0},{5,1},{6,2},{7,3},{8,12},{9,13},{10,... | collective-permute-start | bytes 119240 | tf_op jit(solution)/shard_map/ppermute | solution.py:507
  7.3 0.0 collective-permute-start.3
  7.3 1.5 %before.1 = (f32[4,864,256]{2,1,0:T(8,128)S(1)}, bf16[4,256,256]{2,1,0:T(8,128)(2,1)S(1)}, f32[2,576,128]{2,1,0:T(8,128)S(1)}, bf16[192,576]{1,0:T(8,128)(2,1)S(1)}, bf16[192,192]{1,0:T(8,128)(2,1)S(1)}) custom-call(bf16[2,2,4,1242]{3,2,1,0:T(4,128)(2,1)S(1)} %halves.1.refs_0_, bf16[576,192]{1,0:T(8,128)(2,1)S(1)} %get-tuple-element.42.refs_1_, ...), custom_call_target="tpu_custom_call" | custom-call | flops 2500000000 | bytes 1048576 | tf_op jit(solution)/shard_map/before/pallas_call | solution.py:474
  8.8 0.0 collective-permute-done.1.refs_1_
  8.8 0.7 %collective-permute-done.2.refs_2_ = bf16[2,2,4,1242]{3,2,1,0:T(4,128)(2,1)S(1)} collective-permute-done((bf16[2,2,4,1242]{3,2,1,0:T(4,128)(2,1)S(1)}, bf16[2,2,4,1242]{3,2,1,0:T(4,128)(2,1)S(1)}, u32[]{:S(2)}, u32[]{:S(2)}) %collective-permute-start.2) | collective-permute-done | bytes 39776 | tf_op jit(solution)/shard_map/ppermute | solution.py:507
  9.5 1.8 %collective-permute-done.3.refs_3_ = bf16[2,2,4,1242]{3,2,1,0:T(4,128)(2,1)S(1)} collective-permute-done((bf16[2,2,4,1242]{3,2,1,0:T(4,128)(2,1)S(1)}, bf16[2,2,4,1242]{3,2,1,0:T(4,128)(2,1)S(1)}, u32[]{:S(2)}, u32[]{:S(2)}) %collective-permute-start.3) | collective-permute-done | bytes 39776 | tf_op jit(solution)/shard_map/ppermute | solution.py:507
  11.4 3.3 %collective-permute-start.4 = (bf16[8,2,4,1242]{3,2,1,0:T(4,128)(2,1)S(1)}, bf16[8,2,4,1242]{3,2,1,0:T(4,128)(2,1)S(1)}, u32[]{:S(2)}, u32[]{:S(2)}) collective-permute-start(bf16[8,2,4,1242]{3,2,1,0:T(4,128)(2,1)S(1)} %mine.1.refs_0_), channel_id=1, source_target_pairs={{0,1},{1,0},{2,3},{3,2},{4,5},{5,4},{6,7},{7,6},{8,9},{9,8},{10,11... | collective-permute-start | bytes 476936 | tf_op jit(solution)/shard_map/ppermute | solution.py:507
  14.7 1.1 %prepare.1 = (bf16[192,192]{1,0:T(8,128)(2,1)S(1)}, bf16[192,768]{1,0:T(8,128)(2,1)S(1)}, bf16[192,768]{1,0:T(8,128)(2,1)S(1)}, bf16[138,256]{1,0:T(8,128)(2,1)S...) custom-call(bf16[8,2,4,1242]{3,2,1,0:T(4,128)(2,1)S(1)} %mine.1.refs_0_, ...), custom_call_target="tpu_custom_call" | custom-call | flops 1200000000 | bytes 1048576 | tf_op jit(solution)/shard_map/prepare/pallas_call | solution.py:474
  15.9 0.0 collective-permute-done.4.theirs
  15.9 3.6 %first.1 = (bf16[224,128]{1,0:T(8,128)(2,1)S(1)}, bf16[224,128]{1,0:T(8,128)(2,1)S(1)}, bf16[224,128]{1,0:T(8,128)(2,1)S(1)}, bf16[1152,256]{1,0:T(8,128)(2,1)S(...) custom-call(bf16[8,2,4,1242]{3,2,1,0:T(4,128)(2,1)S(1)} %mine.1.refs_0_, ...), custom_call_target="tpu_custom_call" | custom-call | flops 4499999744 | bytes 1048576 | tf_op jit(solution)/shard_map/first/pallas_call | solution.py:474
  19.5 0.3 collective-permute-start.5
  19.8 6.0 %collective-permute-start.6 = (bf16[224,128]{1,0:T(8,128)(2,1)S(1)}, bf16[224,128]{1,0:T(8,128)(2,1)S(1)}, u32[]{:S(2)}, u32[]{:S(2)}) collective-permute-start(bf16[224,128]{1,0:T(8,128)(2,1)S(1)} %get-tuple-element.62), channel_id=1, source_target_pairs={{0,113},{1,114},{2,115},{3,116},{4,117},{5,118},{6,119},{7,120},{8... | collective-permute-start | bytes 172040 | tf_op jit(solution)/shard_map/ppermute | solution.py:499
  25.9 0.4 collective-permute-start.7
  26.2 1.4 %bias.1 = (bf16[4,864,256]{2,1,0:T(8,128)(2,1)S(1)}, bf16[144,192]{1,0:T(8,128)(2,1)S(1)}) custom-call(bf16[1152,256]{1,0:T(8,128)(2,1)S(1)} %get-tuple-element.56.table, f32[2,144,256]{2,1,0:T(8,128)S(1)} %get-tuple-element.57.second_mask, bf16[2,138,768]{2,1,0:T(8,128)(2,1)S(1)} %get-tuple-element.58.columns, ...), custom_call_target="tpu_custom_call" | custom-call | flops 200000000 | bytes 1048576 | tf_op jit(solution)/shard_map/bias/pallas_call | solution.py:474
  27.6 0.0 collective-permute-done.5.from_lon
  27.6 0.0 collective-permute-done.6.from_both
  27.6 0.3 ready.1.given
  28.0 0.9 %collective-permute-done.7.from_lat = bf16[224,128]{1,0:T(8,128)(2,1)S(1)} collective-permute-done((bf16[224,128]{1,0:T(8,128)(2,1)S(1)}, bf16[224,128]{1,0:T(8,128)(2,1)S(1)}, u32[]{:S(2)}, u32[]{:S(2)}) %collective-permute-start.7) | collective-permute-done | bytes 57376 | tf_op jit(solution)/shard_map/ppermute | solution.py:499
  28.9 0.0 copy-start
  28.9 2.4 %second.1 = (bf16[144,192]{1,0:T(8,128)(2,1)S(1)}, bf16[224,128]{1,0:T(8,128)(2,1)S(1)}, bf16[224,128]{1,0:T(8,128)(2,1)S(1)}, bf16[224,128]{1,0:T(8,128)(2,1)S(1)}) custom-call(f32[2,576,128]{2,1,0:T(8,128)S(1)} %ready.1.given, bf16[224,128]{1,0:T(8,128)(2,1)S(1)} %collective-permute-done.7.from_lat, bf16[4,864,256]{2,1,0:T(8,128)(2,1)S(1)} %get-tuple-element.64.bias, ...), custom_call_target="tpu_custom_call" | custom-call | flops 4499999744 | bytes 1048576 | tf_op jit(solution)/shard_map/second/pallas_call | solution.py:474
  31.3 2.4 %collective-permute-start.8 = (bf16[224,128]{1,0:T(8,128)(2,1)S(1)}, bf16[224,128]{1,0:T(8,128)(2,1)S(1)}, u32[]{:S(2)}, u32[]{:S(2)}) collective-permute-start(bf16[224,128]{1,0:T(8,128)(2,1)S(1)} %get-tuple-element.69), channel_id=1, source_target_pairs={{0,1},{1,2},{2,3},{3,4},{4,5},{5,6},{6,7},{7,8},{8,9},{9,10},{10,1... | collective-permute-start | bytes 172040 | tf_op jit(solution)/shard_map/ppermute | solution.py:499
  33.7 2.6 %collective-permute-start.9 = (bf16[224,128]{1,0:T(8,128)(2,1)S(1)}, bf16[224,128]{1,0:T(8,128)(2,1)S(1)}, u32[]{:S(2)}, u32[]{:S(2)}) collective-permute-start(bf16[224,128]{1,0:T(8,128)(2,1)S(1)} %get-tuple-element.70), channel_id=1, source_target_pairs={{0,17},{1,18},{2,19},{3,20},{4,21},{5,22},{6,23},{7,24},{8,25},{9,... | collective-permute-start | bytes 172040 | tf_op jit(solution)/shard_map/ppermute | solution.py:499
  36.3 0.0 copy-done
  36.3 0.1 reshape.10.merge_gain
  36.4 0.0 collective-permute-start.10
  36.4 1.8 %own.1 = (bf16[144,192]{1,0:T(8,128)(2,1)S(1)}, bf16[192,768]{1,0:T(8,128)(2,1)S(1)}, bf16[192,768]{1,0:T(8,128)(2,1)S(1)}, bf16[768,384]{1,0:T(8,128)(2,1)S(1)}) custom-call(bf16[2,192,768]{2,1,0:T(8,128)(2,1)} %refs_0_.3, bf16[2,192,768]{2,1,0:T(8,128)(2,1)} %bitcast.12, bf16[768,384]{1,0:T(8,128)(2,1)} %refs_2_.3, ...), custom_call_target="tpu_custom_call" | custom-call | flops 500000000 | bytes 1048576 | tf_op jit(solution)/shard_map/own/pallas_call | solution.py:474
  38.2 0.0 collective-permute-done.8.from_lon
  38.2 4.5 %collective-permute-done.9.from_both = bf16[224,128]{1,0:T(8,128)(2,1)S(1)} collective-permute-done((bf16[224,128]{1,0:T(8,128)(2,1)S(1)}, bf16[224,128]{1,0:T(8,128)(2,1)S(1)}, u32[]{:S(2)}, u32[]{:S(2)}) %collective-permute-start.9) | collective-permute-done | bytes 57376 | tf_op jit(solution)/shard_map/ppermute | solution.py:499
  42.7 0.1 add.1.middle
  42.8 0.0 collective-permute-done.10.from_lat
  42.8 2.2 %last.1 = bf16[144,384]{1,0:T(8,128)(2,1)} custom-call(f32[2,144,128]{2,1,0:T(8,128)S(1)} %get-tuple-element.40.keep.refs_3_, bf16[432,192]{1,0:T(8,128)(2,1)S(1)} %get-tuple-element.55.far, bf16[144,192]{1,0:T(8,128)(2,1)S(1)} %get-tuple-element.68.done, f32[2,144,192]{2,1,0:T(8,128)S(1)} %add.1.middle, ...), custom_call_target="tpu_custom_call" | custom-call | flops 2000000000 | bytes 1048576 | tf_op jit(solution)/shard_map/last/pallas_call | solution.py:474
  (2 shorter events, 0.0 us)
Async XLA Ops:
  0.0 5.0 %collective-permute-start = (bf16[2,4,1242]{2,1,0:T(4,128)(2,1)}, bf16[2,4,1242]{2,1,0:T(4,128)(2,1)S(1)}, u32[]{:S(2)}, u32[]{:S(2)}) collective-permute-start(bf16[2,4,1242]{2,1,0:T(4,128)(2,1)} %bitcast.14), channel_id=1, source_target_pairs={{0,8},{1,9},{2,10},{3,11},{4,12},{5,13},{6,14},{7,15},{8,0},{9,1},... | collective-permute-start | bytes 59624 | tf_op jit(solution)/shard_map/ppermute | solution.py:507
  5.0 3.8 %collective-permute-start.1 = (bf16[2,2,4,1242]{3,2,1,0:T(4,128)(2,1)S(1)}, bf16[2,2,4,1242]{3,2,1,0:T(4,128)(2,1)S(1)}, u32[]{:S(2)}, u32[]{:S(2)}) collective-permute-start(bf16[2,2,4,1242]{3,2,1,0:T(4,128)(2,1)S(1)} %halves.1.refs_0_), channel_id=1, source_target_pairs={{0,2},{1,3},{2,4},{3,5},{4,6},{5,7},{6,0},{7,1},{8,10},{9,11},{10,... | collective-permute-start | bytes 119240 | tf_op jit(solution)/shard_map/ppermute | solution.py:507
  5.2 4.4 %collective-permute-start.2 = (bf16[2,2,4,1242]{3,2,1,0:T(4,128)(2,1)S(1)}, bf16[2,2,4,1242]{3,2,1,0:T(4,128)(2,1)S(1)}, u32[]{:S(2)}, u32[]{:S(2)}) collective-permute-start(bf16[2,2,4,1242]{3,2,1,0:T(4,128)(2,1)S(1)} %halves.1.refs_0_), channel_id=1, source_target_pairs={{0,4},{1,5},{2,6},{3,7},{4,0},{5,1},{6,2},{7,3},{8,12},{9,13},{10,... | collective-permute-start | bytes 119240 | tf_op jit(solution)/shard_map/ppermute | solution.py:507
  7.3 4.1 %collective-permute-start.3 = (bf16[2,2,4,1242]{3,2,1,0:T(4,128)(2,1)S(1)}, bf16[2,2,4,1242]{3,2,1,0:T(4,128)(2,1)S(1)}, u32[]{:S(2)}, u32[]{:S(2)}) collective-permute-start(bf16[2,2,4,1242]{3,2,1,0:T(4,128)(2,1)S(1)} %halves.1.refs_0_), channel_id=1, source_target_pairs={{0,6},{1,7},{2,0},{3,1},{4,2},{5,3},{6,4},{7,5},{8,14},{9,15},{10,... | collective-permute-start | bytes 119240 | tf_op jit(solution)/shard_map/ppermute | solution.py:507
  11.4 4.5 %collective-permute-start.4 = (bf16[8,2,4,1242]{3,2,1,0:T(4,128)(2,1)S(1)}, bf16[8,2,4,1242]{3,2,1,0:T(4,128)(2,1)S(1)}, u32[]{:S(2)}, u32[]{:S(2)}) collective-permute-start(bf16[8,2,4,1242]{3,2,1,0:T(4,128)(2,1)S(1)} %mine.1.refs_0_), channel_id=1, source_target_pairs={{0,1},{1,0},{2,3},{3,2},{4,5},{5,4},{6,7},{7,6},{8,9},{9,8},{10,11... | collective-permute-start | bytes 476936 | tf_op jit(solution)/shard_map/ppermute | solution.py:507
  19.5 8.1 %collective-permute-start.5 = (bf16[224,128]{1,0:T(8,128)(2,1)S(1)}, bf16[224,128]{1,0:T(8,128)(2,1)S(1)}, u32[]{:S(2)}, u32[]{:S(2)}) collective-permute-start(bf16[224,128]{1,0:T(8,128)(2,1)S(1)} %get-tuple-element.61), channel_id=1, source_target_pairs={{0,15},{1,0},{2,1},{3,2},{4,3},{5,4},{6,5},{7,6},{8,7},{9,8},{10,9... | collective-permute-start | bytes 172040 | tf_op jit(solution)/shard_map/ppermute | solution.py:499
  19.8 7.8 %collective-permute-start.6 = (bf16[224,128]{1,0:T(8,128)(2,1)S(1)}, bf16[224,128]{1,0:T(8,128)(2,1)S(1)}, u32[]{:S(2)}, u32[]{:S(2)}) collective-permute-start(bf16[224,128]{1,0:T(8,128)(2,1)S(1)} %get-tuple-element.62), channel_id=1, source_target_pairs={{0,113},{1,114},{2,115},{3,116},{4,117},{5,118},{6,119},{7,120},{8... | collective-permute-start | bytes 172040 | tf_op jit(solution)/shard_map/ppermute | solution.py:499
  25.9 3.0 %collective-permute-start.7 = (bf16[224,128]{1,0:T(8,128)(2,1)S(1)}, bf16[224,128]{1,0:T(8,128)(2,1)S(1)}, u32[]{:S(2)}, u32[]{:S(2)}) collective-permute-start(bf16[224,128]{1,0:T(8,128)(2,1)S(1)} %get-tuple-element.63), channel_id=1, source_target_pairs={{0,112},{1,113},{2,114},{3,115},{4,116},{5,117},{6,118},{7,119},{8... | collective-permute-start | bytes 172040 | tf_op jit(solution)/shard_map/ppermute | solution.py:499
  28.9 7.4 %copy-start = (f32[768]{0:T(1024)S(1)}, f32[768]{0:T(1024)}, u32[]{:S(2)}) copy-start(f32[768]{0:T(1024)} %param.20) | copy-start | bytes 9220
  31.3 7.0 %collective-permute-start.8 = (bf16[224,128]{1,0:T(8,128)(2,1)S(1)}, bf16[224,128]{1,0:T(8,128)(2,1)S(1)}, u32[]{:S(2)}, u32[]{:S(2)}) collective-permute-start(bf16[224,128]{1,0:T(8,128)(2,1)S(1)} %get-tuple-element.69), channel_id=1, source_target_pairs={{0,1},{1,2},{2,3},{3,4},{4,5},{5,6},{6,7},{7,8},{8,9},{9,10},{10,1... | collective-permute-start | bytes 172040 | tf_op jit(solution)/shard_map/ppermute | solution.py:499
  33.7 9.0 %collective-permute-start.9 = (bf16[224,128]{1,0:T(8,128)(2,1)S(1)}, bf16[224,128]{1,0:T(8,128)(2,1)S(1)}, u32[]{:S(2)}, u32[]{:S(2)}) collective-permute-start(bf16[224,128]{1,0:T(8,128)(2,1)S(1)} %get-tuple-element.70), channel_id=1, source_target_pairs={{0,17},{1,18},{2,19},{3,20},{4,21},{5,22},{6,23},{7,24},{8,25},{9,... | collective-permute-start | bytes 172040 | tf_op jit(solution)/shard_map/ppermute | solution.py:499
  36.4 6.4 %collective-permute-start.10 = (bf16[224,128]{1,0:T(8,128)(2,1)S(1)}, bf16[224,128]{1,0:T(8,128)(2,1)S(1)}, u32[]{:S(2)}, u32[]{:S(2)}) collective-permute-start(bf16[224,128]{1,0:T(8,128)(2,1)S(1)} %get-tuple-element.71), channel_id=1, source_target_pairs={{0,16},{1,17},{2,18},{3,19},{4,20},{5,21},{6,22},{7,23},{8,24},{9,... | collective-permute-start | bytes 172040 | tf_op jit(solution)/shard_map/ppermute | solution.py:499

commit v5 on v3

--- a/solution.py
+++ b/solution.py
@@ -359,7 +359,8 @@
 def first_kernel(mine, theirs, scores, v, first_mask, keep, inputs, gains, query_choice, proj, fc1, fc2, lanes, rows, sent_lat, sent_lon, sent_both, table_out, out, cells, table_f32, t_top, t_low):
     me = lax.axis_index("lon")
     for g in range(LONS):
-        slot = lax.rem(me // 2 - g // 2 + 8, 4) * 2 + jnp.where(me // 8 == g // 8, 0, 1)
+        hops = lax.rem(me // 2 - g // 2 + 8, 4)
+        slot = jnp.where(hops == 1, 2, jnp.where(hops == 2, 1, hops)) * 2 + jnp.where(me // 8 == g // 8, 0, 1)
         shard = jnp.where(lax.rem(me, 2) == g % 2, mine[slot], theirs[slot]).astype(F32)
         piece = jnp.concatenate([shard[0], shard[1]], axis=0)
         for n in range(9):
@@ -560,7 +561,7 @@
         *[in_hbm(array) for array in late],
         in_specs=[VMEM_SPEC] * 5 + [hbm_spec] * len(late),
     )
-    mine = call(join_kernel, "mine", 0.3, shape(8, 2, WINDOWS, SHARD), [], halves, *ring, v)
+    mine = call(join_kernel, "mine", 0.3, shape(8, 2, WINDOWS, SHARD), [], halves, ring[1], ring[0], ring[2], v)
     theirs = turned(mine, lambda z, x, core: (z, x, 1 - core))
     proj0, fc1_0, fc2_0, lanes, rows, columns = call(
         functools.partial(sliced, prepare_kernel, {1: 0, 2: 0, 3: 0}),

time: 45.1 us -> 45.3 us (level)
    ppermute x5, starting transfers between devices: 9.27 us -> 9.87 us  [turned(): return lax.ppermute(block, 'lon', route)]
    ppermute x6, starting transfers between devices: 11.7 us -> 11.1 us  [sent(): return lax.ppermute(block, ('lat', 'lon'), route)]
  transfers between devices with their start and end apart: 11 -> 11, of which waited for: 5 -> 5; matrix products, arithmetic and copies ran while one was open for 0% -> 0% of each run, Pallas kernels for 17% -> 16%
where the time goes in v5:
time: 45.3 us; the launch traced here: 45.1 us
  starting transfers between devices  21 us (46%)
  Pallas kernels  15.5 us (34%)
  waiting for transfers between devices  8.39 us (19%)
    pallas_call x12, Pallas kernels, call(): pl.pallas_call(kernel, name=name, out_shape=outs, in_specs=in_specs or [V...  15.5 us
    ppermute x6, starting transfers between devices, sent(): return lax.ppermute(block, ('lat', 'lon'), route)  11.1 us
    ppermute x5, starting transfers between devices, turned(): return lax.ppermute(block, 'lon', route)  9.87 us
    ppermute x6, waiting for transfers between devices, sent(): return lax.ppermute(block, ('lat', 'lon'), route)  5.66 us
    ppermute x5, waiting for transfers between devices, turned(): return lax.ppermute(block, 'lon', route)  2.73 us
  transfers between devices with their start and end apart: 11, of which 5 were waited for; matrix products, arithmetic and copies ran while one was open for 0% of the time, Pallas kernels for 16%

profile of v5, /device:TPU:7, one launch (start us, length us, event | category | flops | bytes accessed | tf_op | source)
XLA Modules:
  0.0 45.1 jit_solution(16394096508027733385)
XLA Ops:
  0.0 3.6 %collective-permute-start = (bf16[2,4,1242]{2,1,0:T(4,128)(2,1)}, bf16[2,4,1242]{2,1,0:T(4,128)(2,1)S(1)}, u32[]{:S(2)}, u32[]{:S(2)}) collective-permute-start(bf16[2,4,1242]{2,1,0:T(4,128)(2,1)} %bitcast.14), channel_id=1, source_target_pairs={{0,8},{1,9},{2,10},{3,11},{4,12},{5,13},{6,14},{7,15},{8,0},{9,1},... | collective-permute-start | bytes 59624 | tf_op jit(solution)/shard_map/ppermute | solution.py:506
  3.6 1.2 %fetch.1 = (bf16[1,2,4,1242]{3,2,1,0:T(4,128)(2,1)S(1)}, bf16[576,192]{1,0:T(8,128)(2,1)S(1)}, f32[2,2,192]{2,1,0:T(2,128)S(1)}, bf16[192,576]{1,0:T(8,128)(2,1)...) custom-call(s32[48]{0:T(128)} %refs_0_.2, ...), custom_call_target="tpu_custom_call" | custom-call | flops 1400000000 | bytes 1048576 | tf_op jit(solution)/shard_map/fetch/pallas_call | solution.py:473
  4.8 0.2 collective-permute-done
  5.0 1.1 %collective-permute-start.1 = (bf16[2,2,4,1242]{3,2,1,0:T(4,128)(2,1)S(1)}, bf16[2,2,4,1242]{3,2,1,0:T(4,128)(2,1)S(1)}, u32[]{:S(2)}, u32[]{:S(2)}) collective-permute-start(bf16[2,2,4,1242]{3,2,1,0:T(4,128)(2,1)S(1)} %halves.1.refs_0_), channel_id=1, source_target_pairs={{0,4},{1,5},{2,6},{3,7},{4,0},{5,1},{6,2},{7,3},{8,12},{9,13},{10,... | collective-permute-start | bytes 119240 | tf_op jit(solution)/shard_map/ppermute | solution.py:506
  6.1 1.8 %collective-permute-start.2 = (bf16[2,2,4,1242]{3,2,1,0:T(4,128)(2,1)S(1)}, bf16[2,2,4,1242]{3,2,1,0:T(4,128)(2,1)S(1)}, u32[]{:S(2)}, u32[]{:S(2)}) collective-permute-start(bf16[2,2,4,1242]{3,2,1,0:T(4,128)(2,1)S(1)} %halves.1.refs_0_), channel_id=1, source_target_pairs={{0,2},{1,3},{2,4},{3,5},{4,6},{5,7},{6,0},{7,1},{8,10},{9,11},{10,... | collective-permute-start | bytes 119240 | tf_op jit(solution)/shard_map/ppermute | solution.py:506
  7.9 0.0 collective-permute-start.3
  7.9 1.5 %before.1 = (f32[4,864,256]{2,1,0:T(8,128)S(1)}, bf16[4,256,256]{2,1,0:T(8,128)(2,1)S(1)}, f32[2,576,128]{2,1,0:T(8,128)S(1)}, bf16[192,576]{1,0:T(8,128)(2,1)S(1)}, bf16[192,192]{1,0:T(8,128)(2,1)S(1)}) custom-call(bf16[2,2,4,1242]{3,2,1,0:T(4,128)(2,1)S(1)} %halves.1.refs_0_, bf16[576,192]{1,0:T(8,128)(2,1)S(1)} %get-tuple-element.42.refs_1_, ...), custom_call_target="tpu_custom_call" | custom-call | flops 2500000000 | bytes 1048576 | tf_op jit(solution)/shard_map/before/pallas_call | solution.py:473
  9.4 0.0 collective-permute-done.1.refs_1_
  9.4 0.0 collective-permute-done.2.refs_2_
  9.4 2.6 %collective-permute-done.3.refs_3_ = bf16[2,2,4,1242]{3,2,1,0:T(4,128)(2,1)S(1)} collective-permute-done((bf16[2,2,4,1242]{3,2,1,0:T(4,128)(2,1)S(1)}, bf16[2,2,4,1242]{3,2,1,0:T(4,128)(2,1)S(1)}, u32[]{:S(2)}, u32[]{:S(2)}) %collective-permute-start.3) | collective-permute-done | bytes 39776 | tf_op jit(solution)/shard_map/ppermute | solution.py:506
  12.0 3.3 %collective-permute-start.4 = (bf16[8,2,4,1242]{3,2,1,0:T(4,128)(2,1)S(1)}, bf16[8,2,4,1242]{3,2,1,0:T(4,128)(2,1)S(1)}, u32[]{:S(2)}, u32[]{:S(2)}) collective-permute-start(bf16[8,2,4,1242]{3,2,1,0:T(4,128)(2,1)S(1)} %mine.1.refs_0_), channel_id=1, source_target_pairs={{0,1},{1,0},{2,3},{3,2},{4,5},{5,4},{6,7},{7,6},{8,9},{9,8},{10,11... | collective-permute-start | bytes 476936 | tf_op jit(solution)/shard_map/ppermute | solution.py:506
  15.3 1.1 %prepare.1 = (bf16[192,192]{1,0:T(8,128)(2,1)S(1)}, bf16[192,768]{1,0:T(8,128)(2,1)S(1)}, bf16[192,768]{1,0:T(8,128)(2,1)S(1)}, bf16[138,256]{1,0:T(8,128)(2,1)S...) custom-call(bf16[8,2,4,1242]{3,2,1,0:T(4,128)(2,1)S(1)} %mine.1.refs_0_, ...), custom_call_target="tpu_custom_call" | custom-call | flops 1200000000 | bytes 1048576 | tf_op jit(solution)/shard_map/prepare/pallas_call | solution.py:473
  16.5 0.0 collective-permute-done.4.theirs
  16.5 3.5 %first.1 = (bf16[224,128]{1,0:T(8,128)(2,1)S(1)}, bf16[224,128]{1,0:T(8,128)(2,1)S(1)}, bf16[224,128]{1,0:T(8,128)(2,1)S(1)}, bf16[1152,256]{1,0:T(8,128)(2,1)S(...) custom-call(bf16[8,2,4,1242]{3,2,1,0:T(4,128)(2,1)S(1)} %mine.1.refs_0_, ...), custom_call_target="tpu_custom_call" | custom-call | flops 4499999744 | bytes 1048576 | tf_op jit(solution)/shard_map/first/pallas_call | solution.py:473
  20.0 0.3 collective-permute-start.5
  20.3 5.5 %collective-permute-start.6 = (bf16[224,128]{1,0:T(8,128)(2,1)S(1)}, bf16[224,128]{1,0:T(8,128)(2,1)S(1)}, u32[]{:S(2)}, u32[]{:S(2)}) collective-permute-start(bf16[224,128]{1,0:T(8,128)(2,1)S(1)} %get-tuple-element.62), channel_id=1, source_target_pairs={{0,113},{1,114},{2,115},{3,116},{4,117},{5,118},{6,119},{7,120},{8... | collective-permute-start | bytes 172040 | tf_op jit(solution)/shard_map/ppermute | solution.py:498
  25.8 0.3 collective-permute-start.7
  26.1 1.4 %bias.1 = (bf16[4,864,256]{2,1,0:T(8,128)(2,1)S(1)}, bf16[144,192]{1,0:T(8,128)(2,1)S(1)}) custom-call(bf16[1152,256]{1,0:T(8,128)(2,1)S(1)} %get-tuple-element.56.table, f32[2,144,256]{2,1,0:T(8,128)S(1)} %get-tuple-element.57.second_mask, bf16[2,138,768]{2,1,0:T(8,128)(2,1)S(1)} %get-tuple-element.58.columns, ...), custom_call_target="tpu_custom_call" | custom-call | flops 200000000 | bytes 1048576 | tf_op jit(solution)/shard_map/bias/pallas_call | solution.py:473
  27.5 0.4 collective-permute-done.5.from_lon
  27.9 0.0 collective-permute-done.6.from_both
  27.9 0.3 ready.1.given
  28.2 0.6 %collective-permute-done.7.from_lat = bf16[224,128]{1,0:T(8,128)(2,1)S(1)} collective-permute-done((bf16[224,128]{1,0:T(8,128)(2,1)S(1)}, bf16[224,128]{1,0:T(8,128)(2,1)S(1)}, u32[]{:S(2)}, u32[]{:S(2)}) %collective-permute-start.7) | collective-permute-done | bytes 57376 | tf_op jit(solution)/shard_map/ppermute | solution.py:498
  28.8 0.0 copy-start
  28.8 2.4 %second.1 = (bf16[144,192]{1,0:T(8,128)(2,1)S(1)}, bf16[224,128]{1,0:T(8,128)(2,1)S(1)}, bf16[224,128]{1,0:T(8,128)(2,1)S(1)}, bf16[224,128]{1,0:T(8,128)(2,1)S(1)}) custom-call(f32[2,576,128]{2,1,0:T(8,128)S(1)} %ready.1.given, bf16[224,128]{1,0:T(8,128)(2,1)S(1)} %collective-permute-done.7.from_lat, bf16[4,864,256]{2,1,0:T(8,128)(2,1)S(1)} %get-tuple-element.64.bias, ...), custom_call_target="tpu_custom_call" | custom-call | flops 4499999744 | bytes 1048576 | tf_op jit(solution)/shard_map/second/pallas_call | solution.py:473
  31.2 2.6 %collective-permute-start.8 = (bf16[224,128]{1,0:T(8,128)(2,1)S(1)}, bf16[224,128]{1,0:T(8,128)(2,1)S(1)}, u32[]{:S(2)}, u32[]{:S(2)}) collective-permute-start(bf16[224,128]{1,0:T(8,128)(2,1)S(1)} %get-tuple-element.69), channel_id=1, source_target_pairs={{0,1},{1,2},{2,3},{3,4},{4,5},{5,6},{6,7},{7,8},{8,9},{9,10},{10,1... | collective-permute-start | bytes 172040 | tf_op jit(solution)/shard_map/ppermute | solution.py:498
  33.8 2.4 %collective-permute-start.9 = (bf16[224,128]{1,0:T(8,128)(2,1)S(1)}, bf16[224,128]{1,0:T(8,128)(2,1)S(1)}, u32[]{:S(2)}, u32[]{:S(2)}) collective-permute-start(bf16[224,128]{1,0:T(8,128)(2,1)S(1)} %get-tuple-element.70), channel_id=1, source_target_pairs={{0,17},{1,18},{2,19},{3,20},{4,21},{5,22},{6,23},{7,24},{8,25},{9,... | collective-permute-start | bytes 172040 | tf_op jit(solution)/shard_map/ppermute | solution.py:498
  36.2 0.0 copy-done
  36.2 0.1 reshape.10.merge_gain
  36.3 0.0 collective-permute-start.10
  36.3 1.8 %own.1 = (bf16[144,192]{1,0:T(8,128)(2,1)S(1)}, bf16[192,768]{1,0:T(8,128)(2,1)S(1)}, bf16[192,768]{1,0:T(8,128)(2,1)S(1)}, bf16[768,384]{1,0:T(8,128)(2,1)S(1)}) custom-call(bf16[2,192,768]{2,1,0:T(8,128)(2,1)} %refs_0_.3, bf16[2,192,768]{2,1,0:T(8,128)(2,1)} %bitcast.12, bf16[768,384]{1,0:T(8,128)(2,1)} %refs_2_.3, ...), custom_call_target="tpu_custom_call" | custom-call | flops 500000000 | bytes 1048576 | tf_op jit(solution)/shard_map/own/pallas_call | solution.py:473
  38.2 0.0 collective-permute-done.8.from_lon
  38.2 4.7 %collective-permute-done.9.from_both = bf16[224,128]{1,0:T(8,128)(2,1)S(1)} collective-permute-done((bf16[224,128]{1,0:T(8,128)(2,1)S(1)}, bf16[224,128]{1,0:T(8,128)(2,1)S(1)}, u32[]{:S(2)}, u32[]{:S(2)}) %collective-permute-start.9) | collective-permute-done | bytes 57376 | tf_op jit(solution)/shard_map/ppermute | solution.py:498
  42.9 0.1 add.1.middle
  42.9 0.0 collective-permute-done.10.from_lat
  42.9 2.2 %last.1 = bf16[144,384]{1,0:T(8,128)(2,1)} custom-call(f32[2,144,128]{2,1,0:T(8,128)S(1)} %get-tuple-element.40.keep.refs_3_, bf16[432,192]{1,0:T(8,128)(2,1)S(1)} %get-tuple-element.55.far, bf16[144,192]{1,0:T(8,128)(2,1)S(1)} %get-tuple-element.68.done, f32[2,144,192]{2,1,0:T(8,128)S(1)} %add.1.middle, ...), custom_call_target="tpu_custom_call" | custom-call | flops 2000000000 | bytes 1048576 | tf_op jit(solution)/shard_map/last/pallas_call | solution.py:473
  (2 shorter events, 0.0 us)
Async XLA Ops:
  0.0 5.0 %collective-permute-start = (bf16[2,4,1242]{2,1,0:T(4,128)(2,1)}, bf16[2,4,1242]{2,1,0:T(4,128)(2,1)S(1)}, u32[]{:S(2)}, u32[]{:S(2)}) collective-permute-start(bf16[2,4,1242]{2,1,0:T(4,128)(2,1)} %bitcast.14), channel_id=1, source_target_pairs={{0,8},{1,9},{2,10},{3,11},{4,12},{5,13},{6,14},{7,15},{8,0},{9,1},... | collective-permute-start | bytes 59624 | tf_op jit(solution)/shard_map/ppermute | solution.py:506
  5.0 4.4 %collective-permute-start.1 = (bf16[2,2,4,1242]{3,2,1,0:T(4,128)(2,1)S(1)}, bf16[2,2,4,1242]{3,2,1,0:T(4,128)(2,1)S(1)}, u32[]{:S(2)}, u32[]{:S(2)}) collective-permute-start(bf16[2,2,4,1242]{3,2,1,0:T(4,128)(2,1)S(1)} %halves.1.refs_0_), channel_id=1, source_target_pairs={{0,4},{1,5},{2,6},{3,7},{4,0},{5,1},{6,2},{7,3},{8,12},{9,13},{10,... | collective-permute-start | bytes 119240 | tf_op jit(solution)/shard_map/ppermute | solution.py:506
  6.1 3.3 %collective-permute-start.2 = (bf16[2,2,4,1242]{3,2,1,0:T(4,128)(2,1)S(1)}, bf16[2,2,4,1242]{3,2,1,0:T(4,128)(2,1)S(1)}, u32[]{:S(2)}, u32[]{:S(2)}) collective-permute-start(bf16[2,2,4,1242]{3,2,1,0:T(4,128)(2,1)S(1)} %halves.1.refs_0_), channel_id=1, source_target_pairs={{0,2},{1,3},{2,4},{3,5},{4,6},{5,7},{6,0},{7,1},{8,10},{9,11},{10,... | collective-permute-start | bytes 119240 | tf_op jit(solution)/shard_map/ppermute | solution.py:506
  7.9 4.1 %collective-permute-start.3 = (bf16[2,2,4,1242]{3,2,1,0:T(4,128)(2,1)S(1)}, bf16[2,2,4,1242]{3,2,1,0:T(4,128)(2,1)S(1)}, u32[]{:S(2)}, u32[]{:S(2)}) collective-permute-start(bf16[2,2,4,1242]{3,2,1,0:T(4,128)(2,1)S(1)} %halves.1.refs_0_), channel_id=1, source_target_pairs={{0,6},{1,7},{2,0},{3,1},{4,2},{5,3},{6,4},{7,5},{8,14},{9,15},{10,... | collective-permute-start | bytes 119240 | tf_op jit(solution)/shard_map/ppermute | solution.py:506
  12.0 4.5 %collective-permute-start.4 = (bf16[8,2,4,1242]{3,2,1,0:T(4,128)(2,1)S(1)}, bf16[8,2,4,1242]{3,2,1,0:T(4,128)(2,1)S(1)}, u32[]{:S(2)}, u32[]{:S(2)}) collective-permute-start(bf16[8,2,4,1242]{3,2,1,0:T(4,128)(2,1)S(1)} %mine.1.refs_0_), channel_id=1, source_target_pairs={{0,1},{1,0},{2,3},{3,2},{4,5},{5,4},{6,7},{7,6},{8,9},{9,8},{10,11... | collective-permute-start | bytes 476936 | tf_op jit(solution)/shard_map/ppermute | solution.py:506
  20.0 7.8 %collective-permute-start.5 = (bf16[224,128]{1,0:T(8,128)(2,1)S(1)}, bf16[224,128]{1,0:T(8,128)(2,1)S(1)}, u32[]{:S(2)}, u32[]{:S(2)}) collective-permute-start(bf16[224,128]{1,0:T(8,128)(2,1)S(1)} %get-tuple-element.61), channel_id=1, source_target_pairs={{0,15},{1,0},{2,1},{3,2},{4,3},{5,4},{6,5},{7,6},{8,7},{9,8},{10,9... | collective-permute-start | bytes 172040 | tf_op jit(solution)/shard_map/ppermute | solution.py:498
  20.3 7.5 %collective-permute-start.6 = (bf16[224,128]{1,0:T(8,128)(2,1)S(1)}, bf16[224,128]{1,0:T(8,128)(2,1)S(1)}, u32[]{:S(2)}, u32[]{:S(2)}) collective-permute-start(bf16[224,128]{1,0:T(8,128)(2,1)S(1)} %get-tuple-element.62), channel_id=1, source_target_pairs={{0,113},{1,114},{2,115},{3,116},{4,117},{5,118},{6,119},{7,120},{8... | collective-permute-start | bytes 172040 | tf_op jit(solution)/shard_map/ppermute | solution.py:498
  25.8 3.0 %collective-permute-start.7 = (bf16[224,128]{1,0:T(8,128)(2,1)S(1)}, bf16[224,128]{1,0:T(8,128)(2,1)S(1)}, u32[]{:S(2)}, u32[]{:S(2)}) collective-permute-start(bf16[224,128]{1,0:T(8,128)(2,1)S(1)} %get-tuple-element.63), channel_id=1, source_target_pairs={{0,112},{1,113},{2,114},{3,115},{4,116},{5,117},{6,118},{7,119},{8... | collective-permute-start | bytes 172040 | tf_op jit(solution)/shard_map/ppermute | solution.py:498
  28.8 7.4 %copy-start = (f32[768]{0:T(1024)S(1)}, f32[768]{0:T(1024)}, u32[]{:S(2)}) copy-start(f32[768]{0:T(1024)} %param.20) | copy-start | bytes 9220
  31.2 7.0 %collective-permute-start.8 = (bf16[224,128]{1,0:T(8,128)(2,1)S(1)}, bf16[224,128]{1,0:T(8,128)(2,1)S(1)}, u32[]{:S(2)}, u32[]{:S(2)}) collective-permute-start(bf16[224,128]{1,0:T(8,128)(2,1)S(1)} %get-tuple-element.69), channel_id=1, source_target_pairs={{0,1},{1,2},{2,3},{3,4},{4,5},{5,6},{6,7},{7,8},{8,9},{9,10},{10,1... | collective-permute-start | bytes 172040 | tf_op jit(solution)/shard_map/ppermute | solution.py:498
  33.8 9.0 %collective-permute-start.9 = (bf16[224,128]{1,0:T(8,128)(2,1)S(1)}, bf16[224,128]{1,0:T(8,128)(2,1)S(1)}, u32[]{:S(2)}, u32[]{:S(2)}) collective-permute-start(bf16[224,128]{1,0:T(8,128)(2,1)S(1)} %get-tuple-element.70), channel_id=1, source_target_pairs={{0,17},{1,18},{2,19},{3,20},{4,21},{5,22},{6,23},{7,24},{8,25},{9,... | collective-permute-start | bytes 172040 | tf_op jit(solution)/shard_map/ppermute | solution.py:498
  36.3 6.6 %collective-permute-start.10 = (bf16[224,128]{1,0:T(8,128)(2,1)S(1)}, bf16[224,128]{1,0:T(8,128)(2,1)S(1)}, u32[]{:S(2)}, u32[]{:S(2)}) collective-permute-start(bf16[224,128]{1,0:T(8,128)(2,1)S(1)} %get-tuple-element.71), channel_id=1, source_target_pairs={{0,16},{1,17},{2,18},{3,19},{4,20},{5,21},{6,22},{7,23},{8,24},{9,... | collective-permute-start | bytes 172040 | tf_op jit(solution)/shard_map/ppermute | solution.py:498

commit v6 on v3

--- a/solution.py
+++ b/solution.py
@@ -427,7 +427,7 @@
     result[...] = feed_forward(middle, gains[1, 1:2], refs[0][...], refs[1][...], keep[1][:, :1] > 0)
 
 
-def add_kernel(far, from_lon, from_both, middle):
+def add_kernel(far, from_both, from_lon, middle):
     for at, piece in enumerate((from_lon, from_both)):
         inputs = far[(at + 1) * TOKENS : (at + 2) * TOKENS].astype(F32)
         middle[at] = inputs + unpack_piece(piece[...]).astype(F32)
@@ -608,7 +608,7 @@
         in_specs=[hbm_spec] * 3 + [VMEM_SPEC] * 4,
     )
     middle = call(
-        add_kernel, "add", 0.2, shape(2, TOKENS, C, dtype=F32), [], far, from_lon, from_both
+        add_kernel, "add", 0.2, shape(2, TOKENS, C, dtype=F32), [], far, from_both, from_lon
     )
     merged = call(
         last_kernel,

time: 45.1 us -> 43.7 us (0.969)
  the two profiles are of different devices: /device:TPU:7 before, /device:TPU:24 now
where the time goes in v6:
time: 43.7 us; the launch traced here: 43.5 us
  starting transfers between devices  20.3 us (46%)
  Pallas kernels  15.5 us (35%)
  waiting for transfers between devices  7.53 us (17%)
    pallas_call x12, Pallas kernels, call(): pl.pallas_call(kernel, name=name, out_shape=outs, in_specs=in_specs or [V...  15.5 us
    ppermute x6, starting transfers between devices, sent(): return lax.ppermute(block, ('lat', 'lon'), route)  10.7 us
    ppermute x5, starting transfers between devices, turned(): return lax.ppermute(block, 'lon', route)  9.62 us
    ppermute x6, waiting for transfers between devices, sent(): return lax.ppermute(block, ('lat', 'lon'), route)  5.46 us
    ppermute x5, waiting for transfers between devices, turned(): return lax.ppermute(block, 'lon', route)  2.07 us
  transfers between devices with their start and end apart: 11, of which 7 were waited for; matrix products, arithmetic and copies ran while one was open for 0% of the time, Pallas kernels for 17%

profile of v6, /device:TPU:24, one launch (start us, length us, event | category | flops | bytes accessed | tf_op | source)
XLA Modules:
  0.0 43.5 jit_solution(10760218877737886626)
XLA Ops:
  0.0 3.9 %collective-permute-start = (bf16[2,4,1242]{2,1,0:T(4,128)(2,1)}, bf16[2,4,1242]{2,1,0:T(4,128)(2,1)S(1)}, u32[]{:S(2)}, u32[]{:S(2)}) collective-permute-start(bf16[2,4,1242]{2,1,0:T(4,128)(2,1)} %bitcast.14), channel_id=1, source_target_pairs={{0,8},{1,9},{2,10},{3,11},{4,12},{5,13},{6,14},{7,15},{8,0},{9,1},... | collective-permute-start | bytes 59624 | tf_op jit(solution)/shard_map/ppermute | solution.py:505
  3.9 1.2 %fetch.1 = (bf16[1,2,4,1242]{3,2,1,0:T(4,128)(2,1)S(1)}, bf16[576,192]{1,0:T(8,128)(2,1)S(1)}, f32[2,2,192]{2,1,0:T(2,128)S(1)}, bf16[192,576]{1,0:T(8,128)(2,1)...) custom-call(s32[48]{0:T(128)} %refs_0_.2, ...), custom_call_target="tpu_custom_call" | custom-call | flops 1400000000 | bytes 1048576 | tf_op jit(solution)/shard_map/fetch/pallas_call | solution.py:472
  5.1 0.8 %collective-permute-done = bf16[2,4,1242]{2,1,0:T(4,128)(2,1)S(1)} collective-permute-done((bf16[2,4,1242]{2,1,0:T(4,128)(2,1)}, bf16[2,4,1242]{2,1,0:T(4,128)(2,1)S(1)}, u32[]{:S(2)}, u32[]{:S(2)}) %collective-permute-start) | collective-permute-done | bytes 19904 | tf_op jit(solution)/shard_map/ppermute | solution.py:505
  5.9 1.5 %collective-permute-start.1 = (bf16[2,2,4,1242]{3,2,1,0:T(4,128)(2,1)S(1)}, bf16[2,2,4,1242]{3,2,1,0:T(4,128)(2,1)S(1)}, u32[]{:S(2)}, u32[]{:S(2)}) collective-permute-start(bf16[2,2,4,1242]{3,2,1,0:T(4,128)(2,1)S(1)} %halves.1.refs_0_), channel_id=1, source_target_pairs={{0,2},{1,3},{2,4},{3,5},{4,6},{5,7},{6,0},{7,1},{8,10},{9,11},{10,... | collective-permute-start | bytes 119240 | tf_op jit(solution)/shard_map/ppermute | solution.py:505
  7.3 2.7 %collective-permute-start.2 = (bf16[2,2,4,1242]{3,2,1,0:T(4,128)(2,1)S(1)}, bf16[2,2,4,1242]{3,2,1,0:T(4,128)(2,1)S(1)}, u32[]{:S(2)}, u32[]{:S(2)}) collective-permute-start(bf16[2,2,4,1242]{3,2,1,0:T(4,128)(2,1)S(1)} %halves.1.refs_0_), channel_id=1, source_target_pairs={{0,4},{1,5},{2,6},{3,7},{4,0},{5,1},{6,2},{7,3},{8,12},{9,13},{10,... | collective-permute-start | bytes 119240 | tf_op jit(solution)/shard_map/ppermute | solution.py:505
  10.1 1.4 %collective-permute-start.3 = (bf16[2,2,4,1242]{3,2,1,0:T(4,128)(2,1)S(1)}, bf16[2,2,4,1242]{3,2,1,0:T(4,128)(2,1)S(1)}, u32[]{:S(2)}, u32[]{:S(2)}) collective-permute-start(bf16[2,2,4,1242]{3,2,1,0:T(4,128)(2,1)S(1)} %halves.1.refs_0_), channel_id=1, source_target_pairs={{0,6},{1,7},{2,0},{3,1},{4,2},{5,3},{6,4},{7,5},{8,14},{9,15},{10,... | collective-permute-start | bytes 119240 | tf_op jit(solution)/shard_map/ppermute | solution.py:505
  11.5 1.5 %before.1 = (f32[4,864,256]{2,1,0:T(8,128)S(1)}, bf16[4,256,256]{2,1,0:T(8,128)(2,1)S(1)}, f32[2,576,128]{2,1,0:T(8,128)S(1)}, bf16[192,576]{1,0:T(8,128)(2,1)S(1)}, bf16[192,192]{1,0:T(8,128)(2,1)S(1)}) custom-call(bf16[2,2,4,1242]{3,2,1,0:T(4,128)(2,1)S(1)} %halves.1.refs_0_, bf16[576,192]{1,0:T(8,128)(2,1)S(1)} %get-tuple-element.42.refs_1_, ...), custom_call_target="tpu_custom_call" | custom-call | flops 2500000000 | bytes 1048576 | tf_op jit(solution)/shard_map/before/pallas_call | solution.py:472
  13.0 0.0 collective-permute-done.1.refs_1_
  13.0 0.0 collective-permute-done.2.refs_2_
  13.0 1.1 %collective-permute-done.3.refs_3_ = bf16[2,2,4,1242]{3,2,1,0:T(4,128)(2,1)S(1)} collective-permute-done((bf16[2,2,4,1242]{3,2,1,0:T(4,128)(2,1)S(1)}, bf16[2,2,4,1242]{3,2,1,0:T(4,128)(2,1)S(1)}, u32[]{:S(2)}, u32[]{:S(2)}) %collective-permute-start.3) | collective-permute-done | bytes 39776 | tf_op jit(solution)/shard_map/ppermute | solution.py:505
  14.1 0.1 collective-permute-start.4
  14.2 1.1 %prepare.1 = (bf16[192,192]{1,0:T(8,128)(2,1)S(1)}, bf16[192,768]{1,0:T(8,128)(2,1)S(1)}, bf16[192,768]{1,0:T(8,128)(2,1)S(1)}, bf16[138,256]{1,0:T(8,128)(2,1)S...) custom-call(bf16[8,2,4,1242]{3,2,1,0:T(4,128)(2,1)S(1)} %mine.1.refs_0_, ...), custom_call_target="tpu_custom_call" | custom-call | flops 1200000000 | bytes 1048576 | tf_op jit(solution)/shard_map/prepare/pallas_call | solution.py:472
  15.3 0.2 collective-permute-done.4.theirs
  15.6 3.5 %first.1 = (bf16[224,128]{1,0:T(8,128)(2,1)S(1)}, bf16[224,128]{1,0:T(8,128)(2,1)S(1)}, bf16[224,128]{1,0:T(8,128)(2,1)S(1)}, bf16[1152,256]{1,0:T(8,128)(2,1)S(...) custom-call(bf16[8,2,4,1242]{3,2,1,0:T(4,128)(2,1)S(1)} %mine.1.refs_0_, ...), custom_call_target="tpu_custom_call" | custom-call | flops 4499999744 | bytes 1048576 | tf_op jit(solution)/shard_map/first/pallas_call | solution.py:472
  19.1 5.6 %collective-permute-start.5 = (bf16[224,128]{1,0:T(8,128)(2,1)S(1)}, bf16[224,128]{1,0:T(8,128)(2,1)S(1)}, u32[]{:S(2)}, u32[]{:S(2)}) collective-permute-start(bf16[224,128]{1,0:T(8,128)(2,1)S(1)} %get-tuple-element.61), channel_id=1, source_target_pairs={{0,15},{1,0},{2,1},{3,2},{4,3},{5,4},{6,5},{7,6},{8,7},{9,8},{10,9... | collective-permute-start | bytes 172040 | tf_op jit(solution)/shard_map/ppermute | solution.py:497
  24.6 0.0 collective-permute-start.6
  24.6 0.4 collective-permute-start.7
  25.0 1.4 %bias.1 = (bf16[4,864,256]{2,1,0:T(8,128)(2,1)S(1)}, bf16[144,192]{1,0:T(8,128)(2,1)S(1)}) custom-call(bf16[1152,256]{1,0:T(8,128)(2,1)S(1)} %get-tuple-element.56.table, f32[2,144,256]{2,1,0:T(8,128)S(1)} %get-tuple-element.57.second_mask, bf16[2,138,768]{2,1,0:T(8,128)(2,1)S(1)} %get-tuple-element.58.columns, ...), custom_call_target="tpu_custom_call" | custom-call | flops 200000000 | bytes 1048576 | tf_op jit(solution)/shard_map/bias/pallas_call | solution.py:472
  26.4 0.1 collective-permute-done.5.from_lon
  26.5 1.8 %collective-permute-done.6.from_both = bf16[224,128]{1,0:T(8,128)(2,1)S(1)} collective-permute-done((bf16[224,128]{1,0:T(8,128)(2,1)S(1)}, bf16[224,128]{1,0:T(8,128)(2,1)S(1)}, u32[]{:S(2)}, u32[]{:S(2)}) %collective-permute-start.6) | collective-permute-done | bytes 57376 | tf_op jit(solution)/shard_map/ppermute | solution.py:497
  28.3 0.3 ready.1.given
  28.6 0.8 %collective-permute-done.7.from_lat = bf16[224,128]{1,0:T(8,128)(2,1)S(1)} collective-permute-done((bf16[224,128]{1,0:T(8,128)(2,1)S(1)}, bf16[224,128]{1,0:T(8,128)(2,1)S(1)}, u32[]{:S(2)}, u32[]{:S(2)}) %collective-permute-start.7) | collective-permute-done | bytes 57376 | tf_op jit(solution)/shard_map/ppermute | solution.py:497
  29.4 0.0 copy-start
  29.4 2.4 %second.1 = (bf16[144,192]{1,0:T(8,128)(2,1)S(1)}, bf16[224,128]{1,0:T(8,128)(2,1)S(1)}, bf16[224,128]{1,0:T(8,128)(2,1)S(1)}, bf16[224,128]{1,0:T(8,128)(2,1)S(1)}) custom-call(f32[2,576,128]{2,1,0:T(8,128)S(1)} %ready.1.given, bf16[224,128]{1,0:T(8,128)(2,1)S(1)} %collective-permute-done.7.from_lat, bf16[4,864,256]{2,1,0:T(8,128)(2,1)S(1)} %get-tuple-element.64.bias, ...), custom_call_target="tpu_custom_call" | custom-call | flops 4499999744 | bytes 1048576 | tf_op jit(solution)/shard_map/second/pallas_call | solution.py:472
  31.8 2.3 %collective-permute-start.8 = (bf16[224,128]{1,0:T(8,128)(2,1)S(1)}, bf16[224,128]{1,0:T(8,128)(2,1)S(1)}, u32[]{:S(2)}, u32[]{:S(2)}) collective-permute-start(bf16[224,128]{1,0:T(8,128)(2,1)S(1)} %get-tuple-element.69), channel_id=1, source_target_pairs={{0,17},{1,18},{2,19},{3,20},{4,21},{5,22},{6,23},{7,24},{8,25},{9,... | collective-permute-start | bytes 172040 | tf_op jit(solution)/shard_map/ppermute | solution.py:497
  34.0 0.0 collective-permute-start.9
  34.0 0.0 copy-done
  34.0 0.1 reshape.10.merge_gain
  34.1 2.5 %collective-permute-start.10 = (bf16[224,128]{1,0:T(8,128)(2,1)S(1)}, bf16[224,128]{1,0:T(8,128)(2,1)S(1)}, u32[]{:S(2)}, u32[]{:S(2)}) collective-permute-start(bf16[224,128]{1,0:T(8,128)(2,1)S(1)} %get-tuple-element.71), channel_id=1, source_target_pairs={{0,16},{1,17},{2,18},{3,19},{4,20},{5,21},{6,22},{7,23},{8,24},{9,... | collective-permute-start | bytes 172040 | tf_op jit(solution)/shard_map/ppermute | solution.py:497
  36.6 1.8 %own.1 = (bf16[144,192]{1,0:T(8,128)(2,1)S(1)}, bf16[192,768]{1,0:T(8,128)(2,1)S(1)}, bf16[192,768]{1,0:T(8,128)(2,1)S(1)}, bf16[768,384]{1,0:T(8,128)(2,1)S(1)}) custom-call(bf16[2,192,768]{2,1,0:T(8,128)(2,1)} %refs_0_.3, bf16[2,192,768]{2,1,0:T(8,128)(2,1)} %bitcast.12, bf16[768,384]{1,0:T(8,128)(2,1)} %refs_2_.3, ...), custom_call_target="tpu_custom_call" | custom-call | flops 500000000 | bytes 1048576 | tf_op jit(solution)/shard_map/own/pallas_call | solution.py:472
  38.5 0.0 collective-permute-done.8.from_both
  38.5 2.8 %collective-permute-done.9.from_lon = bf16[224,128]{1,0:T(8,128)(2,1)S(1)} collective-permute-done((bf16[224,128]{1,0:T(8,128)(2,1)S(1)}, bf16[224,128]{1,0:T(8,128)(2,1)S(1)}, u32[]{:S(2)}, u32[]{:S(2)}) %collective-permute-start.9) | collective-permute-done | bytes 57376 | tf_op jit(solution)/shard_map/ppermute | solution.py:497
  41.2 0.1 add.1.middle
  41.3 0.0 collective-permute-done.10.from_lat
  41.3 2.2 %last.1 = bf16[144,384]{1,0:T(8,128)(2,1)} custom-call(f32[2,144,128]{2,1,0:T(8,128)S(1)} %get-tuple-element.40.keep.refs_3_, bf16[432,192]{1,0:T(8,128)(2,1)S(1)} %get-tuple-element.55.far, bf16[144,192]{1,0:T(8,128)(2,1)S(1)} %get-tuple-element.68.done, f32[2,144,192]{2,1,0:T(8,128)S(1)} %add.1.middle, ...), custom_call_target="tpu_custom_call" | custom-call | flops 2000000000 | bytes 1048576 | tf_op jit(solution)/shard_map/last/pallas_call | solution.py:472
  (2 shorter events, 0.0 us)
Async XLA Ops:
  0.0 5.8 %collective-permute-start = (bf16[2,4,1242]{2,1,0:T(4,128)(2,1)}, bf16[2,4,1242]{2,1,0:T(4,128)(2,1)S(1)}, u32[]{:S(2)}, u32[]{:S(2)}) collective-permute-start(bf16[2,4,1242]{2,1,0:T(4,128)(2,1)} %bitcast.14), channel_id=1, source_target_pairs={{0,8},{1,9},{2,10},{3,11},{4,12},{5,13},{6,14},{7,15},{8,0},{9,1},... | collective-permute-start | bytes 59624 | tf_op jit(solution)/shard_map/ppermute | solution.py:505
  5.9 7.1 %collective-permute-start.1 = (bf16[2,2,4,1242]{3,2,1,0:T(4,128)(2,1)S(1)}, bf16[2,2,4,1242]{3,2,1,0:T(4,128)(2,1)S(1)}, u32[]{:S(2)}, u32[]{:S(2)}) collective-permute-start(bf16[2,2,4,1242]{3,2,1,0:T(4,128)(2,1)S(1)} %halves.1.refs_0_), channel_id=1, source_target_pairs={{0,2},{1,3},{2,4},{3,5},{4,6},{5,7},{6,0},{7,1},{8,10},{9,11},{10,... | collective-permute-start | bytes 119240 | tf_op jit(solution)/shard_map/ppermute | solution.py:505
  7.3 5.7 %collective-permute-start.2 = (bf16[2,2,4,1242]{3,2,1,0:T(4,128)(2,1)S(1)}, bf16[2,2,4,1242]{3,2,1,0:T(4,128)(2,1)S(1)}, u32[]{:S(2)}, u32[]{:S(2)}) collective-permute-start(bf16[2,2,4,1242]{3,2,1,0:T(4,128)(2,1)S(1)} %halves.1.refs_0_), channel_id=1, source_target_pairs={{0,4},{1,5},{2,6},{3,7},{4,0},{5,1},{6,2},{7,3},{8,12},{9,13},{10,... | collective-permute-start | bytes 119240 | tf_op jit(solution)/shard_map/ppermute | solution.py:505
  10.1 4.0 %collective-permute-start.3 = (bf16[2,2,4,1242]{3,2,1,0:T(4,128)(2,1)S(1)}, bf16[2,2,4,1242]{3,2,1,0:T(4,128)(2,1)S(1)}, u32[]{:S(2)}, u32[]{:S(2)}) collective-permute-start(bf16[2,2,4,1242]{3,2,1,0:T(4,128)(2,1)S(1)} %halves.1.refs_0_), channel_id=1, source_target_pairs={{0,6},{1,7},{2,0},{3,1},{4,2},{5,3},{6,4},{7,5},{8,14},{9,15},{10,... | collective-permute-start | bytes 119240 | tf_op jit(solution)/shard_map/ppermute | solution.py:505
  14.1 1.5 %collective-permute-start.4 = (bf16[8,2,4,1242]{3,2,1,0:T(4,128)(2,1)S(1)}, bf16[8,2,4,1242]{3,2,1,0:T(4,128)(2,1)S(1)}, u32[]{:S(2)}, u32[]{:S(2)}) collective-permute-start(bf16[8,2,4,1242]{3,2,1,0:T(4,128)(2,1)S(1)} %mine.1.refs_0_), channel_id=1, source_target_pairs={{0,1},{1,0},{2,3},{3,2},{4,5},{5,4},{6,7},{7,6},{8,9},{9,8},{10,11... | collective-permute-start | bytes 476936 | tf_op jit(solution)/shard_map/ppermute | solution.py:505
  19.1 7.4 %collective-permute-start.5 = (bf16[224,128]{1,0:T(8,128)(2,1)S(1)}, bf16[224,128]{1,0:T(8,128)(2,1)S(1)}, u32[]{:S(2)}, u32[]{:S(2)}) collective-permute-start(bf16[224,128]{1,0:T(8,128)(2,1)S(1)} %get-tuple-element.61), channel_id=1, source_target_pairs={{0,15},{1,0},{2,1},{3,2},{4,3},{5,4},{6,5},{7,6},{8,7},{9,8},{10,9... | collective-permute-start | bytes 172040 | tf_op jit(solution)/shard_map/ppermute | solution.py:497
  24.6 3.7 %collective-permute-start.6 = (bf16[224,128]{1,0:T(8,128)(2,1)S(1)}, bf16[224,128]{1,0:T(8,128)(2,1)S(1)}, u32[]{:S(2)}, u32[]{:S(2)}) collective-permute-start(bf16[224,128]{1,0:T(8,128)(2,1)S(1)} %get-tuple-element.62), channel_id=1, source_target_pairs={{0,113},{1,114},{2,115},{3,116},{4,117},{5,118},{6,119},{7,120},{8... | collective-permute-start | bytes 172040 | tf_op jit(solution)/shard_map/ppermute | solution.py:497
  24.6 4.8 %collective-permute-start.7 = (bf16[224,128]{1,0:T(8,128)(2,1)S(1)}, bf16[224,128]{1,0:T(8,128)(2,1)S(1)}, u32[]{:S(2)}, u32[]{:S(2)}) collective-permute-start(bf16[224,128]{1,0:T(8,128)(2,1)S(1)} %get-tuple-element.63), channel_id=1, source_target_pairs={{0,112},{1,113},{2,114},{3,115},{4,116},{5,117},{6,118},{7,119},{8... | collective-permute-start | bytes 172040 | tf_op jit(solution)/shard_map/ppermute | solution.py:497
  29.4 4.6 %copy-start = (f32[768]{0:T(1024)S(1)}, f32[768]{0:T(1024)}, u32[]{:S(2)}) copy-start(f32[768]{0:T(1024)} %param.20) | copy-start | bytes 9220
  31.8 6.7 %collective-permute-start.8 = (bf16[224,128]{1,0:T(8,128)(2,1)S(1)}, bf16[224,128]{1,0:T(8,128)(2,1)S(1)}, u32[]{:S(2)}, u32[]{:S(2)}) collective-permute-start(bf16[224,128]{1,0:T(8,128)(2,1)S(1)} %get-tuple-element.69), channel_id=1, source_target_pairs={{0,17},{1,18},{2,19},{3,20},{4,21},{5,22},{6,23},{7,24},{8,25},{9,... | collective-permute-start | bytes 172040 | tf_op jit(solution)/shard_map/ppermute | solution.py:497
  34.0 7.2 %collective-permute-start.9 = (bf16[224,128]{1,0:T(8,128)(2,1)S(1)}, bf16[224,128]{1,0:T(8,128)(2,1)S(1)}, u32[]{:S(2)}, u32[]{:S(2)}) collective-permute-start(bf16[224,128]{1,0:T(8,128)(2,1)S(1)} %get-tuple-element.70), channel_id=1, source_target_pairs={{0,1},{1,2},{2,3},{3,4},{4,5},{5,6},{6,7},{7,8},{8,9},{9,10},{10,1... | collective-permute-start | bytes 172040 | tf_op jit(solution)/shard_map/ppermute | solution.py:497
  34.1 7.2 %collective-permute-start.10 = (bf16[224,128]{1,0:T(8,128)(2,1)S(1)}, bf16[224,128]{1,0:T(8,128)(2,1)S(1)}, u32[]{:S(2)}, u32[]{:S(2)}) collective-permute-start(bf16[224,128]{1,0:T(8,128)(2,1)S(1)} %get-tuple-element.71), channel_id=1, source_target_pairs={{0,16},{1,17},{2,18},{3,19},{4,20},{5,21},{6,22},{7,23},{8,24},{9,... | collective-permute-start | bytes 172040 | tf_op jit(solution)/shard_map/ppermute | solution.py:497

commit v7 on v6

--- a/solution.py
+++ b/solution.py
@@ -394,7 +394,7 @@
     write_quarter(cells, 1 - ROW_HALF[quarter], window_half(quarter), normed.astype(F32))
 
 
-def ready_kernel(near, from_lon, from_both, gains, cells):
+def ready_kernel(near, from_both, from_lon, gains, cells):
     write_normed(cells, 0, near[...], gains)
     write_normed(cells, 2, unpack_piece(from_lon[...]), gains)
     write_normed(cells, 3, unpack_piece(from_both[...]), gains)
@@ -588,7 +588,7 @@
         [pltpu.VMEM((768, 768), F32), pltpu.VMEM((768, 768), F32)],
         tables, second_mask, columns, rows, inputs, attended, gains, fc1_0, fc2_0, keep,
     )
-    ready = call(ready_kernel, "ready", 0.4, cell_rows, [], near, from_lon, from_both, gains)
+    ready = call(ready_kernel, "ready", 0.4, cell_rows, [], near, from_both, from_lon, gains)
     own, to_lat, to_lon, to_both = call(
         second_kernel,
         "second",

time: 43.7 us -> 47 us (1.076)
  the two profiles are of different devices: /device:TPU:24 before, /device:TPU:7 now
where the time goes in v7:
time: 47 us; the launch traced here: 46.8 us
  starting transfers between devices  19.5 us (41%)
  Pallas kernels  15.5 us (33%)
  waiting for transfers between devices  11.5 us (24%)
    pallas_call x12, Pallas kernels, call(): pl.pallas_call(kernel, name=name, out_shape=outs, in_specs=in_specs or [V...  15.5 us
    ppermute x6, starting transfers between devices, sent(): return lax.ppermute(block, ('lat', 'lon'), route)  10.3 us
    ppermute x5, starting transfers between devices, turned(): return lax.ppermute(block, 'lon', route)  9.27 us
    ppermute x6, waiting for transfers between devices, sent(): return lax.ppermute(block, ('lat', 'lon'), route)  8.8 us
    ppermute x5, waiting for transfers between devices, turned(): return lax.ppermute(block, 'lon', route)  2.74 us
  transfers between devices with their start and end apart: 11, of which 5 were waited for; matrix products, arithmetic and copies ran while one was open for 0% of the time, Pallas kernels for 16%

profile of v7, /device:TPU:7, one launch (start us, length us, event | category | flops | bytes accessed | tf_op | source)
XLA Modules:
  0.0 46.8 jit_solution(7382380920615281721)
XLA Ops:
  0.0 3.6 %collective-permute-start = (bf16[2,4,1242]{2,1,0:T(4,128)(2,1)}, bf16[2,4,1242]{2,1,0:T(4,128)(2,1)S(1)}, u32[]{:S(2)}, u32[]{:S(2)}) collective-permute-start(bf16[2,4,1242]{2,1,0:T(4,128)(2,1)} %bitcast.14), channel_id=1, source_target_pairs={{0,8},{1,9},{2,10},{3,11},{4,12},{5,13},{6,14},{7,15},{8,0},{9,1},... | collective-permute-start | bytes 59624 | tf_op jit(solution)/shard_map/ppermute | solution.py:505
  3.6 1.2 %fetch.1 = (bf16[1,2,4,1242]{3,2,1,0:T(4,128)(2,1)S(1)}, bf16[576,192]{1,0:T(8,128)(2,1)S(1)}, f32[2,2,192]{2,1,0:T(2,128)S(1)}, bf16[192,576]{1,0:T(8,128)(2,1)...) custom-call(s32[48]{0:T(128)} %refs_0_.2, ...), custom_call_target="tpu_custom_call" | custom-call | flops 1400000000 | bytes 1048576 | tf_op jit(solution)/shard_map/fetch/pallas_call | solution.py:472
  4.8 0.2 collective-permute-done
  5.0 0.2 collective-permute-start.1
  5.2 2.1 %collective-permute-start.2 = (bf16[2,2,4,1242]{3,2,1,0:T(4,128)(2,1)S(1)}, bf16[2,2,4,1242]{3,2,1,0:T(4,128)(2,1)S(1)}, u32[]{:S(2)}, u32[]{:S(2)}) collective-permute-start(bf16[2,2,4,1242]{3,2,1,0:T(4,128)(2,1)S(1)} %halves.1.refs_0_), channel_id=1, source_target_pairs={{0,4},{1,5},{2,6},{3,7},{4,0},{5,1},{6,2},{7,3},{8,12},{9,13},{10,... | collective-permute-start | bytes 119240 | tf_op jit(solution)/shard_map/ppermute | solution.py:505
  7.3 0.0 collective-permute-start.3
  7.3 1.5 %before.1 = (f32[4,864,256]{2,1,0:T(8,128)S(1)}, bf16[4,256,256]{2,1,0:T(8,128)(2,1)S(1)}, f32[2,576,128]{2,1,0:T(8,128)S(1)}, bf16[192,576]{1,0:T(8,128)(2,1)S(1)}, bf16[192,192]{1,0:T(8,128)(2,1)S(1)}) custom-call(bf16[2,2,4,1242]{3,2,1,0:T(4,128)(2,1)S(1)} %halves.1.refs_0_, bf16[576,192]{1,0:T(8,128)(2,1)S(1)} %get-tuple-element.42.refs_1_, ...), custom_call_target="tpu_custom_call" | custom-call | flops 2500000000 | bytes 1048576 | tf_op jit(solution)/shard_map/before/pallas_call | solution.py:472
  8.8 0.0 collective-permute-done.1.refs_1_
  8.8 0.7 %collective-permute-done.2.refs_2_ = bf16[2,2,4,1242]{3,2,1,0:T(4,128)(2,1)S(1)} collective-permute-done((bf16[2,2,4,1242]{3,2,1,0:T(4,128)(2,1)S(1)}, bf16[2,2,4,1242]{3,2,1,0:T(4,128)(2,1)S(1)}, u32[]{:S(2)}, u32[]{:S(2)}) %collective-permute-start.2) | collective-permute-done | bytes 39776 | tf_op jit(solution)/shard_map/ppermute | solution.py:505
  9.5 1.8 %collective-permute-done.3.refs_3_ = bf16[2,2,4,1242]{3,2,1,0:T(4,128)(2,1)S(1)} collective-permute-done((bf16[2,2,4,1242]{3,2,1,0:T(4,128)(2,1)S(1)}, bf16[2,2,4,1242]{3,2,1,0:T(4,128)(2,1)S(1)}, u32[]{:S(2)}, u32[]{:S(2)}) %collective-permute-start.3) | collective-permute-done | bytes 39776 | tf_op jit(solution)/shard_map/ppermute | solution.py:505
  11.4 3.3 %collective-permute-start.4 = (bf16[8,2,4,1242]{3,2,1,0:T(4,128)(2,1)S(1)}, bf16[8,2,4,1242]{3,2,1,0:T(4,128)(2,1)S(1)}, u32[]{:S(2)}, u32[]{:S(2)}) collective-permute-start(bf16[8,2,4,1242]{3,2,1,0:T(4,128)(2,1)S(1)} %mine.1.refs_0_), channel_id=1, source_target_pairs={{0,1},{1,0},{2,3},{3,2},{4,5},{5,4},{6,7},{7,6},{8,9},{9,8},{10,11... | collective-permute-start | bytes 476936 | tf_op jit(solution)/shard_map/ppermute | solution.py:505
  14.7 1.1 %prepare.1 = (bf16[192,192]{1,0:T(8,128)(2,1)S(1)}, bf16[192,768]{1,0:T(8,128)(2,1)S(1)}, bf16[192,768]{1,0:T(8,128)(2,1)S(1)}, bf16[138,256]{1,0:T(8,128)(2,1)S...) custom-call(bf16[8,2,4,1242]{3,2,1,0:T(4,128)(2,1)S(1)} %mine.1.refs_0_, ...), custom_call_target="tpu_custom_call" | custom-call | flops 1200000000 | bytes 1048576 | tf_op jit(solution)/shard_map/prepare/pallas_call | solution.py:472
  15.9 0.0 collective-permute-done.4.theirs
  15.9 3.5 %first.1 = (bf16[224,128]{1,0:T(8,128)(2,1)S(1)}, bf16[224,128]{1,0:T(8,128)(2,1)S(1)}, bf16[224,128]{1,0:T(8,128)(2,1)S(1)}, bf16[1152,256]{1,0:T(8,128)(2,1)S(...) custom-call(bf16[8,2,4,1242]{3,2,1,0:T(4,128)(2,1)S(1)} %mine.1.refs_0_, ...), custom_call_target="tpu_custom_call" | custom-call | flops 4499999744 | bytes 1048576 | tf_op jit(solution)/shard_map/first/pallas_call | solution.py:472
  19.4 6.1 %collective-permute-start.5 = (bf16[224,128]{1,0:T(8,128)(2,1)S(1)}, bf16[224,128]{1,0:T(8,128)(2,1)S(1)}, u32[]{:S(2)}, u32[]{:S(2)}) collective-permute-start(bf16[224,128]{1,0:T(8,128)(2,1)S(1)} %get-tuple-element.61), channel_id=1, source_target_pairs={{0,113},{1,114},{2,115},{3,116},{4,117},{5,118},{6,119},{7,120},{8... | collective-permute-start | bytes 172040 | tf_op jit(solution)/shard_map/ppermute | solution.py:497
  25.5 0.0 collective-permute-start.6
  25.5 2.1 %collective-permute-start.7 = (bf16[224,128]{1,0:T(8,128)(2,1)S(1)}, bf16[224,128]{1,0:T(8,128)(2,1)S(1)}, u32[]{:S(2)}, u32[]{:S(2)}) collective-permute-start(bf16[224,128]{1,0:T(8,128)(2,1)S(1)} %get-tuple-element.63), channel_id=1, source_target_pairs={{0,112},{1,113},{2,114},{3,115},{4,116},{5,117},{6,118},{7,119},{8... | collective-permute-start | bytes 172040 | tf_op jit(solution)/shard_map/ppermute | solution.py:497
  27.6 1.4 %bias.1 = (bf16[4,864,256]{2,1,0:T(8,128)(2,1)S(1)}, bf16[144,192]{1,0:T(8,128)(2,1)S(1)}) custom-call(bf16[1152,256]{1,0:T(8,128)(2,1)S(1)} %get-tuple-element.56.table, f32[2,144,256]{2,1,0:T(8,128)S(1)} %get-tuple-element.57.second_mask, bf16[2,138,768]{2,1,0:T(8,128)(2,1)S(1)} %get-tuple-element.58.columns, ...), custom_call_target="tpu_custom_call" | custom-call | flops 200000000 | bytes 1048576 | tf_op jit(solution)/shard_map/bias/pallas_call | solution.py:472
  29.0 0.0 collective-permute-done.5.from_both
  29.0 3.7 %collective-permute-done.6.from_lon = bf16[224,128]{1,0:T(8,128)(2,1)S(1)} collective-permute-done((bf16[224,128]{1,0:T(8,128)(2,1)S(1)}, bf16[224,128]{1,0:T(8,128)(2,1)S(1)}, u32[]{:S(2)}, u32[]{:S(2)}) %collective-permute-start.6) | collective-permute-done | bytes 57376 | tf_op jit(solution)/shard_map/ppermute | solution.py:497
  32.7 0.3 ready.1.given
  33.0 0.0 collective-permute-done.7.from_lat
  33.0 0.0 copy-start
  33.0 2.4 %second.1 = (bf16[144,192]{1,0:T(8,128)(2,1)S(1)}, bf16[224,128]{1,0:T(8,128)(2,1)S(1)}, bf16[224,128]{1,0:T(8,128)(2,1)S(1)}, bf16[224,128]{1,0:T(8,128)(2,1)S(1)}) custom-call(f32[2,576,128]{2,1,0:T(8,128)S(1)} %ready.1.given, bf16[224,128]{1,0:T(8,128)(2,1)S(1)} %collective-permute-done.7.from_lat, bf16[4,864,256]{2,1,0:T(8,128)(2,1)S(1)} %get-tuple-element.64.bias, ...), custom_call_target="tpu_custom_call" | custom-call | flops 4499999744 | bytes 1048576 | tf_op jit(solution)/shard_map/second/pallas_call | solution.py:472
  35.4 0.2 collective-permute-start.8
  35.6 1.9 %collective-permute-start.9 = (bf16[224,128]{1,0:T(8,128)(2,1)S(1)}, bf16[224,128]{1,0:T(8,128)(2,1)S(1)}, u32[]{:S(2)}, u32[]{:S(2)}) collective-permute-start(bf16[224,128]{1,0:T(8,128)(2,1)S(1)} %get-tuple-element.70), channel_id=1, source_target_pairs={{0,1},{1,2},{2,3},{3,4},{4,5},{5,6},{6,7},{7,8},{8,9},{9,10},{10,1... | collective-permute-start | bytes 172040 | tf_op jit(solution)/shard_map/ppermute | solution.py:497
  37.5 0.0 copy-done
  37.5 0.1 reshape.10.merge_gain
  37.6 0.0 collective-permute-start.10
  37.6 1.8 %own.1 = (bf16[144,192]{1,0:T(8,128)(2,1)S(1)}, bf16[192,768]{1,0:T(8,128)(2,1)S(1)}, bf16[192,768]{1,0:T(8,128)(2,1)S(1)}, bf16[768,384]{1,0:T(8,128)(2,1)S(1)}) custom-call(bf16[2,192,768]{2,1,0:T(8,128)(2,1)} %refs_0_.3, bf16[2,192,768]{2,1,0:T(8,128)(2,1)} %bitcast.12, bf16[768,384]{1,0:T(8,128)(2,1)} %refs_2_.3, ...), custom_call_target="tpu_custom_call" | custom-call | flops 500000000 | bytes 1048576 | tf_op jit(solution)/shard_map/own/pallas_call | solution.py:472
  39.4 5.1 %collective-permute-done.8.from_both = bf16[224,128]{1,0:T(8,128)(2,1)S(1)} collective-permute-done((bf16[224,128]{1,0:T(8,128)(2,1)S(1)}, bf16[224,128]{1,0:T(8,128)(2,1)S(1)}, u32[]{:S(2)}, u32[]{:S(2)}) %collective-permute-start.8) | collective-permute-done | bytes 57376 | tf_op jit(solution)/shard_map/ppermute | solution.py:497
  44.5 0.0 collective-permute-done.9.from_lon
  44.5 0.1 add.1.middle
  44.6 0.0 collective-permute-done.10.from_lat
  44.6 2.2 %last.1 = bf16[144,384]{1,0:T(8,128)(2,1)} custom-call(f32[2,144,128]{2,1,0:T(8,128)S(1)} %get-tuple-element.40.keep.refs_3_, bf16[432,192]{1,0:T(8,128)(2,1)S(1)} %get-tuple-element.55.far, bf16[144,192]{1,0:T(8,128)(2,1)S(1)} %get-tuple-element.68.done, f32[2,144,192]{2,1,0:T(8,128)S(1)} %add.1.middle, ...), custom_call_target="tpu_custom_call" | custom-call | flops 2000000000 | bytes 1048576 | tf_op jit(solution)/shard_map/last/pallas_call | solution.py:472
  (2 shorter events, 0.0 us)
Async XLA Ops:
  0.0 5.0 %collective-permute-start = (bf16[2,4,1242]{2,1,0:T(4,128)(2,1)}, bf16[2,4,1242]{2,1,0:T(4,128)(2,1)S(1)}, u32[]{:S(2)}, u32[]{:S(2)}) collective-permute-start(bf16[2,4,1242]{2,1,0:T(4,128)(2,1)} %bitcast.14), channel_id=1, source_target_pairs={{0,8},{1,9},{2,10},{3,11},{4,12},{5,13},{6,14},{7,15},{8,0},{9,1},... | collective-permute-start | bytes 59624 | tf_op jit(solution)/shard_map/ppermute | solution.py:505
  5.0 3.8 %collective-permute-start.1 = (bf16[2,2,4,1242]{3,2,1,0:T(4,128)(2,1)S(1)}, bf16[2,2,4,1242]{3,2,1,0:T(4,128)(2,1)S(1)}, u32[]{:S(2)}, u32[]{:S(2)}) collective-permute-start(bf16[2,2,4,1242]{3,2,1,0:T(4,128)(2,1)S(1)} %halves.1.refs_0_), channel_id=1, source_target_pairs={{0,2},{1,3},{2,4},{3,5},{4,6},{5,7},{6,0},{7,1},{8,10},{9,11},{10,... | collective-permute-start | bytes 119240 | tf_op jit(solution)/shard_map/ppermute | solution.py:505
  5.2 4.4 %collective-permute-start.2 = (bf16[2,2,4,1242]{3,2,1,0:T(4,128)(2,1)S(1)}, bf16[2,2,4,1242]{3,2,1,0:T(4,128)(2,1)S(1)}, u32[]{:S(2)}, u32[]{:S(2)}) collective-permute-start(bf16[2,2,4,1242]{3,2,1,0:T(4,128)(2,1)S(1)} %halves.1.refs_0_), channel_id=1, source_target_pairs={{0,4},{1,5},{2,6},{3,7},{4,0},{5,1},{6,2},{7,3},{8,12},{9,13},{10,... | collective-permute-start | bytes 119240 | tf_op jit(solution)/shard_map/ppermute | solution.py:505
  7.3 4.1 %collective-permute-start.3 = (bf16[2,2,4,1242]{3,2,1,0:T(4,128)(2,1)S(1)}, bf16[2,2,4,1242]{3,2,1,0:T(4,128)(2,1)S(1)}, u32[]{:S(2)}, u32[]{:S(2)}) collective-permute-start(bf16[2,2,4,1242]{3,2,1,0:T(4,128)(2,1)S(1)} %halves.1.refs_0_), channel_id=1, source_target_pairs={{0,6},{1,7},{2,0},{3,1},{4,2},{5,3},{6,4},{7,5},{8,14},{9,15},{10,... | collective-permute-start | bytes 119240 | tf_op jit(solution)/shard_map/ppermute | solution.py:505
  11.4 4.5 %collective-permute-start.4 = (bf16[8,2,4,1242]{3,2,1,0:T(4,128)(2,1)S(1)}, bf16[8,2,4,1242]{3,2,1,0:T(4,128)(2,1)S(1)}, u32[]{:S(2)}, u32[]{:S(2)}) collective-permute-start(bf16[8,2,4,1242]{3,2,1,0:T(4,128)(2,1)S(1)} %mine.1.refs_0_), channel_id=1, source_target_pairs={{0,1},{1,0},{2,3},{3,2},{4,5},{5,4},{6,7},{7,6},{8,9},{9,8},{10,11... | collective-permute-start | bytes 476936 | tf_op jit(solution)/shard_map/ppermute | solution.py:505
  19.4 9.5 %collective-permute-start.5 = (bf16[224,128]{1,0:T(8,128)(2,1)S(1)}, bf16[224,128]{1,0:T(8,128)(2,1)S(1)}, u32[]{:S(2)}, u32[]{:S(2)}) collective-permute-start(bf16[224,128]{1,0:T(8,128)(2,1)S(1)} %get-tuple-element.61), channel_id=1, source_target_pairs={{0,113},{1,114},{2,115},{3,116},{4,117},{5,118},{6,119},{7,120},{8... | collective-permute-start | bytes 172040 | tf_op jit(solution)/shard_map/ppermute | solution.py:497
  25.5 7.2 %collective-permute-start.6 = (bf16[224,128]{1,0:T(8,128)(2,1)S(1)}, bf16[224,128]{1,0:T(8,128)(2,1)S(1)}, u32[]{:S(2)}, u32[]{:S(2)}) collective-permute-start(bf16[224,128]{1,0:T(8,128)(2,1)S(1)} %get-tuple-element.62), channel_id=1, source_target_pairs={{0,15},{1,0},{2,1},{3,2},{4,3},{5,4},{6,5},{7,6},{8,7},{9,8},{10,9... | collective-permute-start | bytes 172040 | tf_op jit(solution)/shard_map/ppermute | solution.py:497
  25.5 7.6 %collective-permute-start.7 = (bf16[224,128]{1,0:T(8,128)(2,1)S(1)}, bf16[224,128]{1,0:T(8,128)(2,1)S(1)}, u32[]{:S(2)}, u32[]{:S(2)}) collective-permute-start(bf16[224,128]{1,0:T(8,128)(2,1)S(1)} %get-tuple-element.63), channel_id=1, source_target_pairs={{0,112},{1,113},{2,114},{3,115},{4,116},{5,117},{6,118},{7,119},{8... | collective-permute-start | bytes 172040 | tf_op jit(solution)/shard_map/ppermute | solution.py:497
  33.0 4.5 %copy-start = (f32[768]{0:T(1024)S(1)}, f32[768]{0:T(1024)}, u32[]{:S(2)}) copy-start(f32[768]{0:T(1024)} %param.20) | copy-start | bytes 9220
  35.4 9.1 %collective-permute-start.8 = (bf16[224,128]{1,0:T(8,128)(2,1)S(1)}, bf16[224,128]{1,0:T(8,128)(2,1)S(1)}, u32[]{:S(2)}, u32[]{:S(2)}) collective-permute-start(bf16[224,128]{1,0:T(8,128)(2,1)S(1)} %get-tuple-element.69), channel_id=1, source_target_pairs={{0,17},{1,18},{2,19},{3,20},{4,21},{5,22},{6,23},{7,24},{8,25},{9,... | collective-permute-start | bytes 172040 | tf_op jit(solution)/shard_map/ppermute | solution.py:497
  35.6 8.9 %collective-permute-start.9 = (bf16[224,128]{1,0:T(8,128)(2,1)S(1)}, bf16[224,128]{1,0:T(8,128)(2,1)S(1)}, u32[]{:S(2)}, u32[]{:S(2)}) collective-permute-start(bf16[224,128]{1,0:T(8,128)(2,1)S(1)} %get-tuple-element.70), channel_id=1, source_target_pairs={{0,1},{1,2},{2,3},{3,4},{4,5},{5,6},{6,7},{7,8},{8,9},{9,10},{10,1... | collective-permute-start | bytes 172040 | tf_op jit(solution)/shard_map/ppermute | solution.py:497
  37.6 7.0 %collective-permute-start.10 = (bf16[224,128]{1,0:T(8,128)(2,1)S(1)}, bf16[224,128]{1,0:T(8,128)(2,1)S(1)}, u32[]{:S(2)}, u32[]{:S(2)}) collective-permute-start(bf16[224,128]{1,0:T(8,128)(2,1)S(1)} %get-tuple-element.71), channel_id=1, source_target_pairs={{0,16},{1,17},{2,18},{3,19},{4,20},{5,21},{6,22},{7,23},{8,24},{9,... | collective-permute-start | bytes 172040 | tf_op jit(solution)/shard_map/ppermute | solution.py:497

commit v8 on v6

--- a/solution.py
+++ b/solution.py
@@ -427,16 +427,19 @@
     result[...] = feed_forward(middle, gains[1, 1:2], refs[0][...], refs[1][...], keep[1][:, :1] > 0)
 
 
-def add_kernel(far, from_both, from_lon, middle):
+def add_kernel(keep, far, from_both, from_lon, gains, fc1, fc2, done):
+    middle = []
     for at, piece in enumerate((from_lon, from_both)):
         inputs = far[(at + 1) * TOKENS : (at + 2) * TOKENS].astype(F32)
-        middle[at] = inputs + unpack_piece(piece[...]).astype(F32)
+        middle.append(inputs + unpack_piece(piece[...]).astype(F32))
+    done[...] = finished((2, 3), middle, gains[1, 1:2], fc1, fc2, keep)
 
 
 def last_kernel(keep, far, done, middle, from_lat, gains, fc1, fc2, merge_gain, merge_weight, merged):
     upper = far[:TOKENS].astype(F32) + unpack_piece(from_lat[...]).astype(F32)
-    fresh = finished((1, 2, 3), [upper, middle[0], middle[1]], gains[1, 1:2], fc1, fc2, keep).astype(F32)
-    results = [done[...].astype(F32)] + [fresh[at * TOKENS : (at + 1) * TOKENS] for at in range(3)]
+    fresh = finished((1,), [upper], gains[1, 1:2], fc1, fc2, keep).astype(F32)
+    others = middle[...].astype(F32)
+    results = [done[...].astype(F32), fresh, others[:TOKENS], others[TOKENS:]]
     odd = lax.rem(lax.axis_index("lat"), 2) == 1
     groups = {}
     for qr, (first, second) in enumerate(((1, 3), (0, 2))):
@@ -608,7 +611,7 @@
         in_specs=[hbm_spec] * 3 + [VMEM_SPEC] * 4,
     )
     middle = call(
-        add_kernel, "add", 0.2, shape(2, TOKENS, C, dtype=F32), [], far, from_both, from_lon
+        add_kernel, "add", 0.7, shape(2 * TOKENS, C), [], keep, far, from_both, from_lon, gains, fc1_1, fc2_1
     )
     merged = call(
         last_kernel,

time: 43.7 us -> 44 us (level)
  transfers between devices with their start and end apart: 11 -> 11, of which waited for: 7 -> 7; matrix products, arithmetic and copies ran while one was open for 0% -> 0% of each run, Pallas kernels for 17% -> 18%
where the time goes in v8:
time: 44 us; the launch traced here: 43.8 us
  starting transfers between devices  20.3 us (46%)
  Pallas kernels  15.8 us (36%)
  waiting for transfers between devices  7.53 us (17%)
    pallas_call x12, Pallas kernels, call(): pl.pallas_call(kernel, name=name, out_shape=outs, in_specs=in_specs or [V...  15.8 us
    ppermute x6, starting transfers between devices, sent(): return lax.ppermute(block, ('lat', 'lon'), route)  10.7 us
    ppermute x5, starting transfers between devices, turned(): return lax.ppermute(block, 'lon', route)  9.62 us
    ppermute x6, waiting for transfers between devices, sent(): return lax.ppermute(block, ('lat', 'lon'), route)  5.46 us
    ppermute x5, waiting for transfers between devices, turned(): return lax.ppermute(block, 'lon', route)  2.07 us
  transfers between devices with their start and end apart: 11, of which 7 were waited for; matrix products, arithmetic and copies ran while one was open for 0% of the time, Pallas kernels for 18%

profile of v8, /device:TPU:24, one launch (start us, length us, event | category | flops | bytes accessed | tf_op | source)
XLA Modules:
  0.0 43.8 jit_solution(12844400996583250096)
XLA Ops:
  0.0 3.9 %collective-permute-start = (bf16[2,4,1242]{2,1,0:T(4,128)(2,1)}, bf16[2,4,1242]{2,1,0:T(4,128)(2,1)S(1)}, u32[]{:S(2)}, u32[]{:S(2)}) collective-permute-start(bf16[2,4,1242]{2,1,0:T(4,128)(2,1)} %bitcast.14), channel_id=1, source_target_pairs={{0,8},{1,9},{2,10},{3,11},{4,12},{5,13},{6,14},{7,15},{8,0},{9,1},... | collective-permute-start | bytes 59624 | tf_op jit(solution)/shard_map/ppermute | solution.py:508
  3.9 1.2 %fetch.1 = (bf16[1,2,4,1242]{3,2,1,0:T(4,128)(2,1)S(1)}, bf16[576,192]{1,0:T(8,128)(2,1)S(1)}, f32[2,2,192]{2,1,0:T(2,128)S(1)}, bf16[192,576]{1,0:T(8,128)(2,1)...) custom-call(s32[48]{0:T(128)} %refs_0_.2, ...), custom_call_target="tpu_custom_call" | custom-call | flops 1400000000 | bytes 1048576 | tf_op jit(solution)/shard_map/fetch/pallas_call | solution.py:475
  5.1 0.8 %collective-permute-done = bf16[2,4,1242]{2,1,0:T(4,128)(2,1)S(1)} collective-permute-done((bf16[2,4,1242]{2,1,0:T(4,128)(2,1)}, bf16[2,4,1242]{2,1,0:T(4,128)(2,1)S(1)}, u32[]{:S(2)}, u32[]{:S(2)}) %collective-permute-start) | collective-permute-done | bytes 19904 | tf_op jit(solution)/shard_map/ppermute | solution.py:508
  5.9 1.5 %collective-permute-start.1 = (bf16[2,2,4,1242]{3,2,1,0:T(4,128)(2,1)S(1)}, bf16[2,2,4,1242]{3,2,1,0:T(4,128)(2,1)S(1)}, u32[]{:S(2)}, u32[]{:S(2)}) collective-permute-start(bf16[2,2,4,1242]{3,2,1,0:T(4,128)(2,1)S(1)} %halves.1.refs_0_), channel_id=1, source_target_pairs={{0,2},{1,3},{2,4},{3,5},{4,6},{5,7},{6,0},{7,1},{8,10},{9,11},{10,... | collective-permute-start | bytes 119240 | tf_op jit(solution)/shard_map/ppermute | solution.py:508
  7.3 2.7 %collective-permute-start.2 = (bf16[2,2,4,1242]{3,2,1,0:T(4,128)(2,1)S(1)}, bf16[2,2,4,1242]{3,2,1,0:T(4,128)(2,1)S(1)}, u32[]{:S(2)}, u32[]{:S(2)}) collective-permute-start(bf16[2,2,4,1242]{3,2,1,0:T(4,128)(2,1)S(1)} %halves.1.refs_0_), channel_id=1, source_target_pairs={{0,4},{1,5},{2,6},{3,7},{4,0},{5,1},{6,2},{7,3},{8,12},{9,13},{10,... | collective-permute-start | bytes 119240 | tf_op jit(solution)/shard_map/ppermute | solution.py:508
  10.1 1.4 %collective-permute-start.3 = (bf16[2,2,4,1242]{3,2,1,0:T(4,128)(2,1)S(1)}, bf16[2,2,4,1242]{3,2,1,0:T(4,128)(2,1)S(1)}, u32[]{:S(2)}, u32[]{:S(2)}) collective-permute-start(bf16[2,2,4,1242]{3,2,1,0:T(4,128)(2,1)S(1)} %halves.1.refs_0_), channel_id=1, source_target_pairs={{0,6},{1,7},{2,0},{3,1},{4,2},{5,3},{6,4},{7,5},{8,14},{9,15},{10,... | collective-permute-start | bytes 119240 | tf_op jit(solution)/shard_map/ppermute | solution.py:508
  11.5 1.5 %before.1 = (f32[4,864,256]{2,1,0:T(8,128)S(1)}, bf16[4,256,256]{2,1,0:T(8,128)(2,1)S(1)}, f32[2,576,128]{2,1,0:T(8,128)S(1)}, bf16[192,576]{1,0:T(8,128)(2,1)S(1)}, bf16[192,192]{1,0:T(8,128)(2,1)S(1)}) custom-call(bf16[2,2,4,1242]{3,2,1,0:T(4,128)(2,1)S(1)} %halves.1.refs_0_, bf16[576,192]{1,0:T(8,128)(2,1)S(1)} %get-tuple-element.42.refs_1_, ...), custom_call_target="tpu_custom_call" | custom-call | flops 2500000000 | bytes 1048576 | tf_op jit(solution)/shard_map/before/pallas_call | solution.py:475
  13.0 0.0 collective-permute-done.1.refs_1_
  13.0 0.0 collective-permute-done.2.refs_2_
  13.0 1.1 %collective-permute-done.3.refs_3_ = bf16[2,2,4,1242]{3,2,1,0:T(4,128)(2,1)S(1)} collective-permute-done((bf16[2,2,4,1242]{3,2,1,0:T(4,128)(2,1)S(1)}, bf16[2,2,4,1242]{3,2,1,0:T(4,128)(2,1)S(1)}, u32[]{:S(2)}, u32[]{:S(2)}) %collective-permute-start.3) | collective-permute-done | bytes 39776 | tf_op jit(solution)/shard_map/ppermute | solution.py:508
  14.1 0.1 collective-permute-start.4
  14.2 1.1 %prepare.1 = (bf16[192,192]{1,0:T(8,128)(2,1)S(1)}, bf16[192,768]{1,0:T(8,128)(2,1)S(1)}, bf16[192,768]{1,0:T(8,128)(2,1)S(1)}, bf16[138,256]{1,0:T(8,128)(2,1)S...) custom-call(bf16[8,2,4,1242]{3,2,1,0:T(4,128)(2,1)S(1)} %mine.1.refs_0_, ...), custom_call_target="tpu_custom_call" | custom-call | flops 1200000000 | bytes 1048576 | tf_op jit(solution)/shard_map/prepare/pallas_call | solution.py:475
  15.3 0.2 collective-permute-done.4.theirs
  15.6 3.5 %first.1 = (bf16[224,128]{1,0:T(8,128)(2,1)S(1)}, bf16[224,128]{1,0:T(8,128)(2,1)S(1)}, bf16[224,128]{1,0:T(8,128)(2,1)S(1)}, bf16[1152,256]{1,0:T(8,128)(2,1)S(...) custom-call(bf16[8,2,4,1242]{3,2,1,0:T(4,128)(2,1)S(1)} %mine.1.refs_0_, ...), custom_call_target="tpu_custom_call" | custom-call | flops 4499999744 | bytes 1048576 | tf_op jit(solution)/shard_map/first/pallas_call | solution.py:475
  19.1 5.6 %collective-permute-start.5 = (bf16[224,128]{1,0:T(8,128)(2,1)S(1)}, bf16[224,128]{1,0:T(8,128)(2,1)S(1)}, u32[]{:S(2)}, u32[]{:S(2)}) collective-permute-start(bf16[224,128]{1,0:T(8,128)(2,1)S(1)} %get-tuple-element.61), channel_id=1, source_target_pairs={{0,15},{1,0},{2,1},{3,2},{4,3},{5,4},{6,5},{7,6},{8,7},{9,8},{10,9... | collective-permute-start | bytes 172040 | tf_op jit(solution)/shard_map/ppermute | solution.py:500
  24.6 0.0 collective-permute-start.6
  24.6 0.4 collective-permute-start.7
  25.0 1.4 %bias.1 = (bf16[4,864,256]{2,1,0:T(8,128)(2,1)S(1)}, bf16[144,192]{1,0:T(8,128)(2,1)S(1)}) custom-call(bf16[1152,256]{1,0:T(8,128)(2,1)S(1)} %get-tuple-element.56.table, f32[2,144,256]{2,1,0:T(8,128)S(1)} %get-tuple-element.57.second_mask, bf16[2,138,768]{2,1,0:T(8,128)(2,1)S(1)} %get-tuple-element.58.columns, ...), custom_call_target="tpu_custom_call" | custom-call | flops 200000000 | bytes 1048576 | tf_op jit(solution)/shard_map/bias/pallas_call | solution.py:475
  26.4 0.1 collective-permute-done.5.from_lon
  26.5 1.8 %collective-permute-done.6.from_both = bf16[224,128]{1,0:T(8,128)(2,1)S(1)} collective-permute-done((bf16[224,128]{1,0:T(8,128)(2,1)S(1)}, bf16[224,128]{1,0:T(8,128)(2,1)S(1)}, u32[]{:S(2)}, u32[]{:S(2)}) %collective-permute-start.6) | collective-permute-done | bytes 57376 | tf_op jit(solution)/shard_map/ppermute | solution.py:500
  28.3 0.3 ready.1.given
  28.6 0.8 %collective-permute-done.7.from_lat = bf16[224,128]{1,0:T(8,128)(2,1)S(1)} collective-permute-done((bf16[224,128]{1,0:T(8,128)(2,1)S(1)}, bf16[224,128]{1,0:T(8,128)(2,1)S(1)}, u32[]{:S(2)}, u32[]{:S(2)}) %collective-permute-start.7) | collective-permute-done | bytes 57376 | tf_op jit(solution)/shard_map/ppermute | solution.py:500
  29.4 0.0 copy-start
  29.4 2.4 %second.1 = (bf16[144,192]{1,0:T(8,128)(2,1)S(1)}, bf16[224,128]{1,0:T(8,128)(2,1)S(1)}, bf16[224,128]{1,0:T(8,128)(2,1)S(1)}, bf16[224,128]{1,0:T(8,128)(2,1)S(1)}) custom-call(f32[2,576,128]{2,1,0:T(8,128)S(1)} %ready.1.given, bf16[224,128]{1,0:T(8,128)(2,1)S(1)} %collective-permute-done.7.from_lat, bf16[4,864,256]{2,1,0:T(8,128)(2,1)S(1)} %get-tuple-element.64.bias, ...), custom_call_target="tpu_custom_call" | custom-call | flops 4499999744 | bytes 1048576 | tf_op jit(solution)/shard_map/second/pallas_call | solution.py:475
  31.8 2.3 %collective-permute-start.8 = (bf16[224,128]{1,0:T(8,128)(2,1)S(1)}, bf16[224,128]{1,0:T(8,128)(2,1)S(1)}, u32[]{:S(2)}, u32[]{:S(2)}) collective-permute-start(bf16[224,128]{1,0:T(8,128)(2,1)S(1)} %get-tuple-element.69), channel_id=1, source_target_pairs={{0,17},{1,18},{2,19},{3,20},{4,21},{5,22},{6,23},{7,24},{8,25},{9,... | collective-permute-start | bytes 172040 | tf_op jit(solution)/shard_map/ppermute | solution.py:500
  34.0 0.0 collective-permute-start.9
  34.0 0.0 copy-done
  34.0 0.1 reshape.10.merge_gain
  34.1 2.5 %collective-permute-start.10 = (bf16[224,128]{1,0:T(8,128)(2,1)S(1)}, bf16[224,128]{1,0:T(8,128)(2,1)S(1)}, u32[]{:S(2)}, u32[]{:S(2)}) collective-permute-start(bf16[224,128]{1,0:T(8,128)(2,1)S(1)} %get-tuple-element.73), channel_id=1, source_target_pairs={{0,16},{1,17},{2,18},{3,19},{4,20},{5,21},{6,22},{7,23},{8,24},{9,... | collective-permute-start | bytes 172040 | tf_op jit(solution)/shard_map/ppermute | solution.py:500
  36.6 1.8 %own.1 = (bf16[144,192]{1,0:T(8,128)(2,1)S(1)}, bf16[192,768]{1,0:T(8,128)(2,1)S(1)}, bf16[192,768]{1,0:T(8,128)(2,1)S(1)}, bf16[768,384]{1,0:T(8,128)(2,1)S(1)}) custom-call(bf16[2,192,768]{2,1,0:T(8,128)(2,1)} %refs_0_.3, bf16[2,192,768]{2,1,0:T(8,128)(2,1)} %bitcast.12, bf16[768,384]{1,0:T(8,128)(2,1)} %refs_2_.3, ...), custom_call_target="tpu_custom_call" | custom-call | flops 500000000 | bytes 1048576 | tf_op jit(solution)/shard_map/own/pallas_call | solution.py:475
  38.5 0.0 collective-permute-done.8.from_both
  38.5 2.8 %collective-permute-done.9.from_lon = bf16[224,128]{1,0:T(8,128)(2,1)S(1)} collective-permute-done((bf16[224,128]{1,0:T(8,128)(2,1)S(1)}, bf16[224,128]{1,0:T(8,128)(2,1)S(1)}, u32[]{:S(2)}, u32[]{:S(2)}) %collective-permute-start.9) | collective-permute-done | bytes 57376 | tf_op jit(solution)/shard_map/ppermute | solution.py:500
  41.2 0.7 %add.1.middle = bf16[288,192]{1,0:T(8,128)(2,1)S(1)} custom-call(f32[2,144,128]{2,1,0:T(8,128)S(1)} %get-tuple-element.40.keep.refs_3_, bf16[432,192]{1,0:T(8,128)(2,1)S(1)} %get-tuple-element.55.far, bf16[224,128]{1,0:T(8,128)(2,1)S(1)} %collective-permute-done.8.from_both, bf16[224,128]{1,0:T(8,128)(2,1)S(1)} %collective-permute-done.9.from_lon, ...), custom_call_target="tpu_custom_call" | custom-call | flops 700000000 | bytes 1048576 | tf_op jit(solution)/shard_map/add/pallas_call | solution.py:475
  42.0 0.0 collective-permute-done.10.from_lat
  42.0 1.9 %last.1 = bf16[144,384]{1,0:T(8,128)(2,1)} custom-call(f32[2,144,128]{2,1,0:T(8,128)S(1)} %get-tuple-element.40.keep.refs_3_, bf16[432,192]{1,0:T(8,128)(2,1)S(1)} %get-tuple-element.55.far, bf16[144,192]{1,0:T(8,128)(2,1)S(1)} %get-tuple-element.68.done, bf16[288,192]{1,0:T(8,128)(2,1)S(1)} %add.1.middle, ...), custom_call_target="tpu_custom_call" | custom-call | flops 2000000000 | bytes 1048576 | tf_op jit(solution)/shard_map/last/pallas_call | solution.py:475
  (2 shorter events, 0.0 us)
Async XLA Ops:
  0.0 5.8 %collective-permute-start = (bf16[2,4,1242]{2,1,0:T(4,128)(2,1)}, bf16[2,4,1242]{2,1,0:T(4,128)(2,1)S(1)}, u32[]{:S(2)}, u32[]{:S(2)}) collective-permute-start(bf16[2,4,1242]{2,1,0:T(4,128)(2,1)} %bitcast.14), channel_id=1, source_target_pairs={{0,8},{1,9},{2,10},{3,11},{4,12},{5,13},{6,14},{7,15},{8,0},{9,1},... | collective-permute-start | bytes 59624 | tf_op jit(solution)/shard_map/ppermute | solution.py:508
  5.9 7.1 %collective-permute-start.1 = (bf16[2,2,4,1242]{3,2,1,0:T(4,128)(2,1)S(1)}, bf16[2,2,4,1242]{3,2,1,0:T(4,128)(2,1)S(1)}, u32[]{:S(2)}, u32[]{:S(2)}) collective-permute-start(bf16[2,2,4,1242]{3,2,1,0:T(4,128)(2,1)S(1)} %halves.1.refs_0_), channel_id=1, source_target_pairs={{0,2},{1,3},{2,4},{3,5},{4,6},{5,7},{6,0},{7,1},{8,10},{9,11},{10,... | collective-permute-start | bytes 119240 | tf_op jit(solution)/shard_map/ppermute | solution.py:508
  7.3 5.7 %collective-permute-start.2 = (bf16[2,2,4,1242]{3,2,1,0:T(4,128)(2,1)S(1)}, bf16[2,2,4,1242]{3,2,1,0:T(4,128)(2,1)S(1)}, u32[]{:S(2)}, u32[]{:S(2)}) collective-permute-start(bf16[2,2,4,1242]{3,2,1,0:T(4,128)(2,1)S(1)} %halves.1.refs_0_), channel_id=1, source_target_pairs={{0,4},{1,5},{2,6},{3,7},{4,0},{5,1},{6,2},{7,3},{8,12},{9,13},{10,... | collective-permute-start | bytes 119240 | tf_op jit(solution)/shard_map/ppermute | solution.py:508
  10.1 4.0 %collective-permute-start.3 = (bf16[2,2,4,1242]{3,2,1,0:T(4,128)(2,1)S(1)}, bf16[2,2,4,1242]{3,2,1,0:T(4,128)(2,1)S(1)}, u32[]{:S(2)}, u32[]{:S(2)}) collective-permute-start(bf16[2,2,4,1242]{3,2,1,0:T(4,128)(2,1)S(1)} %halves.1.refs_0_), channel_id=1, source_target_pairs={{0,6},{1,7},{2,0},{3,1},{4,2},{5,3},{6,4},{7,5},{8,14},{9,15},{10,... | collective-permute-start | bytes 119240 | tf_op jit(solution)/shard_map/ppermute | solution.py:508
  14.1 1.5 %collective-permute-start.4 = (bf16[8,2,4,1242]{3,2,1,0:T(4,128)(2,1)S(1)}, bf16[8,2,4,1242]{3,2,1,0:T(4,128)(2,1)S(1)}, u32[]{:S(2)}, u32[]{:S(2)}) collective-permute-start(bf16[8,2,4,1242]{3,2,1,0:T(4,128)(2,1)S(1)} %mine.1.refs_0_), channel_id=1, source_target_pairs={{0,1},{1,0},{2,3},{3,2},{4,5},{5,4},{6,7},{7,6},{8,9},{9,8},{10,11... | collective-permute-start | bytes 476936 | tf_op jit(solution)/shard_map/ppermute | solution.py:508
  19.1 7.4 %collective-permute-start.5 = (bf16[224,128]{1,0:T(8,128)(2,1)S(1)}, bf16[224,128]{1,0:T(8,128)(2,1)S(1)}, u32[]{:S(2)}, u32[]{:S(2)}) collective-permute-start(bf16[224,128]{1,0:T(8,128)(2,1)S(1)} %get-tuple-element.61), channel_id=1, source_target_pairs={{0,15},{1,0},{2,1},{3,2},{4,3},{5,4},{6,5},{7,6},{8,7},{9,8},{10,9... | collective-permute-start | bytes 172040 | tf_op jit(solution)/shard_map/ppermute | solution.py:500
  24.6 3.7 %collective-permute-start.6 = (bf16[224,128]{1,0:T(8,128)(2,1)S(1)}, bf16[224,128]{1,0:T(8,128)(2,1)S(1)}, u32[]{:S(2)}, u32[]{:S(2)}) collective-permute-start(bf16[224,128]{1,0:T(8,128)(2,1)S(1)} %get-tuple-element.62), channel_id=1, source_target_pairs={{0,113},{1,114},{2,115},{3,116},{4,117},{5,118},{6,119},{7,120},{8... | collective-permute-start | bytes 172040 | tf_op jit(solution)/shard_map/ppermute | solution.py:500
  24.6 4.8 %collective-permute-start.7 = (bf16[224,128]{1,0:T(8,128)(2,1)S(1)}, bf16[224,128]{1,0:T(8,128)(2,1)S(1)}, u32[]{:S(2)}, u32[]{:S(2)}) collective-permute-start(bf16[224,128]{1,0:T(8,128)(2,1)S(1)} %get-tuple-element.63), channel_id=1, source_target_pairs={{0,112},{1,113},{2,114},{3,115},{4,116},{5,117},{6,118},{7,119},{8... | collective-permute-start | bytes 172040 | tf_op jit(solution)/shard_map/ppermute | solution.py:500
  29.4 4.6 %copy-start = (f32[768]{0:T(1024)S(1)}, f32[768]{0:T(1024)}, u32[]{:S(2)}) copy-start(f32[768]{0:T(1024)} %param.20) | copy-start | bytes 9220
  31.8 6.7 %collective-permute-start.8 = (bf16[224,128]{1,0:T(8,128)(2,1)S(1)}, bf16[224,128]{1,0:T(8,128)(2,1)S(1)}, u32[]{:S(2)}, u32[]{:S(2)}) collective-permute-start(bf16[224,128]{1,0:T(8,128)(2,1)S(1)} %get-tuple-element.69), channel_id=1, source_target_pairs={{0,17},{1,18},{2,19},{3,20},{4,21},{5,22},{6,23},{7,24},{8,25},{9,... | collective-permute-start | bytes 172040 | tf_op jit(solution)/shard_map/ppermute | solution.py:500
  34.0 7.2 %collective-permute-start.9 = (bf16[224,128]{1,0:T(8,128)(2,1)S(1)}, bf16[224,128]{1,0:T(8,128)(2,1)S(1)}, u32[]{:S(2)}, u32[]{:S(2)}) collective-permute-start(bf16[224,128]{1,0:T(8,128)(2,1)S(1)} %get-tuple-element.70), channel_id=1, source_target_pairs={{0,1},{1,2},{2,3},{3,4},{4,5},{5,6},{6,7},{7,8},{8,9},{9,10},{10,1... | collective-permute-start | bytes 172040 | tf_op jit(solution)/shard_map/ppermute | solution.py:500
  34.1 7.9 %collective-permute-start.10 = (bf16[224,128]{1,0:T(8,128)(2,1)S(1)}, bf16[224,128]{1,0:T(8,128)(2,1)S(1)}, u32[]{:S(2)}, u32[]{:S(2)}) collective-permute-start(bf16[224,128]{1,0:T(8,128)(2,1)S(1)} %get-tuple-element.73), channel_id=1, source_target_pairs={{0,16},{1,17},{2,18},{3,19},{4,20},{5,21},{6,22},{7,23},{8,24},{9,... | collective-permute-start | bytes 172040 | tf_op jit(solution)/shard_map/ppermute | solution.py:500
